TPU v7x, 256 devices: a whole 4x4x8 slice. The times are simulated.
256 devices in a mesh: tm: 64 (over z_hi, y, x), inp: 4 (over z_lo, core).
Axes of the slice: x: 4, y: 4, z: 8 (z_hi: 4, z_lo: 2; z = z_hi * 2 + z_lo), core: 2. Of those that a mesh axis runs over, the one named last changes fastest.
Arguments:
- samples: bfloat16 [1024, 262144], P('inp', 'tm'), may hold values from -6 to 6
- coeffs: float32 [16, 2048], replicated, may hold values from -1.5 to 1.5
- delays: float32 [512, 1024], replicated, may hold values from -32 to 32
Outputs:
- beams: bfloat16 [2, 1024, 512, 128], P(None, ('tm', 'inp'))
All inputs are finite; a program needn't handle non-finite values.
Results may differ from a plain program's by a relative error of at most 0.015.
Values may be sent and summed in bfloat16 or wider, within the bound.
No kernel may reach another device: no remote copies, remote signals or barrier semaphores. Data moves between devices by JAX's collectives and lax.ppermute only.
A program may use at most 128 MiB of HBM per device.

v0:
```python
import math

import jax
import jax.numpy as jnp
from jax import lax
from jax.sharding import PartitionSpec as P

CHAN = 1024
FRAME = 2048
TAPS = 16
INPUTS = 1024


def passed_along(array, axis, by):
    count = lax.axis_size(axis)
    pairs = [(i, i + by) for i in range(count) if 0 <= i + by < count]
    return lax.ppermute(array, axis, pairs)


def form_beams(channel_spectra, delay_part, chan_start):
    count = channel_spectra.shape[4]
    channels = (chan_start + jnp.arange(count, dtype=jnp.int32)).astype(jnp.float32)
    angle = channels[:, None, None] * delay_part[None] * (2.0 * math.pi / FRAME)
    weight_re = jnp.cos(angle).astype(jnp.bfloat16)
    weight_im = (-jnp.sin(angle)).astype(jnp.bfloat16)
    part_re = channel_spectra[:, :, 0, 0, :]
    part_im = channel_spectra[:, :, 1, 0, :]

    def contract(beam_weight, sample_values):
        return jnp.einsum(
            "vhu,uav->vha", beam_weight, sample_values, preferred_element_type=jnp.float32
        )

    out_re = contract(weight_re, part_re) - contract(weight_im, part_im)
    out_im = contract(weight_re, part_im) + contract(weight_im, part_re)
    return jnp.stack([out_re, out_im]) * (1.0 / math.sqrt(INPUTS))


def apply_taps(extended, coeffs, frames_here):
    history_len = TAPS - 1
    filtered = jnp.zeros((extended.shape[0], frames_here, FRAME), jnp.float32)
    for tap in range(TAPS):
        filtered = filtered + coeffs[tap] * extended[
            :, history_len - tap : history_len - tap + frames_here
        ].astype(jnp.float32)
    return filtered.astype(jnp.bfloat16)


def transform(filtered):
    row_total = filtered.shape[0] * filtered.shape[1]
    flat_rows = filtered.reshape(row_total, FRAME)
    positions = jnp.arange(FRAME, dtype=jnp.int32)
    channels = jnp.arange(CHAN, dtype=jnp.int32)
    weighted_product = positions[:, None] * channels[None, :] % FRAME
    angle = weighted_product.astype(jnp.float32) * (2.0 * math.pi / FRAME)
    table = jnp.concatenate([jnp.cos(angle), -jnp.sin(angle)], axis=1) * (1.0 / math.sqrt(FRAME))
    table_high = table.astype(jnp.bfloat16)
    table_low = (table - table_high.astype(jnp.float32)).astype(jnp.bfloat16)
    spectrum = jnp.dot(flat_rows, table_high, preferred_element_type=jnp.float32) + jnp.dot(
        flat_rows, table_low, preferred_element_type=jnp.float32
    )
    return spectrum.astype(jnp.bfloat16)


def body(samples, coeffs, delays):
    inputs_here = samples.shape[0]
    frames_here = samples.shape[1] // FRAME
    history_len = TAPS - 1
    time_groups = lax.axis_size("tm")
    block_channel_start = CHAN // time_groups
    own = samples.reshape(inputs_here, frames_here, FRAME)
    count_shifts = -(-history_len // frames_here)
    received = []
    for offset in range(1, count_shifts + 1):
        sent_len = min(frames_here, history_len - (offset - 1) * frames_here)
        received.append(passed_along(own[:, frames_here - sent_len :], "tm", offset))
    extended = jnp.concatenate(received[::-1] + [own], axis=1)
    filtered = apply_taps(extended, coeffs, frames_here)
    spectrum = transform(filtered).reshape(
        inputs_here, frames_here, 2, time_groups, block_channel_start
    )
    turned = lax.all_to_all(spectrum, "tm", split_axis=3, concat_axis=1, tiled=True)
    delay_part = lax.dynamic_slice_in_dim(
        delays, lax.axis_index("inp") * inputs_here, inputs_here, 1
    )
    partial_value = form_beams(turned, delay_part, lax.axis_index("tm") * block_channel_start)
    beam_output = lax.psum_scatter(partial_value, "inp", scatter_dimension=1, tiled=True)
    return beam_output.astype(jnp.bfloat16)


def solution(mesh):
    in_specs = (P("inp", "tm"), P(), P())
    out_specs = P(None, ("tm", "inp"), None, None)
    return jax.shard_map(body, mesh=mesh, in_specs=in_specs, out_specs=out_specs, check_vma=False)
```

profile of v0, /device:TPU:1, one launch (start us, length us, event | category | flops | bytes accessed | tf_op | source)
XLA Modules:
  0.0 1340.7 jit_solution(14004010963879049844)
XLA Ops:
  0.0 4.2 copy.11
  4.3 5.3 collective-permute-start
  9.5 4.3 collective-permute-start.1
  16.6 4.5 collective-permute-start.7
  21.1 5.1 collective-permute-start.2
  26.2 4.0 collective-permute-start.3
  30.2 138.8 %collective-permute-done.7 = bf16[256,1,2048]{2,0,1:T(8,128)(2,1)} collective-permute-done((bf16[256,1,2048]{2,0,1:T(8,128)(2,1)}, bf16[256,1,2048]{2,0,1:T(8,128)(2,1)}, u32[]{:S(2)}, u32[]{:S(2)}) %collective-permute-start.7) | collective-permute-done | bytes 1048608 | tf_op jit(solution)/shard_map/ppermute | solution.py:17
  169.0 2.6 collective-permute-start.4
  171.6 2.7 collective-permute-start.5
  174.3 2.6 collective-permute-start.6
  177.0 34.5 %sine_negate_fusion = (f32[2048,1024]{1,0:T(8,128)}, f32[2048,1024]{1,0:T(8,128)}) fusion(), kind=kLoop, calls=%fused_computation.13 | loop fusion | flops 31457280 | bytes 16777216 | tf_op jit(solution)/shard_map/neg | solution.py:56
  211.5 1.5 copy.13
  213.0 135.7 %collective-permute-done.3 = bf16[256,2,2048]{0,2,1:T(8,128)(2,1)} collective-permute-done((bf16[256,2,2048]{0,2,1:T(8,128)(2,1)}, bf16[256,2,2048]{0,2,1:T(8,128)(2,1)}, u32[]{:S(2)}, u32[]{:S(2)}) %collective-permute-start.3) | collective-permute-done | bytes 2097184 | tf_op jit(solution)/shard_map/ppermute | solution.py:17
  348.8 12.7 add_convert_fusion.1
  361.5 6.2 copy.14
  367.7 4.1 reshape.32
  371.9 11.1 fusion.10
  382.9 11.7 add_convert_fusion
  394.7 16.8 %reshape.33 = bf16[256,2,2,64,16]{4,3,2,1,0:T(8,128)(2,1)} reshape(bf16[512,2048]{1,0:T(8,128)(2,1)} %add_convert_fusion) | data formatting | bytes 4194304 | tf_op jit(solution)/shard_map/reshape | solution.py:79
  411.5 18.4 %copy.15 = bf16[256,2,2,64,16]{0,4,2,1,3:T(8,128)(2,1)} copy(bf16[256,2,2,64,16]{4,3,2,1,0:T(8,128)(2,1)} %reshape.33) | data formatting | bytes 4194304 | tf_op jit(solution)/shard_map/reshape | solution.py:79
  429.8 542.2 %all-to-all-start = ((bf16[256,2,2,64,16]{0,4,2,1,3:T(8,128)(2,1)}), bf16[256,2,2,64,16]{0,4,2,1,3:T(8,128)(2,1)}, u32[]{:S(2)}, u32[]{:S(2)}) async-start(bf16[256,2,2,64,16]{0,4,2,1,3:T(8,128)(2,1)} %copy.15), calls=%async_computation | async-start | bytes 4194304 | tf_op jit(solution)/shard_map/all_to_all | solution.py:82
  974.2 36.1 %all-to-all-done = bf16[256,2,2,64,16]{0,4,2,1,3:T(8,128)(2,1)} async-done(((bf16[256,2,2,64,16]{0,4,2,1,3:T(8,128)(2,1)}), bf16[256,2,2,64,16]{0,4,2,1,3:T(8,128)(2,1)}, u32[]{:S(2)}, u32[]{:S(2)}) %all-to-all-start) | async-done | bytes 2097184 | tf_op jit(solution)/shard_map/all_to_all | solution.py:82
  1010.3 2.7 fusion.42
  1012.9 2.7 copy.20
  1015.6 1.7 copy.21
  1017.3 28.7 %fusion.12 = f32[16,512,128]{2,1,0:T(8,128)S(1)} fusion(f32[512,256]{1,0:T(8,128)} %constant_dynamic-slice_fusion, f32[16]{0:T(128)S(1)} %add_convert_fusion.2, bf16[256,128,1,1,16]{1,0,4,3,2:T(8,128)(2,1)} %copy.20), kind=kOutput, calls=%fused_computation.21 | convolution fusion | flops 543162368 | bytes 5767232 | tf_op jit(solution)/shard_map/vhu,uav->vha/dot_general | solution.py:30
  1046.0 27.6 %fusion.11 = f32[16,512,128]{2,1,0:T(8,128)S(1)} fusion(f32[512,256]{1,0:T(8,128)S(1)} %copy-done.4, f32[16]{0:T(128)S(1)} %add_convert_fusion.2, bf16[256,128,1,1,16]{1,0,4,3,2:T(8,128)(2,1)S(1)} %copy-done.3), kind=kOutput, calls=%fused_computation.20 | convolution fusion | flops 543162368 | bytes 5767232 | tf_op jit(solution)/shard_map/vhu,uav->vha/dot_general | solution.py:30
  1073.6 28.1 %subtract_bitcast_fusion = f32[1,16,512,128]{3,2,1,0:T(8,128)S(1)} fusion(f32[16,512,128]{2,1,0:T(8,128)S(1)} %fusion.12, f32[512,256]{1,0:T(8,128)S(1)} %copy-done.4, f32[16]{0:T(128)S(1)} %add_convert_fusion.2, bf16[256,128,1,1,16]{1,0,4,3,2:T(8,128)(2,1)S(1)} %copy-done.3), kind=kOutput, calls=%fused_computation.25 | convolution fusion | flops 546308096 | bytes 9961536 | tf_op jit(solution)/shard_map/vhu,uav->vha/dot_general | solution.py:30
  1101.7 28.1 %add_bitcast_fusion = f32[1,16,512,128]{3,2,1,0:T(8,128)S(1)} fusion(f32[16,512,128]{2,1,0:T(8,128)S(1)} %fusion.11, f32[512,256]{1,0:T(8,128)S(1)} %copy-done.4, f32[16]{0:T(128)S(1)} %add_convert_fusion.2, bf16[256,128,1,1,16]{1,0,4,3,2:T(8,128)(2,1)S(1)} %copy-done.2), kind=kOutput, calls=%fused_computation.24 | convolution fusion | flops 546308096 | bytes 9961536 | tf_op jit(solution)/shard_map/vhu,uav->vha/dot_general | solution.py:30
  1129.8 3.9 maximum_multiply_fusion.1
  1133.7 204.3 %all-reduce.2 = bf16[2,16,512,128]{3,2,1,0:T(8,128)(2,1)} all-reduce(f32[2,16,512,128]{3,2,1,0:T(8,128)} %maximum_multiply_fusion.1), channel_id=2, replica_groups=mesh['tm'=64,'inp'=4] {'inp'}, use_global_device_ids=true, to_apply=%region_0.1.clone | all-reduce | flops 2097152 | bytes 12582912
  1338.0 2.3 dynamic-slice_convert_fusion
  (26 shorter events, 4.3 us)
Async XLA Ops:
  0.0 973.3 %copy-start = (f32[512,1024]{1,0:T(8,128)S(1)}, f32[512,1024]{1,0:T(8,128)}, u32[]{:S(2)}) copy-start(f32[512,1024]{1,0:T(8,128)} %param.5) | copy-start | bytes 6291460
  0.0 176.9 %copy-start.5 = (f32[16,2048]{1,0:T(8,128)S(1)}, f32[16,2048]{1,0:T(8,128)}, u32[]{:S(2)}) copy-start(f32[16,2048]{1,0:T(8,128)} %param.4) | copy-start | bytes 393220
  4.3 167.4 %collective-permute-start = (bf16[256,2,2048]{0,2,1:T(8,128)(2,1)}, bf16[256,2,2048]{0,2,1:T(8,128)(2,1)}, u32[]{:S(2)}, u32[]{:S(2)}) collective-permute-start(bf16[256,2,2048]{0,2,1:T(8,128)(2,1)} %bitcast.45), channel_id=1, source_target_pairs={{0,4},{4,8},{8,12},{12,16},{16,20},{20,24},{24,28},{28,32},{32,36}... | collective-permute-start | bytes 6291464 | tf_op jit(solution)/shard_map/ppermute | solution.py:17
  9.5 164.7 %collective-permute-start.1 = (bf16[256,2,2048]{0,2,1:T(8,128)(2,1)}, bf16[256,2,2048]{0,2,1:T(8,128)(2,1)}, u32[]{:S(2)}, u32[]{:S(2)}) collective-permute-start(bf16[256,2,2048]{0,2,1:T(8,128)(2,1)} %bitcast.46), channel_id=1, source_target_pairs={{0,8},{4,12},{8,16},{12,20},{16,24},{20,28},{24,32},{28,36},{32,40... | collective-permute-start | bytes 6291464 | tf_op jit(solution)/shard_map/ppermute | solution.py:17
  16.6 152.4 %collective-permute-start.7 = (bf16[256,1,2048]{2,0,1:T(8,128)(2,1)}, bf16[256,1,2048]{2,0,1:T(8,128)(2,1)}, u32[]{:S(2)}, u32[]{:S(2)}) collective-permute-start(bf16[256,1,2048]{2,0,1:T(8,128)(2,1)} %copy.12), channel_id=1, source_target_pairs={{0,32},{4,36},{8,40},{12,44},{16,48},{20,52},{24,56},{28,60},{32,6... | collective-permute-start | bytes 3145736 | tf_op jit(solution)/shard_map/ppermute | solution.py:17
  21.1 191.9 %collective-permute-start.2 = (bf16[256,2,2048]{0,2,1:T(8,128)(2,1)}, bf16[256,2,2048]{0,2,1:T(8,128)(2,1)}, u32[]{:S(2)}, u32[]{:S(2)}) collective-permute-start(bf16[256,2,2048]{0,2,1:T(8,128)(2,1)} %bitcast.48), channel_id=1, source_target_pairs={{0,12},{4,16},{8,20},{12,24},{16,28},{20,32},{24,36},{28,40},{32,4... | collective-permute-start | bytes 6291464 | tf_op jit(solution)/shard_map/ppermute | solution.py:17
  26.2 322.6 %collective-permute-start.3 = (bf16[256,2,2048]{0,2,1:T(8,128)(2,1)}, bf16[256,2,2048]{0,2,1:T(8,128)(2,1)}, u32[]{:S(2)}, u32[]{:S(2)}) collective-permute-start(bf16[256,2,2048]{0,2,1:T(8,128)(2,1)} %bitcast.49), channel_id=1, source_target_pairs={{0,16},{4,20},{8,24},{12,28},{16,32},{20,36},{24,40},{28,44},{32,4... | collective-permute-start | bytes 6291464 | tf_op jit(solution)/shard_map/ppermute | solution.py:17
  169.0 179.8 %collective-permute-start.4 = (bf16[256,2,2048]{0,2,1:T(8,128)(2,1)}, bf16[256,2,2048]{0,2,1:T(8,128)(2,1)}, u32[]{:S(2)}, u32[]{:S(2)}) collective-permute-start(bf16[256,2,2048]{0,2,1:T(8,128)(2,1)} %bitcast.50), channel_id=1, source_target_pairs={{0,20},{4,24},{8,28},{12,32},{16,36},{20,40},{24,44},{28,48},{32,5... | collective-permute-start | bytes 6291464 | tf_op jit(solution)/shard_map/ppermute | solution.py:17
  171.6 177.1 %collective-permute-start.5 = (bf16[256,2,2048]{0,2,1:T(8,128)(2,1)}, bf16[256,2,2048]{0,2,1:T(8,128)(2,1)}, u32[]{:S(2)}, u32[]{:S(2)}) collective-permute-start(bf16[256,2,2048]{0,2,1:T(8,128)(2,1)} %bitcast.51), channel_id=1, source_target_pairs={{0,24},{4,28},{8,32},{12,36},{16,40},{20,44},{24,48},{28,52},{32,5... | collective-permute-start | bytes 6291464 | tf_op jit(solution)/shard_map/ppermute | solution.py:17
  174.3 174.5 %collective-permute-start.6 = (bf16[256,2,2048]{0,2,1:T(8,128)(2,1)}, bf16[256,2,2048]{0,2,1:T(8,128)(2,1)}, u32[]{:S(2)}, u32[]{:S(2)}) collective-permute-start(bf16[256,2,2048]{0,2,1:T(8,128)(2,1)} %bitcast.52), channel_id=1, source_target_pairs={{0,28},{4,32},{8,36},{12,40},{16,44},{20,48},{24,52},{28,56},{32,6... | collective-permute-start | bytes 6291464 | tf_op jit(solution)/shard_map/ppermute | solution.py:17
  371.9 11.1 copy-start.1
  429.8 542.2 %copy-start.6 = (u32[256]{0:T(256)S(1)}, u32[256]{0:T(256)}, u32[]{:S(2)}) copy-start(u32[256]{0:T(256)} %constant.40) | copy-start | bytes 3076
  429.8 580.4 %all-to-all-start = ((bf16[256,2,2,64,16]{0,4,2,1,3:T(8,128)(2,1)}), bf16[256,2,2,64,16]{0,4,2,1,3:T(8,128)(2,1)}, u32[]{:S(2)}, u32[]{:S(2)}) async-start(bf16[256,2,2,64,16]{0,4,2,1,3:T(8,128)(2,1)} %copy.15), calls=%async_computation | async-start | bytes 4194304 | tf_op jit(solution)/shard_map/all_to_all | solution.py:82
  1017.3 28.7 %copy-start.3 = (bf16[256,128,1,1,16]{1,0,4,3,2:T(8,128)(2,1)S(1)}, bf16[256,128,1,1,16]{1,0,4,3,2:T(8,128)(2,1)}, u32[]{:S(2)}) copy-start(bf16[256,128,1,1,16]{1,0,4,3,2:T(8,128)(2,1)} %copy.21) | copy-start | bytes 3145732
  1017.3 28.7 %copy-start.4 = (f32[512,256]{1,0:T(8,128)S(1)}, f32[512,256]{1,0:T(8,128)}, u32[]{:S(2)}) copy-start(f32[512,256]{1,0:T(8,128)} %constant_dynamic-slice_fusion) | copy-start | bytes 1572868
  1073.6 28.1 %copy-start.2 = (bf16[256,128,1,1,16]{1,0,4,3,2:T(8,128)(2,1)S(1)}, bf16[256,128,1,1,16]{1,0,4,3,2:T(8,128)(2,1)}, u32[]{:S(2)}) copy-start(bf16[256,128,1,1,16]{1,0,4,3,2:T(8,128)(2,1)} %copy.20) | copy-start | bytes 3145732
where the time goes:
time: 1350 us; the launch traced here: 1340 us
  starting transfers between devices  573 us (42%)
  waiting for transfers between devices  311 us (23%)
  blocking collectives  204 us (15%)
  matrix products  135 us (10%)
  local copies, waits for them, and re-layouts  64.8 us (5%)
  other arithmetic  51.1 us (4%)
    all_to_all x1, starting transfers between devices, body(): lax.all_to_all(spectrum, 'tm', split_axis=3, concat_axis=1, tiled=True)  542 us
    ppermute x8, waiting for transfers between devices, passed_along(): return lax.ppermute(array, axis, pairs)  275 us
    unnamed x1, blocking collectives  204 us
    dot_general x4, matrix products, contract(): jnp.einsum('vhu,uav->vha', beam_weight, sample_values, preferred_element_...  113 us
    all_to_all x1, waiting for transfers between devices, body(): lax.all_to_all(spectrum, 'tm', split_axis=3, concat_axis=1, tiled=True)  36.1 us
    reshape x2, local copies, waits for them, and re-layouts, body(): transform(filtered)  35.2 us
    neg x1, other arithmetic, transform(): -jnp.sin(angle)  34.5 us
    ppermute x8, starting transfers between devices, passed_along(): return lax.ppermute(array, axis, pairs)  31.1 us
  transfers between devices with their start and end apart: 9, of which 3 were waited for; matrix products, arithmetic and copies ran while one was open for 3% of the time, Pallas kernels for 0%

commit v1 on v0

v1 whole, which is shorter than its diff:
```python
import math

import jax
import jax.numpy as jnp
import numpy as np
from jax import lax
from jax.experimental import pallas as pl
from jax.experimental.pallas import tpu as pltpu
from jax.sharding import Mesh
from jax.sharding import PartitionSpec as P

CHAN = 1024
FRAME = 2048
TAPS = 16
INPUTS = 1024
BEAMS = 512
FRAMES = 128

ZH, YX, INP, DEVICES = 4, 16, 4, 256
PLANE = FRAMES // ZH
LATE = 8
EARLY = TAPS - 1 - LATE
ROWS = INPUTS // INP // YX
OWN = CHAN // DEVICES
PLACES = YX * INP
LANES = 128
ALL = ("zh", "y", "x", "zl", "core")


def dft_table():
    turn = np.arange(FRAME) * (2.0 * np.pi / FRAME)
    index = np.outer(np.arange(CHAN), np.arange(FRAME)) % FRAME
    table = np.stack([np.cos(turn)[index], -np.sin(turn)[index]], axis=1)
    return table.reshape(2 * CHAN, FRAME).astype(jnp.bfloat16)


def spectra_kernel(keep_ref, prev_ref, own_ref, next_ref, coeffs_ref, table_ref, out_ref, filtered, turned):
    rows = own_ref.shape[1]

    @pl.when(pl.program_id(0) == 0)
    def _():
        keep = keep_ref[0]

        def tile(step, carry):
            lanes = pl.ds(pl.multiple_of(step * LANES, LANES), LANES)
            frames = [prev_ref[k, :, lanes] for k in range(EARLY)]
            frames += [own_ref[k, :, lanes] for k in range(PLANE)]
            frames += [next_ref[k, :, lanes] for k in range(LATE)]
            frames = [value.astype(jnp.float32) for value in frames]
            taps = [coeffs_ref[t : t + 1, lanes] for t in range(TAPS)]
            for j in range(PLANE):
                newest = TAPS - 1 + j
                wrapped = max(0, j - (PLANE - LATE) + 1)
                near = min(wrapped, TAPS) if wrapped else TAPS
                total = taps[0] * frames[newest]
                for t in range(1, near):
                    total = total + taps[t] * frames[newest - t]
                if near < TAPS:
                    old = taps[near] * frames[newest - near]
                    for t in range(near + 1, TAPS):
                        old = old + taps[t] * frames[newest - t]
                    total = total + keep * old
                turned[pl.ds(j, rows, stride=PLANE), :] = total
            filtered[:, lanes] = turned[...].astype(jnp.bfloat16)
            return carry

        lax.fori_loop(0, FRAME // LANES, tile, 0)

    spectrum = lax.dot_general(
        table_ref[...], filtered[...], (((1,), (1,)), ((), ())), preferred_element_type=jnp.float32
    )
    out_ref[...] = (spectrum * (1.0 / math.sqrt(FRAME))).astype(jnp.bfloat16)


def spectra(keep, prev, own, following, coeffs, table):
    rows = own.shape[1]
    block = 256
    whole = lambda shape: pl.BlockSpec(shape, lambda i: (0,) * len(shape))
    return pl.pallas_call(
        spectra_kernel,
        grid=(2 * CHAN // block,),
        in_specs=[
            pl.BlockSpec(memory_space=pltpu.SMEM),
            whole(prev.shape),
            whole(own.shape),
            whole(following.shape),
            whole(coeffs.shape),
            pl.BlockSpec((block, FRAME), lambda i: (i, 0)),
        ],
        out_specs=pl.BlockSpec((block, rows * PLANE), lambda i: (i, 0)),
        out_shape=jax.ShapeDtypeStruct((2 * CHAN, rows * PLANE), jnp.bfloat16),
        scratch_shapes=[
            pltpu.VMEM((rows * PLANE, FRAME), jnp.bfloat16),
            pltpu.VMEM((rows * PLANE, LANES), jnp.float32),
        ],
        compiler_params=pltpu.CompilerParams(vmem_limit_bytes=40 << 20),
        cost_estimate=pl.CostEstimate(
            flops=2 * 2 * CHAN * FRAME * rows * PLANE, bytes_accessed=14 << 20, transcendentals=0
        ),
    )(keep, prev, own, following, coeffs, table)


def fit(values):
    nodes = (np.cos(np.pi * (np.arange(64) + 0.5) / 64) + 1.0) / 8.0
    return [float(v) for v in np.polynomial.Polynomial.fit(nodes, values(np.sqrt(nodes)), 7, domain=[0, 0.25], window=[0, 0.25]).coef]


COS = fit(lambda r: np.cos(2 * np.pi * r))
SIN = fit(lambda r: np.sin(2 * np.pi * r) / r)


def cos_sin(turns):
    rest = turns - jnp.round(turns)
    square = rest * rest
    cos, sin = COS[-1], SIN[-1]
    for a, b in zip(COS[-2::-1], SIN[-2::-1]):
        cos = cos * square + a
        sin = sin * square + b
    return cos, sin * rest


def weights_kernel(first_ref, delays_ref, out_ref):
    delay = delays_ref[...] * (1.0 / FRAME)
    step_cos, step_sin = cos_sin(delay)
    cos, sin = cos_sin(delay * first_ref[0])
    for c in range(OWN):
        if c:
            cos, sin = cos * step_cos - sin * step_sin, sin * step_cos + cos * step_sin
        out_ref[c, 0] = cos.astype(jnp.bfloat16)
        out_ref[c, 1] = (-sin).astype(jnp.bfloat16)


def weights(first, delays):
    block = 64
    return pl.pallas_call(
        weights_kernel,
        grid=(BEAMS // block,),
        in_specs=[
            pl.BlockSpec(memory_space=pltpu.SMEM),
            pl.BlockSpec((block, INPUTS), lambda i: (i, 0)),
        ],
        out_specs=pl.BlockSpec((OWN, 2, block, INPUTS), lambda i: (0, 0, i, 0)),
        out_shape=jax.ShapeDtypeStruct((OWN, 2, BEAMS, INPUTS), jnp.bfloat16),
        compiler_params=pltpu.CompilerParams(vmem_limit_bytes=24 << 20),
        cost_estimate=pl.CostEstimate(
            flops=60 * BEAMS * INPUTS, bytes_accessed=10 << 20, transcendentals=0
        ),
    )(first, delays)


def beams_kernel(spectra_ref, weights_ref, out_ref, wide, values):
    tiles = spectra_ref.shape[2] // LANES
    group = LANES // PLANE
    channel = pl.program_id(0)

    @pl.when(channel == 0)
    def _():
        lane = lax.broadcasted_iota(jnp.int32, (PLACES, LANES), 1)
        low = lane < 2 * PLANE
        even = lax.rem(lane, 2 * PLANE) < PLANE
        for tile in range(tiles):
            part = spectra_ref[:, :, tile * LANES : (tile + 1) * LANES]
            wide[...] = part.astype(jnp.float32).reshape(DEVICES * 2 * OWN, LANES)
            for own in range(OWN):
                for side in range(2):
                    a = [
                        wide[pl.ds(zh * PLACES * 2 * OWN + 2 * own + side, PLACES, stride=2 * OWN), :]
                        for zh in range(ZH)
                    ]
                    half = 2 * PLANE
                    low_a = jnp.where(low, a[0], pltpu.roll(a[2], half, 1))
                    low_b = jnp.where(low, a[1], pltpu.roll(a[3], half, 1))
                    high_a = jnp.where(low, pltpu.roll(a[0], half, 1), a[2])
                    high_b = jnp.where(low, pltpu.roll(a[1], half, 1), a[3])
                    b = [
                        jnp.where(even, low_a, pltpu.roll(low_b, PLANE, 1)),
                        jnp.where(even, pltpu.roll(low_a, LANES - PLANE, 1), low_b),
                        jnp.where(even, high_a, pltpu.roll(high_b, PLANE, 1)),
                        jnp.where(even, pltpu.roll(high_a, LANES - PLANE, 1), high_b),
                    ]
                    for k in range(group):
                        at = (tile * group + k) * PLACES
                        values[own, at : at + PLACES, side * LANES : (side + 1) * LANES] = b[k].astype(
                            jnp.bfloat16
                        )

    here = values[channel]
    by_re = jnp.dot(weights_ref[0, 0], here, preferred_element_type=jnp.float32)
    by_im = jnp.dot(weights_ref[0, 1], here, preferred_element_type=jnp.float32)
    out_re = (by_re[:, :LANES] - by_im[:, LANES:]) * (1.0 / math.sqrt(INPUTS))
    out_im = (by_re[:, LANES:] + by_im[:, :LANES]) * (1.0 / math.sqrt(INPUTS))
    out_ref[0, 0] = pltpu.roll(out_re, LATE, 1).astype(jnp.bfloat16)
    out_ref[1, 0] = pltpu.roll(out_im, LATE, 1).astype(jnp.bfloat16)


def beams(received, weight):
    return pl.pallas_call(
        beams_kernel,
        grid=(OWN,),
        in_specs=[
            pl.BlockSpec(received.shape, lambda i: (0, 0, 0)),
            pl.BlockSpec((1, 2, BEAMS, INPUTS), lambda i: (i, 0, 0, 0)),
        ],
        out_specs=pl.BlockSpec((2, 1, BEAMS, FRAMES), lambda i: (0, i, 0, 0)),
        out_shape=jax.ShapeDtypeStruct((2, OWN, BEAMS, FRAMES), jnp.bfloat16),
        scratch_shapes=[
            pltpu.VMEM((DEVICES * 2 * OWN, LANES), jnp.float32),
            pltpu.VMEM((OWN, INPUTS, 2 * LANES), jnp.bfloat16),
        ],
        compiler_params=pltpu.CompilerParams(vmem_limit_bytes=40 << 20),
        cost_estimate=pl.CostEstimate(
            flops=8 * OWN * BEAMS * INPUTS * FRAMES, bytes_accessed=11 << 20, transcendentals=0
        ),
    )(received, weight)


def body(samples, coeffs, delays):
    zh = lax.axis_index("zh")
    first = (lax.axis_index(ALL) * OWN).astype(jnp.float32).reshape(1)
    keep = jnp.where(zh == ZH - 1, 0.0, 1.0).astype(jnp.float32).reshape(1)
    table = jnp.asarray(dft_table())

    ordered = delays.reshape(BEAMS, INP, YX, ROWS).transpose(0, 3, 2, 1).reshape(BEAMS, INPUTS)
    weight = weights(first, ordered)

    own = lax.all_to_all(samples.reshape(YX, ROWS, 2 * FRAME), ("y", "x"), 0, 0, tiled=True)
    own = own.reshape(YX, ROWS, 2, FRAME).transpose(0, 2, 1, 3).reshape(PLANE, ROWS, FRAME)
    prev = lax.ppermute(own[PLANE - EARLY :], "zh", [(i, i + 1) for i in range(ZH - 1)])
    following = lax.ppermute(own[:LATE], "zh", [(i, (i - 1) % ZH) for i in range(ZH)])
    spectrum = spectra(keep, prev, own, following, coeffs, table)
    blocks = spectrum.reshape(DEVICES, 2 * OWN, ROWS * PLANE)
    received = lax.all_to_all(blocks, ALL, 0, 0, tiled=True)
    return beams(received, weight)


def solution(mesh):
    fine = Mesh(mesh.devices.reshape(4, 4, 4, 2, 2), ALL)
    in_specs = (P(("zl", "core"), ("zh", "y", "x")), P(), P())
    out_specs = P(None, ALL, None, None)
    return jax.shard_map(body, mesh=fine, in_specs=in_specs, out_specs=out_specs, check_vma=False)
```

time: 1350 us -> 159 us (0.12)
  starting transfers between devices: 573 us -> 20.1 us
  waiting for transfers between devices: 311 us -> 46.6 us
  blocking collectives: 204 us -> 34.9 us
  matrix products: 135 us -> 0 us
  other arithmetic: 51.1 us -> 0.97 us
  local copies, waits for them, and re-layouts: 64.8 us -> 26.9 us
  Pallas kernels: 0 us -> 28.9 us
    all_to_all x1, starting transfers between devices: 542 us -> 12.7 us  [body(): received = lax.all_to_all(blocks, ALL, 0, 0, tiled=True)]
    ppermute x8 -> x2, waiting for transfers between devices: 275 us -> 17.4 us  [the longest x1 9.25 us: body(): lax.ppermute(own[:LATE], 'zh', [(i, (i - 1) % ZH) for i in range(ZH)])]
    unnamed x1 -> x0, blocking collectives: 204 us -> none
    dot_general x6 -> x0, matrix products: 135 us -> none  [the longest x4 113 us: contract(): jnp.einsum('vhu,uav->vha', beam_weight, sample_values, preferred_element_...]
    all_to_all x0 -> x1, blocking collectives: none -> 34.9 us  [body(): lax.all_to_all(samples.reshape(YX, ROWS, 2 * FRAME), ('y', 'x'), 0, 0, ti...]
    neg x1 -> x0, other arithmetic: 34.5 us -> none  [transform(): -jnp.sin(angle)]
    reshape x3 -> x2, local copies, waits for them, and re-layouts: 39.3 us -> 5.88 us  [body(): delays.reshape(BEAMS, INP, YX, ROWS).transpose(0, 3, 2, 1)]
    pallas_call x0 -> x3, Pallas kernels: none -> 28.9 us  [the longest x1 14 us: spectra(): pl.pallas_call(spectra_kernel, grid=(2 * CHAN // block,), in_specs=[pl.Bl...]
  transfers between devices with their start and end apart: 9 -> 3, of which waited for: 3 -> 3; matrix products, arithmetic and copies ran while one was open for 3% -> 9% of each run, Pallas kernels for 0% -> 5%
where the time goes in v1:
time: 159 us; the launch traced here: 158 us
  waiting for transfers between devices  46.6 us (29%)
  blocking collectives  34.9 us (22%)
  Pallas kernels  28.9 us (18%)
  local copies, waits for them, and re-layouts  26.9 us (17%)
  starting transfers between devices  20.1 us (13%)
    all_to_all x1, blocking collectives, body(): lax.all_to_all(samples.reshape(YX, ROWS, 2 * FRAME), ('y', 'x'), 0, 0, ti...  34.9 us
    all_to_all x1, waiting for transfers between devices, body(): received = lax.all_to_all(blocks, ALL, 0, 0, tiled=True)  29.1 us
    unnamed x13, local copies, waits for them, and re-layouts  15.8 us
    pallas_call x1, Pallas kernels, spectra(): pl.pallas_call(spectra_kernel, grid=(2 * CHAN // block,), in_specs=[pl.Bl...  14 us
    all_to_all x1, starting transfers between devices, body(): received = lax.all_to_all(blocks, ALL, 0, 0, tiled=True)  12.7 us
    ppermute x1, waiting for transfers between devices, body(): lax.ppermute(own[:LATE], 'zh', [(i, (i - 1) % ZH) for i in range(ZH)])  9.25 us
    ppermute x1, waiting for transfers between devices, body(): lax.ppermute(own[PLANE - EARLY:], 'zh', [(i, i + 1) for i in range(ZH - 1)])  8.18 us
    pallas_call x1, Pallas kernels, weights(): pl.pallas_call(weights_kernel, grid=(BEAMS // block,), in_specs=[pl.Block...  7.7 us
  transfers between devices with their start and end apart: 3, of which 3 were waited for; matrix products, arithmetic and copies ran while one was open for 9% of the time, Pallas kernels for 5%

profile of v1, /device:TPU:1, one launch (start us, length us, event | category | flops | bytes accessed | tf_op | source)
XLA Modules:
  0.0 158.4 jit_solution(17999055153439221264)
XLA Ops:
  0.0 34.9 %all_to_all.10 = bf16[16,16,4096]{2,1,0:T(8,128)(2,1)S(1)} all-to-all(bf16[16,16,4096]{2,1,0:T(8,128)(2,1)} %bitcast.15), channel_id=1, replica_groups=mesh['zh'=4,'y'=4,'x'=4,'zl'=2,'core'=2] {'y','x'}, dimensions={0} | all-to-all | bytes 4194304 | tf_op jit(solution)/shard_map/all_to_all | solution.py:226
  34.9 0.1 fusion.1
  35.1 0.8 fusion
  35.9 0.0 copy-start.4
  35.9 6.0 %collective-permute-start.1 = (bf16[8,16,2048]{2,1,0:T(8,128)(2,1)}, bf16[8,16,2048]{2,1,0:T(8,128)(2,1)S(1)}, u32[]{:S(2)}, u32[]{:S(2)}) collective-permute-start(bf16[8,16,2048]{2,1,0:T(8,128)(2,1)} %bitcast.3), channel_id=1, source_target_pairs={{0,192},{64,0},{128,64},{192,128},{1,193},{65,1},{129,65},{193,129... | collective-permute-start | bytes 1572872 | tf_op jit(solution)/shard_map/ppermute | solution.py:229
  41.9 0.1 pad_maximum_fusion
  42.1 0.8 slice.22
  42.9 1.3 collective-permute-start
  44.2 8.2 %collective-permute-done.prev_ref = bf16[7,16,2048]{2,1,0:T(8,128)(2,1)S(1)} collective-permute-done((bf16[7,16,2048]{2,1,0:T(8,128)(2,1)}, bf16[7,16,2048]{2,1,0:T(8,128)(2,1)S(1)}, u32[]{:S(2)}, u32[]{:S(2)}) %collective-permute-start) | collective-permute-done | bytes 458784 | tf_op jit(solution)/shard_map/ppermute | solution.py:228
  52.4 9.2 %collective-permute-done.1.next_ref = bf16[8,16,2048]{2,1,0:T(8,128)(2,1)S(1)} collective-permute-done((bf16[8,16,2048]{2,1,0:T(8,128)(2,1)}, bf16[8,16,2048]{2,1,0:T(8,128)(2,1)S(1)}, u32[]{:S(2)}, u32[]{:S(2)}) %collective-permute-start.1) | collective-permute-done | bytes 524320 | tf_op jit(solution)/shard_map/ppermute | solution.py:229
  61.6 0.0 copy-done.4
  61.6 0.0 copy-start.5
  61.6 3.4 %copy-done.5 = bf16[2048,2048]{1,0:T(8,128)(2,1)S(1)} copy-done((bf16[2048,2048]{1,0:T(8,128)(2,1)S(1)}, bf16[2048,2048]{1,0:T(8,128)(2,1)}, u32[]{:S(2)}) %copy-start.5) | copy-done | bytes 8388632
  65.0 14.0 %shard_map.46 = bf16[2048,512]{1,0:T(8,128)(2,1)S(1)} custom-call(f32[1]{0:T(128)} %bitcast.keep_ref, bf16[7,16,2048]{2,1,0:T(8,128)(2,1)S(1)} %collective-permute-done.prev_ref, bf16[32,16,2048]{2,1,0:T(8,128)(2,1)S(1)} %bitcast.12, bf16[8,16,2048]{2,1,0:T(8,128)(2,1)S(1)} %collective-permute-done.1.next_ref, f32[16,2048]{1,0:T(8,128)S(1)} %copy-done.4, ...), custom_call_target="tpu_custom_call" | custom-call | flops 4294967296 | bytes 14680064 | tf_op jit(solution)/shard_map/pallas_call | solution.py:79
  79.0 0.0 copy-start.3
  79.0 1.3 copy-done.3
  80.4 12.7 %all-to-all-start.1 = ((bf16[256,8,512]{2,1,0:T(8,128)(2,1)}), bf16[256,8,512]{2,1,0:T(8,128)(2,1)S(1)}, u32[]{:S(2)}, u32[]{:S(2)}) async-start(bf16[256,8,512]{2,1,0:T(8,128)(2,1)} %bitcast.13), calls=%async_computation.1 | async-start | bytes 4194304 | tf_op jit(solution)/shard_map/all_to_all | solution.py:232
  93.1 2.9 %copy.6 = f32[512,1024]{0,1:T(8,128)} copy(f32[512,1024]{1,0:T(8,128)} %param.6) | data formatting | bytes 4194304 | tf_op args[2]
  96.1 4.3 %copy.7 = f32[512,16,16,4]{0,3,2,1:T(4,128)} copy(f32[512,16,16,4]{0,1,2,3:T(8,128)} %bitcast.14) | data formatting | bytes 4194304 | tf_op jit(solution)/shard_map/transpose | solution.py:223
  100.3 2.9 %reshape.29 = f32[512,1024]{0,1:T(8,128)} reshape(f32[512,16,16,4]{0,3,2,1:T(4,128)} %copy.7) | data formatting | bytes 4194304 | tf_op jit(solution)/shard_map/reshape | solution.py:223
  103.3 2.9 %copy.8.delays_ref = f32[512,1024]{1,0:T(8,128)} copy(f32[512,1024]{0,1:T(8,128)} %reshape.29) | data formatting | bytes 4194304 | tf_op jit(solution)/shard_map/reshape | solution.py:223
  106.2 0.0 copy-start.2
  106.2 1.6 %copy-done.2 = f32[512,1024]{1,0:T(8,128)S(1)} copy-done((f32[512,1024]{1,0:T(8,128)S(1)}, f32[512,1024]{1,0:T(8,128)}, u32[]{:S(2)}) %copy-start.2) | copy-done | bytes 2097176
  107.8 7.7 %shard_map.47.weights_ref = bf16[4,2,512,1024]{3,2,1,0:T(8,128)(2,1)S(1)} custom-call(f32[1]{0:T(128)} %bitcast.5.first_ref, f32[512,1024]{1,0:T(8,128)S(1)} %copy-done.2), custom_call_target="tpu_custom_call" | custom-call | flops 31457280 | bytes 10485760 | tf_op jit(solution)/shard_map/pallas_call | solution.py:135
  115.5 0.0 copy-start
  115.5 3.2 %copy-done = bf16[4,2,512,1024]{3,2,1,0:T(8,128)(2,1)} copy-done((bf16[4,2,512,1024]{3,2,1,0:T(8,128)(2,1)}, bf16[4,2,512,1024]{3,2,1,0:T(8,128)(2,1)S(1)}, u32[]{:S(2)}) %copy-start) | copy-done | bytes 8388632
  118.7 29.1 %all-to-all-done.1.spectra_ref = bf16[256,8,512]{2,1,0:T(8,128)(2,1)S(1)} async-done(((bf16[256,8,512]{2,1,0:T(8,128)(2,1)}), bf16[256,8,512]{2,1,0:T(8,128)(2,1)S(1)}, u32[]{:S(2)}, u32[]{:S(2)}) %all-to-all-start.1) | async-done | bytes 2097184 | tf_op jit(solution)/shard_map/all_to_all | solution.py:232
  147.9 0.0 copy-start.1
  147.9 3.4 %copy-done.1 = bf16[4,2,512,1024]{3,2,1,0:T(8,128)(2,1)S(1)} copy-done((bf16[4,2,512,1024]{3,2,1,0:T(8,128)(2,1)S(1)}, bf16[4,2,512,1024]{3,2,1,0:T(8,128)(2,1)}, u32[]{:S(2)}) %copy-start.1) | copy-done | bytes 8388632
  151.2 7.2 %shard_map.48 = bf16[2,4,512,128]{3,2,1,0:T(8,128)(2,1)} custom-call(bf16[256,8,512]{2,1,0:T(8,128)(2,1)S(1)} %all-to-all-done.1.spectra_ref, bf16[4,2,512,1024]{3,2,1,0:T(8,128)(2,1)S(1)} %copy-done.1), custom_call_target="tpu_custom_call" | custom-call | flops 2147483648 | bytes 11534336 | tf_op jit(solution)/shard_map/pallas_call | solution.py:197
Async XLA Ops:
  35.9 25.7 %copy-start.4 = (f32[16,2048]{1,0:T(8,128)S(1)}, f32[16,2048]{1,0:T(8,128)}, u32[]{:S(2)}) copy-start(f32[16,2048]{1,0:T(8,128)} %coeffs_ref.1) | copy-start | bytes 393220
  35.9 25.7 %collective-permute-start.1 = (bf16[8,16,2048]{2,1,0:T(8,128)(2,1)}, bf16[8,16,2048]{2,1,0:T(8,128)(2,1)S(1)}, u32[]{:S(2)}, u32[]{:S(2)}) collective-permute-start(bf16[8,16,2048]{2,1,0:T(8,128)(2,1)} %bitcast.3), channel_id=1, source_target_pairs={{0,192},{64,0},{128,64},{192,128},{1,193},{65,1},{129,65},{193,129... | collective-permute-start | bytes 1572872 | tf_op jit(solution)/shard_map/ppermute | solution.py:229
  42.9 9.5 %collective-permute-start = (bf16[7,16,2048]{2,1,0:T(8,128)(2,1)}, bf16[7,16,2048]{2,1,0:T(8,128)(2,1)S(1)}, u32[]{:S(2)}, u32[]{:S(2)}) collective-permute-start(bf16[7,16,2048]{2,1,0:T(8,128)(2,1)} %slice.22), channel_id=1, source_target_pairs={{0,64},{64,128},{128,192},{1,65},{65,129},{129,193},{2,66},{66,130... | collective-permute-start | bytes 1376264 | tf_op jit(solution)/shard_map/ppermute | solution.py:228
  61.6 3.4 %copy-start.5 = (bf16[2048,2048]{1,0:T(8,128)(2,1)S(1)}, bf16[2048,2048]{1,0:T(8,128)(2,1)}, u32[]{:S(2)}) copy-start(bf16[2048,2048]{1,0:T(8,128)(2,1)} %constant.35.clone.table_ref) | copy-start | bytes 25165828
  79.0 1.4 copy-start.3
  80.4 67.5 %all-to-all-start.1 = ((bf16[256,8,512]{2,1,0:T(8,128)(2,1)}), bf16[256,8,512]{2,1,0:T(8,128)(2,1)S(1)}, u32[]{:S(2)}, u32[]{:S(2)}) async-start(bf16[256,8,512]{2,1,0:T(8,128)(2,1)} %bitcast.13), calls=%async_computation.1 | async-start | bytes 4194304 | tf_op jit(solution)/shard_map/all_to_all | solution.py:232
  106.2 1.6 %copy-start.2 = (f32[512,1024]{1,0:T(8,128)S(1)}, f32[512,1024]{1,0:T(8,128)}, u32[]{:S(2)}) copy-start(f32[512,1024]{1,0:T(8,128)} %copy.8.delays_ref) | copy-start | bytes 6291460
  115.5 3.2 %copy-start = (bf16[4,2,512,1024]{3,2,1,0:T(8,128)(2,1)}, bf16[4,2,512,1024]{3,2,1,0:T(8,128)(2,1)S(1)}, u32[]{:S(2)}) copy-start(bf16[4,2,512,1024]{3,2,1,0:T(8,128)(2,1)S(1)} %shard_map.47.weights_ref) | copy-start | bytes 25165828
  147.9 3.4 %copy-start.1 = (bf16[4,2,512,1024]{3,2,1,0:T(8,128)(2,1)S(1)}, bf16[4,2,512,1024]{3,2,1,0:T(8,128)(2,1)}, u32[]{:S(2)}) copy-start(bf16[4,2,512,1024]{3,2,1,0:T(8,128)(2,1)} %copy-done) | copy-start | bytes 25165828

commit v2 on v0

v2 whole, which is shorter than its diff:
```python
import math

import jax
import jax.numpy as jnp
import numpy as np
from jax import lax
from jax.experimental import pallas as pl
from jax.experimental.pallas import tpu as pltpu
from jax.sharding import Mesh
from jax.sharding import PartitionSpec as P

CHAN = 1024
FRAME = 2048
TAPS = 16
INPUTS = 1024
BEAMS = 512
FRAMES = 128

ZH, YX, INP, DEVICES = 4, 16, 4, 256
PLANE = FRAMES // ZH
LATE = 8
HALO = LATE // 2
CHUNKS = 2
ROWS = INPUTS // INP // YX // CHUNKS
OWN = CHAN // DEVICES
PLACES = YX * INP
LANES = 128
ALL = ("zh", "y", "x", "zl", "core")


def dft_tables():
    turn = np.arange(FRAME) * (2.0 * np.pi / FRAME)
    index = np.outer(np.arange(CHAN), np.arange(FRAME // 2)) % FRAME
    table = np.stack([np.cos(turn)[index], -np.sin(turn)[index]], axis=1)
    table = table.reshape(CHAN // 2, 2, 2, FRAME // 2).transpose(1, 0, 2, 3)
    return table.reshape(2, CHAN, FRAME // 2).astype(jnp.bfloat16)


def filter_frames(frame, taps, turned, keep):
    frames = [frame(k) for k in range(PLANE + TAPS - 1)]
    for j in range(PLANE):
        newest = TAPS - 1 + j
        near = j - (PLANE - LATE) + 1
        near = near if near > 0 else TAPS
        total = taps[0] * frames[newest]
        for t in range(1, near):
            total = total + taps[t] * frames[newest - t]
        if near < TAPS:
            old = taps[near] * frames[newest - near]
            for t in range(near + 1, TAPS):
                old = old + taps[t] * frames[newest - t]
            total = total + keep * old
        turned[pl.ds(j, ROWS, stride=PLANE), :] = total


def resident(value):
    return pltpu.with_memory_space_constraint(value, pltpu.VMEM)


def spectra_kernel(chunk, keep_ref, prev_ref, own_ref, next_ref, coeffs_ref, table_ref, *refs):
    out_ref, tables, sums, turned, result, table_sems, out_sems = refs[min(chunk, 1) :]
    steps = out_sems.shape[0]
    block = CHAN // steps
    width = ROWS * PLANE

    def table_copy(step):
        cut = pl.ds(step * block, block)
        return pltpu.make_async_copy(table_ref.at[:, cut], tables.at[:, cut], table_sems.at[step])

    def out_copy(step):
        cut = pl.ds(step * block // 4, block // 4)
        lanes = pl.ds(chunk * width, width)
        return pltpu.make_async_copy(result.at[cut], out_ref.at[cut, :, lanes], out_sems.at[step])

    for step in range(steps):
        table_copy(step).start()

    def tile(step, carry):
        for side in range(2):
            base = pl.multiple_of(step * LANES, LANES) + side * (FRAME // 2)

            def frame(k):
                k += 1
                ref = prev_ref if k < LATE else own_ref if k < LATE + PLANE else next_ref
                k = k if k < LATE else k - LATE if k < LATE + PLANE else k - LATE - PLANE
                return ref[k // 2, :, pl.ds(base + (k % 2) * FRAME, LANES)].astype(jnp.float32)

            taps = [coeffs_ref[t : t + 1, pl.ds(base, LANES)] for t in range(TAPS)]
            filter_frames(frame, taps, turned.at[side], keep_ref[0])
        lanes = pl.ds(pl.multiple_of(step * LANES, LANES), LANES)
        first, second = turned[0], turned[1]
        sums[0, :, lanes] = (first + second).astype(jnp.bfloat16)
        sums[1, :, lanes] = (first - second).astype(jnp.bfloat16)
        return carry

    lax.fori_loop(0, FRAME // 2 // LANES, tile, 0)

    upper = lax.broadcasted_iota(jnp.int32, (block // 8, 8, width), 1) < 4
    for step in range(steps):
        table_copy(step).wait()
        cut = slice(step * block, (step + 1) * block)
        even, odd = (
            lax.dot_general(
                tables[k, cut], sums[k], (((1,), (1,)), ((), ())), preferred_element_type=jnp.float32
            ).reshape(block // 8, 8, width)
            * (1.0 / math.sqrt(FRAME))
            for k in range(2)
        )
        one = jnp.where(upper, even, pltpu.roll(odd, 4, 1)).astype(jnp.bfloat16)
        two = jnp.where(upper, pltpu.roll(even, 4, 1), odd).astype(jnp.bfloat16)
        for k in range(block // 8):
            result[step * block // 4 + 2 * k] = one[k]
            result[step * block // 4 + 2 * k + 1] = two[k]
        out_copy(step).start()
    for step in range(steps):
        out_copy(step).wait()


def spectra(chunk, keep, prev, own, following, coeffs, table, earlier=()):
    steps = 4
    vmem = pl.BlockSpec(memory_space=pltpu.VMEM)
    hbm = pl.BlockSpec(memory_space=pl.ANY)
    return pl.pallas_call(
        lambda *refs: spectra_kernel(chunk, *refs),
        in_specs=[pl.BlockSpec(memory_space=pltpu.SMEM)] + [vmem] * 4 + [hbm] + [hbm] * len(earlier),
        out_specs=hbm,
        out_shape=jax.ShapeDtypeStruct((DEVICES, 2 * OWN, CHUNKS * ROWS * PLANE), jnp.bfloat16),
        scratch_shapes=[
            pltpu.VMEM(table.shape, jnp.bfloat16),
            pltpu.VMEM((2, ROWS * PLANE, FRAME // 2), jnp.bfloat16),
            pltpu.VMEM((2, ROWS * PLANE, LANES), jnp.float32),
            pltpu.VMEM((DEVICES, 2 * OWN, ROWS * PLANE), jnp.bfloat16),
            pltpu.SemaphoreType.DMA((steps,)),
            pltpu.SemaphoreType.DMA((steps,)),
        ],
        input_output_aliases={6: 0} if earlier else {},
        compiler_params=pltpu.CompilerParams(vmem_limit_bytes=20 << 20),
        cost_estimate=pl.CostEstimate(
            flops=2 * CHAN * FRAME * ROWS * PLANE, bytes_accessed=7 << 20, transcendentals=0
        ),
    )(keep, prev, own, following, coeffs, table, *earlier)


def fit(values):
    nodes = (np.cos(np.pi * (np.arange(64) + 0.5) / 64) + 1.0) / 8.0
    return [float(v) for v in np.polynomial.Polynomial.fit(nodes, values(np.sqrt(nodes)), 7, domain=[0, 0.25], window=[0, 0.25]).coef]


COS = fit(lambda r: np.cos(2 * np.pi * r))
SIN = fit(lambda r: np.sin(2 * np.pi * r) / r)


def cos_sin(turns):
    rest = turns - jnp.round(turns)
    square = rest * rest
    cos, sin = COS[-1], SIN[-1]
    for a, b in zip(COS[-2::-1], SIN[-2::-1]):
        cos = cos * square + a
        sin = sin * square + b
    return cos, sin * rest


def weights_kernel(first_ref, delays_ref, out_ref):
    block = 16

    def rows(step, carry):
        at = pl.ds(pl.multiple_of(step * block, block), block)
        delay = delays_ref[at] * (1.0 / FRAME)
        step_cos, step_sin = cos_sin(delay)
        cos, sin = cos_sin(delay * first_ref[0])
        for c in range(OWN):
            if c:
                cos, sin = cos * step_cos - sin * step_sin, sin * step_cos + cos * step_sin
            out_ref[c, 0, at] = cos.astype(jnp.bfloat16)
            out_ref[c, 1, at] = (-sin).astype(jnp.bfloat16)
        return carry

    lax.fori_loop(0, BEAMS // block, rows, 0)


def weights(first, delays):
    return pl.pallas_call(
        weights_kernel,
        in_specs=[pl.BlockSpec(memory_space=pltpu.SMEM), pl.BlockSpec(memory_space=pltpu.VMEM)],
        out_specs=pl.BlockSpec(memory_space=pltpu.VMEM),
        out_shape=pltpu.VMEM((OWN, 2, BEAMS, INPUTS), jnp.bfloat16),
        compiler_params=pltpu.CompilerParams(vmem_limit_bytes=14 << 20),
        cost_estimate=pl.CostEstimate(
            flops=60 * BEAMS * INPUTS, bytes_accessed=10 << 20, transcendentals=0
        ),
    )(first, delays)


def arrange(spectra_ref, wide, values):
    lane = lax.broadcasted_iota(jnp.int32, (PLACES, LANES), 1)
    rows = 2 * OWN
    for tile in range(spectra_ref.shape[2] // LANES):
        part = spectra_ref[:, :, tile * LANES : (tile + 1) * LANES]
        wide[...] = part.astype(jnp.float32).reshape(DEVICES * rows, LANES)
        for own in range(OWN):
            for side in range(2):
                row = 4 * (own % 2) + 2 * (own // 2) + side
                a = [wide[pl.ds(zh * PLACES * rows + row, PLACES, stride=rows), :] for zh in range(ZH)]
                for bit in (2, 1):
                    size = bit * PLANE
                    keep = lax.rem(lane, 2 * size) < size
                    for k in range(ZH):
                        if not k & bit:
                            x, y = a[k], a[k + bit]
                            a[k] = jnp.where(keep, x, pltpu.roll(y, size, 1))
                            a[k + bit] = jnp.where(keep, pltpu.roll(x, LANES - size, 1), y)
                for k in range(ZH):
                    at = (tile * ZH + k) * PLACES
                    cut = slice(side * LANES, (side + 1) * LANES)
                    values[own, at : at + PLACES, cut] = a[k].astype(jnp.bfloat16)


def beams_kernel(spectra_ref, weight, out_ref, wide, values):
    arrange(spectra_ref, wide, values)
    for channel in range(OWN):
        here = values[channel]
        by_re = jnp.dot(weight[channel, 0], here, preferred_element_type=jnp.float32)
        by_im = jnp.dot(weight[channel, 1], here, preferred_element_type=jnp.float32)
        parts = (by_re[:, :LANES] - by_im[:, LANES:], by_re[:, LANES:] + by_im[:, :LANES])
        for side, part in enumerate(parts):
            part = pltpu.roll(part, LATE, 1) * (1.0 / math.sqrt(INPUTS))
            out_ref[side, channel] = part.astype(jnp.bfloat16)


def beams(received, weight):
    vmem = pl.BlockSpec(memory_space=pltpu.VMEM)
    return pl.pallas_call(
        beams_kernel,
        in_specs=[vmem, vmem],
        out_specs=vmem,
        out_shape=jax.ShapeDtypeStruct((2, OWN, BEAMS, FRAMES), jnp.bfloat16),
        scratch_shapes=[
            pltpu.VMEM((DEVICES * 2 * OWN, LANES), jnp.float32),
            pltpu.VMEM((OWN, INPUTS, 2 * LANES), jnp.bfloat16),
        ],
        compiler_params=pltpu.CompilerParams(vmem_limit_bytes=20 << 20),
        cost_estimate=pl.CostEstimate(
            flops=8 * OWN * BEAMS * INPUTS * FRAMES, bytes_accessed=11 << 20, transcendentals=0
        ),
    )(received, resident(weight))


def body(samples, coeffs, delays):
    first = (lax.axis_index(ALL) * OWN).astype(jnp.float32).reshape(1)
    keep = jnp.where(lax.axis_index("zh") == ZH - 1, 0.0, 1.0).astype(jnp.float32).reshape(1)
    table = jnp.asarray(dft_tables())
    up = [(i, i + 1) for i in range(ZH - 1)]
    down = [(i, (i - 1) % ZH) for i in range(ZH)]

    step = YX * ROWS
    parts = []
    for h in range(CHUNKS):
        part = samples[h * step : (h + 1) * step].reshape(YX, ROWS, 2 * FRAME)
        part, samples = lax.optimization_barrier((part, samples))
        parts.append(part)
    owns = [lax.all_to_all(part, ("y", "x"), 0, 0, tiled=True) for part in parts]
    blocks = ()
    for h, own in enumerate(owns):
        prev = lax.ppermute(own[YX - HALO :], "zh", up)
        following = lax.ppermute(own[:HALO], "zh", down)
        blocks = (spectra(h, keep, prev, own, following, coeffs, table, blocks),)

    ordered = delays.reshape(BEAMS, INP, CHUNKS, YX, ROWS).transpose(0, 2, 4, 3, 1)
    weight = weights(first, ordered.reshape(BEAMS, INPUTS))
    received = lax.all_to_all(blocks[0], ALL, 0, 0, tiled=True)
    return beams(received, weight)


def solution(mesh):
    fine = Mesh(mesh.devices.reshape(4, 4, 4, 2, 2), ALL)
    in_specs = (P(("zl", "core"), ("zh", "y", "x")), P(), P())
    out_specs = P(None, ALL, None, None)
    return jax.shard_map(body, mesh=fine, in_specs=in_specs, out_specs=out_specs, check_vma=False)
```

time: 1350 us -> 147 us (0.11)
  starting transfers between devices: 573 us -> 41.2 us
  waiting for transfers between devices: 311 us -> 51.7 us
  blocking collectives: 204 us -> 0 us
  matrix products: 135 us -> 0 us
  other arithmetic: 51.1 us -> 0 us
  local copies, waits for them, and re-layouts: 64.8 us -> 28.5 us
  Pallas kernels: 0 us -> 24.4 us
    all_to_all x1 -> x3, starting transfers between devices: 542 us -> 26.6 us  [the longest x1 14.8 us: body(): received = lax.all_to_all(blocks[0], ALL, 0, 0, tiled=True)]
    ppermute x8 -> x4, waiting for transfers between devices: 275 us -> 0.01 us  [the longest x2 0.01 us: body(): following = lax.ppermute(own[:HALO], 'zh', down)]
    unnamed x1 -> x0, blocking collectives: 204 us -> none
    dot_general x6 -> x0, matrix products: 135 us -> none  [the longest x4 113 us: contract(): jnp.einsum('vhu,uav->vha', beam_weight, sample_values, preferred_element_...]
    neg x1 -> x0, other arithmetic: 34.5 us -> none  [transform(): -jnp.sin(angle)]
    reshape x3 -> x4, local copies, waits for them, and re-layouts: 39.3 us -> 9.35 us  [the longest x2 5.86 us: body(): weight = weights(first, ordered.reshape(BEAMS, INPUTS))]
    pallas_call x0 -> x4, Pallas kernels: none -> 24.4 us  [the longest x2 12.5 us: spectra(): pl.pallas_call(lambda *refs: spectra_kernel(chunk, *refs), in_specs=[pl.B...]
    ppermute x8 -> x4, starting transfers between devices: 31.1 us -> 14.6 us  [the longest x2 12 us: body(): following = lax.ppermute(own[:HALO], 'zh', down)]
  transfers between devices with their start and end apart: 9 -> 7, of which waited for: 3 -> 3; matrix products, arithmetic and copies ran while one was open for 3% -> 11% of each run, Pallas kernels for 0% -> 9%
where the time goes in v2:
time: 147 us; the launch traced here: 146 us
  waiting for transfers between devices  51.7 us (35%)
  starting transfers between devices  41.2 us (28%)
  local copies, waits for them, and re-layouts  28.5 us (19%)
  Pallas kernels  24.4 us (17%)
    all_to_all x1, waiting for transfers between devices, body(): received = lax.all_to_all(blocks[0], ALL, 0, 0, tiled=True)  29.8 us
    all_to_all x2, waiting for transfers between devices, body(): lax.all_to_all(part, ('y', 'x'), 0, 0, tiled=True)  21.9 us
    all_to_all x1, starting transfers between devices, body(): received = lax.all_to_all(blocks[0], ALL, 0, 0, tiled=True)  14.8 us
    unnamed x15, local copies, waits for them, and re-layouts  13.3 us
    pallas_call x2, Pallas kernels, spectra(): pl.pallas_call(lambda *refs: spectra_kernel(chunk, *refs), in_specs=[pl.B...  12.5 us
    ppermute x2, starting transfers between devices, body(): following = lax.ppermute(own[:HALO], 'zh', down)  12 us
    all_to_all x2, starting transfers between devices, body(): lax.all_to_all(part, ('y', 'x'), 0, 0, tiled=True)  11.8 us
    pallas_call x1, Pallas kernels, weights(): pl.pallas_call(weights_kernel, in_specs=[pl.BlockSpec(memory_space=pltpu....  7.05 us
  transfers between devices with their start and end apart: 7, of which 3 were waited for; matrix products, arithmetic and copies ran while one was open for 11% of the time, Pallas kernels for 9%

profile of v2, /device:TPU:1, one launch (start us, length us, event | category | flops | bytes accessed | tf_op | source)
XLA Modules:
  0.0 146.0 jit_solution(788878776652668884)
XLA Ops:
  0.0 2.4 %slice_bitcast_fusion.1 = bf16[16,8,4096]{2,1,0:T(8,128)(2,1)} fusion(bf16[256,4096]{1,0:T(8,128)(2,1)} %param.4), kind=kLoop, calls=%fused_computation.1 | loop fusion | bytes 2097152 | tf_op jit(solution)/shard_map/reshape | solution.py:258
  2.5 7.6 %all-to-all-start.1 = ((bf16[16,8,4096]{2,1,0:T(8,128)(2,1)}), bf16[16,8,4096]{2,1,0:T(8,128)(2,1)S(1)}, u32[]{:S(2)}, u32[]{:S(2)}) async-start(bf16[16,8,4096]{2,1,0:T(8,128)(2,1)} %slice_bitcast_fusion.1), calls=%async_computation.1 | async-start | bytes 2097152 | tf_op jit(solution)/shard_map/all_to_all | solution.py:261
  10.0 0.0 copy-done.6
  10.1 1.0 slice_bitcast_fusion
  11.1 14.9 %all-to-all-done.1.refs_2_ = bf16[16,8,4096]{2,1,0:T(8,128)(2,1)S(1)} async-done(((bf16[16,8,4096]{2,1,0:T(8,128)(2,1)}), bf16[16,8,4096]{2,1,0:T(8,128)(2,1)S(1)}, u32[]{:S(2)}, u32[]{:S(2)}) %all-to-all-start.1) | async-done | bytes 1048608 | tf_op jit(solution)/shard_map/all_to_all | solution.py:261
  26.0 4.2 %all-to-all-start = ((bf16[16,8,4096]{2,1,0:T(8,128)(2,1)}), bf16[16,8,4096]{2,1,0:T(8,128)(2,1)S(1)}, u32[]{:S(2)}, u32[]{:S(2)}) async-start(bf16[16,8,4096]{2,1,0:T(8,128)(2,1)} %slice_bitcast_fusion), calls=%async_computation | async-start | bytes 2097152 | tf_op jit(solution)/shard_map/all_to_all | solution.py:261
  30.2 0.7 fusion
  31.0 6.0 %collective-permute-start.3 = (bf16[4,8,4096]{2,1,0:T(8,128)(2,1)}, bf16[4,8,4096]{2,1,0:T(8,128)(2,1)S(1)}, u32[]{:S(2)}, u32[]{:S(2)}) collective-permute-start(bf16[4,8,4096]{2,1,0:T(8,128)(2,1)} %get-tuple-element.11), channel_id=1, source_target_pairs={{0,192},{64,0},{128,64},{192,128},{1,193},{65,1},{129,65},{193,129... | collective-permute-start | bytes 786440 | tf_op jit(solution)/shard_map/ppermute | solution.py:265
  37.0 1.3 collective-permute-start.2
  38.3 7.0 %all-to-all-done.refs_2_ = bf16[16,8,4096]{2,1,0:T(8,128)(2,1)S(1)} async-done(((bf16[16,8,4096]{2,1,0:T(8,128)(2,1)}), bf16[16,8,4096]{2,1,0:T(8,128)(2,1)S(1)}, u32[]{:S(2)}, u32[]{:S(2)}) %all-to-all-start) | async-done | bytes 1048608 | tf_op jit(solution)/shard_map/all_to_all | solution.py:261
  45.3 0.8 fusion.1
  46.1 6.0 %collective-permute-start.1 = (bf16[4,8,4096]{2,1,0:T(8,128)(2,1)}, bf16[4,8,4096]{2,1,0:T(8,128)(2,1)S(1)}, u32[]{:S(2)}, u32[]{:S(2)}) collective-permute-start(bf16[4,8,4096]{2,1,0:T(8,128)(2,1)} %get-tuple-element.13), channel_id=1, source_target_pairs={{0,192},{64,0},{128,64},{192,128},{1,193},{65,1},{129,65},{193,129... | collective-permute-start | bytes 786440 | tf_op jit(solution)/shard_map/ppermute | solution.py:265
  52.1 1.3 collective-permute-start
  53.4 0.0 collective-permute-done.3.refs_3_
  53.5 0.0 collective-permute-done.2.refs_1_
  53.5 0.0 copy-start.2
  53.5 2.2 %copy-done.2 = bf16[2,1024,1024]{2,1,0:T(8,128)(2,1)S(1)} copy-done((bf16[2,1024,1024]{2,1,0:T(8,128)(2,1)S(1)}, bf16[2,1024,1024]{2,1,0:T(8,128)(2,1)}, u32[]{:S(2)}) %copy-start.2) | copy-done | bytes 4194328
  55.7 6.2 %shard_map.46.refs_6_ = bf16[256,8,512]{2,1,0:T(8,128)(2,1)} custom-call(f32[1]{0:T(128)} %bitcast.refs_0_, bf16[4,8,4096]{2,1,0:T(8,128)(2,1)S(1)} %collective-permute-done.2.refs_1_, bf16[16,8,4096]{2,1,0:T(8,128)(2,1)S(1)} %all-to-all-done.1.refs_2_, bf16[4,8,4096]{2,1,0:T(8,128)(2,1)S(1)} %collective-permute-done.3.refs_3_, f32[16,2048]{1,0:T(8,128)S(1)} %copy-done.5, ...), custom_call_target="tpu_custom_call" | custom-call | flops 1073741824 | bytes 7340032 | tf_op jit(solution)/shard_map/pallas_call | solution.py:123
  61.9 0.0 collective-permute-done.1.refs_3_
  61.9 0.0 collective-permute-done.refs_1_
  61.9 6.2 %shard_map.47 = bf16[256,8,512]{2,1,0:T(8,128)(2,1)} custom-call(f32[1]{0:T(128)} %bitcast.refs_0_, bf16[4,8,4096]{2,1,0:T(8,128)(2,1)S(1)} %collective-permute-done.refs_1_, bf16[16,8,4096]{2,1,0:T(8,128)(2,1)S(1)} %all-to-all-done.refs_2_, bf16[4,8,4096]{2,1,0:T(8,128)(2,1)S(1)} %collective-permute-done.1.refs_3_, ...), custom_call_target="tpu_custom_call", output_to_operand_aliasing={{}: (6, {})} | custom-call | flops 1073741824 | bytes 7340032 | tf_op jit(solution)/shard_map/pallas_call | solution.py:123
  68.2 14.8 %all-to-all-start.2 = ((bf16[256,8,512]{2,1,0:T(8,128)(2,1)}), bf16[256,8,512]{2,1,0:T(8,128)(2,1)S(1)}, u32[]{:S(2)}, u32[]{:S(2)}) async-start(bf16[256,8,512]{2,1,0:T(8,128)(2,1)} %shard_map.47), calls=%async_computation.2 | async-start | bytes 4194304 | tf_op jit(solution)/shard_map/all_to_all | solution.py:270
  83.0 2.9 %copy.7 = f32[512,1024]{0,1:T(8,128)} copy(f32[512,1024]{1,0:T(8,128)} %param.6) | data formatting | bytes 4194304 | tf_op args[2]
  85.9 4.3 %copy.8 = f32[512,2,8,16,4]{0,4,3,2,1:T(4,128)} copy(f32[512,2,8,16,4]{0,2,3,1,4:T(8,128)} %bitcast.11) | data formatting | bytes 4194304 | tf_op jit(solution)/shard_map/transpose | solution.py:268
  90.2 3.0 %reshape.23 = f32[512,1024]{0,1:T(8,128)} reshape(f32[512,2,8,16,4]{0,4,3,2,1:T(4,128)} %copy.8) | data formatting | bytes 4194304 | tf_op jit(solution)/shard_map/reshape | solution.py:269
  93.1 2.9 %copy.9.delays_ref = f32[512,1024]{1,0:T(8,128)} copy(f32[512,1024]{0,1:T(8,128)} %reshape.23) | data formatting | bytes 4194304 | tf_op jit(solution)/shard_map/reshape | solution.py:269
  96.1 1.6 %copy-done.4 = f32[512,1024]{1,0:T(8,128)S(1)} copy-done((f32[512,1024]{1,0:T(8,128)S(1)}, f32[512,1024]{1,0:T(8,128)}, u32[]{:S(2)}) %copy-start.4) | copy-done | bytes 2097176
  97.6 7.1 %shard_map.48.weight = bf16[4,2,512,1024]{3,2,1,0:T(8,128)(2,1)S(1)} custom-call(f32[1]{0:T(128)} %bitcast.3.first_ref, f32[512,1024]{1,0:T(8,128)S(1)} %copy-done.4), custom_call_target="tpu_custom_call" | custom-call | flops 31457280 | bytes 10485760 | tf_op jit(solution)/shard_map/pallas_call | solution.py:182
  104.7 3.2 %copy-done = bf16[4,2,512,1024]{3,2,1,0:T(8,128)(2,1)} copy-done((bf16[4,2,512,1024]{3,2,1,0:T(8,128)(2,1)}, bf16[4,2,512,1024]{3,2,1,0:T(8,128)(2,1)S(1)}, u32[]{:S(2)}) %copy-start) | copy-done | bytes 8388632
  107.9 29.8 %all-to-all-done.2.spectra_ref = bf16[256,8,512]{2,1,0:T(8,128)(2,1)S(1)} async-done(((bf16[256,8,512]{2,1,0:T(8,128)(2,1)}), bf16[256,8,512]{2,1,0:T(8,128)(2,1)S(1)}, u32[]{:S(2)}, u32[]{:S(2)}) %all-to-all-start.2) | async-done | bytes 2097184 | tf_op jit(solution)/shard_map/all_to_all | solution.py:270
  137.7 3.4 %copy-done.1 = bf16[4,2,512,1024]{3,2,1,0:T(8,128)(2,1)S(1)} copy-done((bf16[4,2,512,1024]{3,2,1,0:T(8,128)(2,1)S(1)}, bf16[4,2,512,1024]{3,2,1,0:T(8,128)(2,1)}, u32[]{:S(2)}) %copy-start.1) | copy-done | bytes 8388632
  141.1 4.9 %shard_map.49 = bf16[2,4,512,128]{3,2,1,0:T(8,128)(2,1)} custom-call(bf16[256,8,512]{2,1,0:T(8,128)(2,1)S(1)} %all-to-all-done.2.spectra_ref, bf16[4,2,512,1024]{3,2,1,0:T(8,128)(2,1)S(1)} %copy-done.1), custom_call_target="tpu_custom_call" | custom-call | flops 2147483648 | bytes 11534336 | tf_op jit(solution)/shard_map/pallas_call | solution.py:232
  (8 shorter events, 0.0 us)
Async XLA Ops:
  0.0 10.0 %copy-start.6 = (bf16[256,4096]{1,0:T(8,128)(2,1)S(1)}, bf16[256,4096]{1,0:T(8,128)(2,1)}, u32[]{:S(2)}) copy-start(bf16[256,4096]{1,0:T(8,128)(2,1)} %param.4) | copy-start | bytes 6291460
  2.5 23.6 %all-to-all-start.1 = ((bf16[16,8,4096]{2,1,0:T(8,128)(2,1)}), bf16[16,8,4096]{2,1,0:T(8,128)(2,1)S(1)}, u32[]{:S(2)}, u32[]{:S(2)}) async-start(bf16[16,8,4096]{2,1,0:T(8,128)(2,1)} %slice_bitcast_fusion.1), calls=%async_computation.1 | async-start | bytes 2097152 | tf_op jit(solution)/shard_map/all_to_all | solution.py:261
  11.1 42.4 %copy-start.5 = (f32[16,2048]{1,0:T(8,128)S(1)}, f32[16,2048]{1,0:T(8,128)}, u32[]{:S(2)}) copy-start(f32[16,2048]{1,0:T(8,128)} %refs_4_.3) | copy-start | bytes 393220
  26.0 19.3 %all-to-all-start = ((bf16[16,8,4096]{2,1,0:T(8,128)(2,1)}), bf16[16,8,4096]{2,1,0:T(8,128)(2,1)S(1)}, u32[]{:S(2)}, u32[]{:S(2)}) async-start(bf16[16,8,4096]{2,1,0:T(8,128)(2,1)} %slice_bitcast_fusion), calls=%async_computation | async-start | bytes 2097152 | tf_op jit(solution)/shard_map/all_to_all | solution.py:261
  31.0 22.5 %collective-permute-start.3 = (bf16[4,8,4096]{2,1,0:T(8,128)(2,1)}, bf16[4,8,4096]{2,1,0:T(8,128)(2,1)S(1)}, u32[]{:S(2)}, u32[]{:S(2)}) collective-permute-start(bf16[4,8,4096]{2,1,0:T(8,128)(2,1)} %get-tuple-element.11), channel_id=1, source_target_pairs={{0,192},{64,0},{128,64},{192,128},{1,193},{65,1},{129,65},{193,129... | collective-permute-start | bytes 786440 | tf_op jit(solution)/shard_map/ppermute | solution.py:265
  37.0 16.5 %collective-permute-start.2 = (bf16[4,8,4096]{2,1,0:T(8,128)(2,1)S(1)}, bf16[4,8,4096]{2,1,0:T(8,128)(2,1)S(1)}, u32[]{:S(2)}, u32[]{:S(2)}) collective-permute-start(bf16[4,8,4096]{2,1,0:T(8,128)(2,1)S(1)} %get-tuple-element.12), channel_id=1, source_target_pairs={{0,64},{64,128},{128,192},{1,65},{65,129},{129,193},{2,66},{66,130... | collective-permute-start | bytes 786440 | tf_op jit(solution)/shard_map/ppermute | solution.py:264
  46.1 15.8 %collective-permute-start.1 = (bf16[4,8,4096]{2,1,0:T(8,128)(2,1)}, bf16[4,8,4096]{2,1,0:T(8,128)(2,1)S(1)}, u32[]{:S(2)}, u32[]{:S(2)}) collective-permute-start(bf16[4,8,4096]{2,1,0:T(8,128)(2,1)} %get-tuple-element.13), channel_id=1, source_target_pairs={{0,192},{64,0},{128,64},{192,128},{1,193},{65,1},{129,65},{193,129... | collective-permute-start | bytes 786440 | tf_op jit(solution)/shard_map/ppermute | solution.py:265
  52.1 9.8 %collective-permute-start = (bf16[4,8,4096]{2,1,0:T(8,128)(2,1)}, bf16[4,8,4096]{2,1,0:T(8,128)(2,1)S(1)}, u32[]{:S(2)}, u32[]{:S(2)}) collective-permute-start(bf16[4,8,4096]{2,1,0:T(8,128)(2,1)} %get-tuple-element.14), channel_id=1, source_target_pairs={{0,64},{64,128},{128,192},{1,65},{65,129},{129,193},{2,66},{66,130... | collective-permute-start | bytes 786440 | tf_op jit(solution)/shard_map/ppermute | solution.py:264
  53.5 2.2 %copy-start.2 = (bf16[2,1024,1024]{2,1,0:T(8,128)(2,1)S(1)}, bf16[2,1024,1024]{2,1,0:T(8,128)(2,1)}, u32[]{:S(2)}) copy-start(bf16[2,1024,1024]{2,1,0:T(8,128)(2,1)} %constant.35.clone.refs_5_) | copy-start | bytes 12582916
  55.7 6.2 %copy-start.3 = (bf16[2,1024,1024]{2,1,0:T(8,128)(2,1)S(1)}, bf16[2,1024,1024]{2,1,0:T(8,128)(2,1)}, u32[]{:S(2)}) copy-start(bf16[2,1024,1024]{2,1,0:T(8,128)(2,1)} %constant.35.clone.refs_5_) | copy-start | bytes 12582916
  68.2 69.5 %all-to-all-start.2 = ((bf16[256,8,512]{2,1,0:T(8,128)(2,1)}), bf16[256,8,512]{2,1,0:T(8,128)(2,1)S(1)}, u32[]{:S(2)}, u32[]{:S(2)}) async-start(bf16[256,8,512]{2,1,0:T(8,128)(2,1)} %shard_map.47), calls=%async_computation.2 | async-start | bytes 4194304 | tf_op jit(solution)/shard_map/all_to_all | solution.py:270
  96.1 1.6 %copy-start.4 = (f32[512,1024]{1,0:T(8,128)S(1)}, f32[512,1024]{1,0:T(8,128)}, u32[]{:S(2)}) copy-start(f32[512,1024]{1,0:T(8,128)} %copy.9.delays_ref) | copy-start | bytes 6291460
  104.7 3.2 %copy-start = (bf16[4,2,512,1024]{3,2,1,0:T(8,128)(2,1)}, bf16[4,2,512,1024]{3,2,1,0:T(8,128)(2,1)S(1)}, u32[]{:S(2)}) copy-start(bf16[4,2,512,1024]{3,2,1,0:T(8,128)(2,1)S(1)} %shard_map.48.weight) | copy-start | bytes 25165828
  137.7 3.4 %copy-start.1 = (bf16[4,2,512,1024]{3,2,1,0:T(8,128)(2,1)S(1)}, bf16[4,2,512,1024]{3,2,1,0:T(8,128)(2,1)}, u32[]{:S(2)}) copy-start(bf16[4,2,512,1024]{3,2,1,0:T(8,128)(2,1)} %copy-done) | copy-start | bytes 25165828

commit v3 on v2

v3 whole, which is shorter than its diff:
```python
import math

import jax
import jax.numpy as jnp
import numpy as np
from jax import lax
from jax.experimental import pallas as pl
from jax.experimental.pallas import tpu as pltpu
from jax.sharding import Mesh
from jax.sharding import PartitionSpec as P

CHAN = 1024
FRAME = 2048
TAPS = 16
INPUTS = 1024
BEAMS = 512
FRAMES = 128

ZH, YX, INP, DEVICES = 4, 16, 4, 256
PLANE = FRAMES // ZH
LATE = 8
HALO = LATE // 2
PART = PLANE // 2
ROWS = INPUTS // INP // YX
OWN = CHAN // DEVICES
PLACES = YX * INP
LANES = 128
ALL = ("zh", "y", "x", "zl", "core")


def dft_tables():
    turn = np.arange(FRAME) * (2.0 * np.pi / FRAME)
    index = np.outer(np.arange(CHAN), np.arange(FRAME // 2)) % FRAME
    table = np.stack([np.cos(turn)[index], -np.sin(turn)[index]], axis=1)
    table = table.reshape(CHAN // 2, 2, 2, FRAME // 2).transpose(1, 0, 2, 3)
    return table.reshape(2, CHAN, FRAME // 2).astype(jnp.bfloat16)


def filter_frames(frame, count, taps, turned, at, keep=None):
    frames = [frame(k) for k in range(count + TAPS - 1)]
    for j in range(count):
        newest = TAPS - 1 + j
        near = TAPS if keep is None else j + 1
        total = taps[0] * frames[newest]
        for t in range(1, near):
            total = total + taps[t] * frames[newest - t]
        if near < TAPS:
            old = taps[near] * frames[newest - near]
            for t in range(near + 1, TAPS):
                old = old + taps[t] * frames[newest - t]
            total = total + keep * old
        turned[pl.ds(at + j, ROWS, stride=PART), :] = total


def resident(value):
    return pltpu.with_memory_space_constraint(value, pltpu.VMEM)


def spectra_kernel(outer, *refs):
    if outer:
        keep_ref, prev_ref, next_ref, own_ref, coeffs_ref, table_ref, _, out_ref, *scratch = refs
    else:
        own_ref, coeffs_ref, table_ref, out_ref, *scratch = refs
    tables, sums, turned, result, table_sems, out_sems = scratch
    steps = out_sems.shape[0]
    block = CHAN // steps

    def table_copy(step):
        cut = pl.ds(step * block, block)
        return pltpu.make_async_copy(table_ref.at[:, cut], tables.at[:, cut], table_sems.at[step])

    def out_copy(step):
        cut = pl.ds(step * block // 4, block // 4)
        lanes = pl.ds(int(outer) * ROWS * PART, ROWS * PART)
        return pltpu.make_async_copy(result.at[cut], out_ref.at[cut, :, lanes], out_sems.at[step])

    for step in range(steps):
        table_copy(step).start()

    def tile(step, carry):
        for side in range(2):
            base = pl.multiple_of(step * LANES, LANES) + side * (FRAME // 2)

            def load(ref, k):
                return ref[k // 2, :, pl.ds(base + (k % 2) * FRAME, LANES)].astype(jnp.float32)

            def late(k):
                k += PLANE + LATE - (TAPS - 1 + LATE)
                return load(own_ref, k) if k < PLANE else load(next_ref, k - PLANE)

            def early(k):
                k -= TAPS - 1 - LATE
                return load(own_ref, k) if k >= 0 else load(prev_ref, k + LATE)

            taps = [coeffs_ref[t : t + 1, pl.ds(base, LANES)] for t in range(TAPS)]
            if outer:
                filter_frames(late, LATE, taps, turned.at[side], 0, keep_ref[0])
                filter_frames(early, LATE, taps, turned.at[side], LATE)
            else:
                filter_frames(lambda k: load(own_ref, k + 1), PART, taps, turned.at[side], 0)
        lanes = pl.ds(pl.multiple_of(step * LANES, LANES), LANES)
        first, second = turned[0], turned[1]
        sums[0, :, lanes] = (first + second).astype(jnp.bfloat16)
        sums[1, :, lanes] = (first - second).astype(jnp.bfloat16)
        return carry

    lax.fori_loop(0, FRAME // 2 // LANES, tile, 0)

    width = ROWS * PART
    upper = lax.broadcasted_iota(jnp.int32, (block // 8, 8, width), 1) < 4
    for step in range(steps):
        table_copy(step).wait()
        cut = slice(step * block, (step + 1) * block)
        even, odd = (
            lax.dot_general(
                tables[k, cut], sums[k], (((1,), (1,)), ((), ())), preferred_element_type=jnp.float32
            ).reshape(block // 8, 8, width)
            * (1.0 / math.sqrt(FRAME))
            for k in range(2)
        )
        one = jnp.where(upper, even, pltpu.roll(odd, 4, 1)).astype(jnp.bfloat16)
        two = jnp.where(upper, pltpu.roll(even, 4, 1), odd).astype(jnp.bfloat16)
        for k in range(block // 8):
            result[step * block // 4 + 2 * k] = one[k]
            result[step * block // 4 + 2 * k + 1] = two[k]
        out_copy(step).start()
    for step in range(steps):
        out_copy(step).wait()


def spectra(own, coeffs, table, halo=(), inner=()):
    steps = 4
    outer = len(halo) > 0
    vmem = pl.BlockSpec(memory_space=pltpu.VMEM)
    hbm = pl.BlockSpec(memory_space=pl.ANY)
    return pl.pallas_call(
        lambda *refs: spectra_kernel(outer, *refs),
        in_specs=([pl.BlockSpec(memory_space=pltpu.SMEM), vmem, vmem] if outer else [])
        + [vmem, vmem, hbm]
        + [hbm] * outer,
        out_specs=hbm,
        out_shape=jax.ShapeDtypeStruct((DEVICES, 2 * OWN, ROWS * PLANE), jnp.bfloat16),
        scratch_shapes=[
            pltpu.VMEM(table.shape, jnp.bfloat16),
            pltpu.VMEM((2, ROWS * PART, FRAME // 2), jnp.bfloat16),
            pltpu.VMEM((2, ROWS * PART, LANES), jnp.float32),
            pltpu.VMEM((DEVICES, 2 * OWN, ROWS * PART), jnp.bfloat16),
            pltpu.SemaphoreType.DMA((steps,)),
            pltpu.SemaphoreType.DMA((steps,)),
        ],
        input_output_aliases={6: 0} if outer else {},
        compiler_params=pltpu.CompilerParams(vmem_limit_bytes=20 << 20),
        cost_estimate=pl.CostEstimate(
            flops=2 * CHAN * FRAME * ROWS * PART, bytes_accessed=7 << 20, transcendentals=0
        ),
    )(*halo, own, coeffs, pltpu.with_memory_space_constraint(table, pltpu.HBM), *inner)


def fit(values):
    nodes = (np.cos(np.pi * (np.arange(64) + 0.5) / 64) + 1.0) / 8.0
    return [float(v) for v in np.polynomial.Polynomial.fit(nodes, values(np.sqrt(nodes)), 7, domain=[0, 0.25], window=[0, 0.25]).coef]


COS = fit(lambda r: np.cos(2 * np.pi * r))
SIN = fit(lambda r: np.sin(2 * np.pi * r) / r)


def cos_sin(turns):
    rest = turns - jnp.round(turns)
    square = rest * rest
    cos, sin = COS[-1], SIN[-1]
    for a, b in zip(COS[-2::-1], SIN[-2::-1]):
        cos = cos * square + a
        sin = sin * square + b
    return cos, sin * rest


def input_order():
    order = np.arange(INPUTS).reshape(INP, YX, ROWS).transpose(2, 1, 0).reshape(-1)
    return (np.arange(INPUTS)[:, None] == order).astype(jnp.bfloat16)


def weights_kernel(first_ref, delays_ref, order_ref, out_ref, delays):
    block = 128

    def reorder(step, carry):
        at = pl.ds(pl.multiple_of(step * block, block), block)
        rest = delays_ref[at]
        total = jnp.zeros_like(rest)
        for _ in range(3):
            part = rest.astype(jnp.bfloat16)
            rest = rest - part.astype(jnp.float32)
            total = total + jnp.dot(part, order_ref[...], preferred_element_type=jnp.float32)
        delays[at] = total * (1.0 / FRAME)
        return carry

    lax.fori_loop(0, BEAMS // block, reorder, 0)
    block = 16

    def rows(step, carry):
        at = pl.ds(pl.multiple_of(step * block, block), block)
        delay = delays[at]
        step_cos, step_sin = cos_sin(delay)
        cos, sin = cos_sin(delay * first_ref[0])
        for c in range(OWN):
            if c:
                cos, sin = cos * step_cos - sin * step_sin, sin * step_cos + cos * step_sin
            out_ref[c, 0, at] = cos.astype(jnp.bfloat16)
            out_ref[c, 1, at] = (-sin).astype(jnp.bfloat16)
        return carry

    lax.fori_loop(0, BEAMS // block, rows, 0)


def weights(first, delays):
    vmem = pl.BlockSpec(memory_space=pltpu.VMEM)
    return pl.pallas_call(
        weights_kernel,
        in_specs=[pl.BlockSpec(memory_space=pltpu.SMEM), vmem, vmem],
        out_specs=vmem,
        out_shape=pltpu.VMEM((OWN, 2, BEAMS, INPUTS), jnp.bfloat16),
        scratch_shapes=[pltpu.VMEM((BEAMS, INPUTS), jnp.float32)],
        compiler_params=pltpu.CompilerParams(vmem_limit_bytes=20 << 20),
        cost_estimate=pl.CostEstimate(
            flops=60 * BEAMS * INPUTS, bytes_accessed=12 << 20, transcendentals=0
        ),
    )(first, delays, jnp.asarray(input_order()))


def arrange(spectra_ref, wide, values):
    lane = lax.broadcasted_iota(jnp.int32, (PLACES, LANES), 1)
    group = LANES // PART
    rows = 2 * OWN
    for half in range(ROWS // group):
        for inner in range(2):
            at = (half if inner else half + ROWS // group) * LANES
            part = spectra_ref[:, :, at : at + LANES]
            wide[inner] = part.astype(jnp.float32).reshape(DEVICES * rows, LANES)
        for own in range(OWN):
            for side in range(2):
                row = 4 * (own % 2) + 2 * (own // 2) + side
                a = [
                    wide[inner, pl.ds(zh * PLACES * rows + row, PLACES, stride=rows), :]
                    for zh in range(ZH)
                    for inner in range(2)
                ]
                for bit in (4, 2, 1):
                    keep = lax.rem(lane, 2 * bit * PART) < bit * PART
                    for k in range(group):
                        if not k & bit:
                            x, y = a[k], a[k + bit]
                            a[k] = jnp.where(keep, x, pltpu.roll(y, bit * PART, 1))
                            a[k + bit] = jnp.where(keep, pltpu.roll(x, LANES - bit * PART, 1), y)
                for k in range(group):
                    at = (half * group + k) * PLACES
                    cut = slice(side * LANES, (side + 1) * LANES)
                    values[own, at : at + PLACES, cut] = a[k].astype(jnp.bfloat16)


def beams_kernel(spectra_ref, weight, out_ref, wide, values):
    arrange(spectra_ref, wide, values)
    lane = lax.broadcasted_iota(jnp.int32, (BEAMS, LANES), 1)
    taken_over = lax.rem(lane, PLANE) < LATE
    for channel in range(OWN):
        here = values[channel]
        by_re = jnp.dot(weight[channel, 0], here, preferred_element_type=jnp.float32)
        by_im = jnp.dot(weight[channel, 1], here, preferred_element_type=jnp.float32)
        parts = (by_re[:, :LANES] - by_im[:, LANES:], by_re[:, LANES:] + by_im[:, :LANES])
        for side, part in enumerate(parts):
            part = jnp.where(taken_over, pltpu.roll(part, PLANE, 1), part) * (1.0 / math.sqrt(INPUTS))
            out_ref[side, channel] = part.astype(jnp.bfloat16)


def beams(received, weight):
    vmem = pl.BlockSpec(memory_space=pltpu.VMEM)
    return pl.pallas_call(
        beams_kernel,
        in_specs=[vmem, vmem],
        out_specs=vmem,
        out_shape=jax.ShapeDtypeStruct((2, OWN, BEAMS, FRAMES), jnp.bfloat16),
        scratch_shapes=[
            pltpu.VMEM((2, DEVICES * 2 * OWN, LANES), jnp.float32),
            pltpu.VMEM((OWN, INPUTS, 2 * LANES), jnp.bfloat16),
        ],
        compiler_params=pltpu.CompilerParams(vmem_limit_bytes=20 << 20),
        cost_estimate=pl.CostEstimate(
            flops=8 * OWN * BEAMS * INPUTS * FRAMES, bytes_accessed=11 << 20, transcendentals=0
        ),
    )(received, resident(weight))


def body(samples, coeffs, delays):
    first = (lax.axis_index(ALL) * OWN).astype(jnp.float32).reshape(1)
    keep = jnp.where(lax.axis_index("zh") == ZH - 1, 0.0, 1.0).astype(jnp.float32).reshape(1)
    table = jnp.asarray(dft_tables())
    up = [(i, i + 1) for i in range(ZH - 1)]
    down = [(i, (i - 1) % ZH) for i in range(ZH)]

    own = lax.all_to_all(samples.reshape(YX, ROWS, 2 * FRAME), ("y", "x"), 0, 0, tiled=True)
    prev = lax.ppermute(own[YX - HALO :], "zh", up)
    following = lax.ppermute(own[:HALO], "zh", down)
    weight = weights(first, delays)
    inner = spectra(own, coeffs, table)
    prev, weight = lax.optimization_barrier((prev, weight))
    blocks = spectra(own, coeffs, table, (keep, prev, following), (inner,))
    received = lax.all_to_all(blocks, ALL, 0, 0, tiled=True)
    return beams(received, weight)


def solution(mesh):
    fine = Mesh(mesh.devices.reshape(4, 4, 4, 2, 2), ALL)
    in_specs = (P(("zl", "core"), ("zh", "y", "x")), P(), P())
    out_specs = P(None, ALL, None, None)
    return jax.shard_map(body, mesh=fine, in_specs=in_specs, out_specs=out_specs, check_vma=False)
```

time: 147 us -> 143 us (0.973)
  blocking collectives: 0 us -> 97.9 us
  waiting for transfers between devices: 51.7 us -> 5.68 us
  starting transfers between devices: 41.2 us -> 7.38 us
  local copies, waits for them, and re-layouts: 28.5 us -> 4.21 us
  Pallas kernels: 24.4 us -> 27.3 us
    all_to_all x0 -> x2, blocking collectives: none -> 97.9 us  [the longest x1 62.9 us: body(): received = lax.all_to_all(blocks, ALL, 0, 0, tiled=True)]
    all_to_all x3 -> x0, waiting for transfers between devices: 51.7 us -> none  [the longest x1 29.8 us: body(): received = lax.all_to_all(blocks[0], ALL, 0, 0, tiled=True)]
    all_to_all x3 -> x0, starting transfers between devices: 26.6 us -> none  [the longest x1 14.8 us: body(): received = lax.all_to_all(blocks[0], ALL, 0, 0, tiled=True)]
    unnamed x15 -> x6, local copies, waits for them, and re-layouts: 13.3 us -> 3.18 us
    ppermute x2 -> x1, starting transfers between devices: 12 us -> 2.46 us  [body(): following = lax.ppermute(own[:HALO], 'zh', down)]
    reshape x4 -> x0, local copies, waits for them, and re-layouts: 9.35 us -> none  [the longest x2 5.86 us: body(): weight = weights(first, ordered.reshape(BEAMS, INPUTS))]
    ppermute x2 -> x1, waiting for transfers between devices: 0.01 us -> 5.68 us  [body(): following = lax.ppermute(own[:HALO], 'zh', down)]
    transpose x1 -> x0, local copies, waits for them, and re-layouts: 4.28 us -> none  [body(): delays.reshape(BEAMS, INP, CHUNKS, YX, ROWS).transpose(0, 2, 4, 3, 1)]
  transfers between devices with their start and end apart: 7 -> 2, of which waited for: 3 -> 1; matrix products, arithmetic and copies ran while one was open for 11% -> 0% of each run, Pallas kernels for 9% -> 11%
where the time goes in v3:
time: 143 us
  blocking collectives  97.9 us (68%)
  Pallas kernels  27.3 us (19%)
  starting transfers between devices  7.38 us (5%)
  waiting for transfers between devices  5.68 us (4%)
  local copies, waits for them, and re-layouts  4.21 us (3%)
    all_to_all x1, blocking collectives, body(): received = lax.all_to_all(blocks, ALL, 0, 0, tiled=True)  62.9 us
    all_to_all x1, blocking collectives, body(): lax.all_to_all(samples.reshape(YX, ROWS, 2 * FRAME), ('y', 'x'), 0, 0, ti...  34.9 us
    pallas_call x1, Pallas kernels, weights(): pl.pallas_call(weights_kernel, in_specs=[pl.BlockSpec(memory_space=pltpu....  10.9 us
    pallas_call x2, Pallas kernels, spectra(): pl.pallas_call(lambda *refs: spectra_kernel(outer, *refs), in_specs=([pl....  10.8 us
    ppermute x1, waiting for transfers between devices, body(): following = lax.ppermute(own[:HALO], 'zh', down)  5.68 us
    pallas_call x1, Pallas kernels, beams(): pl.pallas_call(beams_kernel, in_specs=[vmem, vmem], out_specs=vmem, out_s...  5.63 us
    ppermute x1, starting transfers between devices, body(): prev = lax.ppermute(own[YX - HALO:], 'zh', up)  4.92 us
    unnamed x6, local copies, waits for them, and re-layouts  3.18 us
  transfers between devices with their start and end apart: 2, of which 1 were waited for; matrix products, arithmetic and copies ran while one was open for 0% of the time, Pallas kernels for 11%

profile of v3, /device:TPU:1, one launch (start us, length us, event | category | flops | bytes accessed | tf_op | source)
XLA Modules:
  0.0 142.5 jit_solution(2879603383551302653)
XLA Ops:
  0.0 34.9 %all_to_all.10.refs_0_.refs_3_ = bf16[16,16,4096]{2,1,0:T(8,128)(2,1)S(1)} all-to-all(bf16[16,16,4096]{2,1,0:T(8,128)(2,1)} %bitcast.3), channel_id=1, replica_groups=mesh['zh'=4,'y'=4,'x'=4,'zl'=2,'core'=2] {'y','x'}, dimensions={0} | all-to-all | bytes 4194304 | tf_op jit(solution)/shard_map/all_to_all | solution.py:299
  34.9 1.0 fusion
  36.0 4.9 %collective-permute-start = (bf16[4,16,4096]{2,1,0:T(8,128)(2,1)}, bf16[4,16,4096]{2,1,0:T(8,128)(2,1)S(1)}, u32[]{:S(2)}, u32[]{:S(2)}) collective-permute-start(bf16[4,16,4096]{2,1,0:T(8,128)(2,1)} %get-tuple-element.10), channel_id=1, source_target_pairs={{0,64},{64,128},{128,192},{1,65},{65,129},{129,193},{2,66},{66,130... | collective-permute-start | bytes 1572872 | tf_op jit(solution)/shard_map/ppermute | solution.py:300
  40.9 2.5 %collective-permute-start.1 = (bf16[4,16,4096]{2,1,0:T(8,128)(2,1)}, bf16[4,16,4096]{2,1,0:T(8,128)(2,1)S(1)}, u32[]{:S(2)}, u32[]{:S(2)}) collective-permute-start(bf16[4,16,4096]{2,1,0:T(8,128)(2,1)} %get-tuple-element.9), channel_id=1, source_target_pairs={{0,192},{64,0},{128,64},{192,128},{1,193},{65,1},{129,65},{193,129... | collective-permute-start | bytes 1572872 | tf_op jit(solution)/shard_map/ppermute | solution.py:301
  43.4 0.0 copy-start
  43.4 1.6 %copy-done = f32[512,1024]{1,0:T(8,128)S(1)} copy-done((f32[512,1024]{1,0:T(8,128)S(1)}, f32[512,1024]{1,0:T(8,128)}, u32[]{:S(2)}) %copy-start) | copy-done | bytes 2097176
  45.0 0.0 copy-start.1
  45.0 1.6 %copy-done.1 = bf16[1024,1024]{1,0:T(8,128)(2,1)S(1)} copy-done((bf16[1024,1024]{1,0:T(8,128)(2,1)S(1)}, bf16[1024,1024]{1,0:T(8,128)(2,1)}, u32[]{:S(2)}) %copy-start.1) | copy-done | bytes 2097176
  46.5 0.0 copy-start.2
  46.5 10.9 %shard_map.55.weight = bf16[4,2,512,1024]{3,2,1,0:T(8,128)(2,1)S(1)} custom-call(f32[1]{0:T(128)} %bitcast.2.first_ref, f32[512,1024]{1,0:T(8,128)S(1)} %copy-done, bf16[1024,1024]{1,0:T(8,128)(2,1)S(1)} %copy-done.1), custom_call_target="tpu_custom_call" | custom-call | flops 31457280 | bytes 12582912 | tf_op jit(solution)/shard_map/pallas_call | solution.py:217
  57.5 0.0 copy-done.2
  57.5 5.3 %shard_map.56.refs_6_ = bf16[256,8,512]{2,1,0:T(8,128)(2,1)S(1)} custom-call(bf16[16,16,4096]{2,1,0:T(8,128)(2,1)S(1)} %all_to_all.10.refs_0_.refs_3_, f32[16,2048]{1,0:T(8,128)S(1)} %copy-done.2, bf16[2,1024,1024]{2,1,0:T(8,128)(2,1)} %constant.37.clone.refs_2_.refs_5_), custom_call_target="tpu_custom_call" | custom-call | flops 1073741824 | bytes 7340032 | tf_op jit(solution)/shard_map/pallas_call | solution.py:136
  62.8 0.0 collective-permute-done.refs_1_
  62.8 5.7 %collective-permute-done.1.refs_2_ = bf16[4,16,4096]{2,1,0:T(8,128)(2,1)S(1)} collective-permute-done((bf16[4,16,4096]{2,1,0:T(8,128)(2,1)}, bf16[4,16,4096]{2,1,0:T(8,128)(2,1)S(1)}, u32[]{:S(2)}, u32[]{:S(2)}) %collective-permute-start.1) | collective-permute-done | bytes 524320 | tf_op jit(solution)/shard_map/ppermute | solution.py:301
  68.5 5.5 %shard_map.57 = bf16[256,8,512]{2,1,0:T(8,128)(2,1)S(1)} custom-call(f32[1]{0:T(128)} %bitcast.refs_0_, bf16[4,16,4096]{2,1,0:T(8,128)(2,1)S(1)} %collective-permute-done.refs_1_, bf16[4,16,4096]{2,1,0:T(8,128)(2,1)S(1)} %collective-permute-done.1.refs_2_, bf16[16,16,4096]{2,1,0:T(8,128)(2,1)S(1)} %all_to_all.10.refs_0_.refs_3_, ...), custom_call_target="tpu_custom_call", output_to_operand_aliasing={{}: (6, {})} | custom-call | flops 1073741824 | bytes 7340032 | tf_op jit(solution)/shard_map/pallas_call | solution.py:136
  73.9 62.9 %all_to_all.11.spectra_ref = bf16[256,8,512]{2,1,0:T(8,128)(2,1)S(1)} all-to-all(bf16[256,8,512]{2,1,0:T(8,128)(2,1)S(1)} %shard_map.57), channel_id=1, replica_groups=mesh['zh'=4,'y'=4,'x'=4,'zl'=2,'core'=2] {'zh','y','x','zl','core'}, dimensions={0} | all-to-all | bytes 4194304 | tf_op jit(solution)/shard_map/all_to_all | solution.py:306
  136.9 5.6 %shard_map.58 = bf16[2,4,512,128]{3,2,1,0:T(8,128)(2,1)} custom-call(bf16[256,8,512]{2,1,0:T(8,128)(2,1)S(1)} %all_to_all.11.spectra_ref, bf16[4,2,512,1024]{3,2,1,0:T(8,128)(2,1)S(1)} %shard_map.55.weight), custom_call_target="tpu_custom_call" | custom-call | flops 2147483648 | bytes 11534336 | tf_op jit(solution)/shard_map/pallas_call | solution.py:276
Async XLA Ops:
  36.0 26.8 %collective-permute-start = (bf16[4,16,4096]{2,1,0:T(8,128)(2,1)}, bf16[4,16,4096]{2,1,0:T(8,128)(2,1)S(1)}, u32[]{:S(2)}, u32[]{:S(2)}) collective-permute-start(bf16[4,16,4096]{2,1,0:T(8,128)(2,1)} %get-tuple-element.10), channel_id=1, source_target_pairs={{0,64},{64,128},{128,192},{1,65},{65,129},{129,193},{2,66},{66,130... | collective-permute-start | bytes 1572872 | tf_op jit(solution)/shard_map/ppermute | solution.py:300
  40.9 27.6 %collective-permute-start.1 = (bf16[4,16,4096]{2,1,0:T(8,128)(2,1)}, bf16[4,16,4096]{2,1,0:T(8,128)(2,1)S(1)}, u32[]{:S(2)}, u32[]{:S(2)}) collective-permute-start(bf16[4,16,4096]{2,1,0:T(8,128)(2,1)} %get-tuple-element.9), channel_id=1, source_target_pairs={{0,192},{64,0},{128,64},{192,128},{1,193},{65,1},{129,65},{193,129... | collective-permute-start | bytes 1572872 | tf_op jit(solution)/shard_map/ppermute | solution.py:301
  43.4 1.6 %copy-start = (f32[512,1024]{1,0:T(8,128)S(1)}, f32[512,1024]{1,0:T(8,128)}, u32[]{:S(2)}) copy-start(f32[512,1024]{1,0:T(8,128)} %delays_ref.1) | copy-start | bytes 6291460
  45.0 1.6 %copy-start.1 = (bf16[1024,1024]{1,0:T(8,128)(2,1)S(1)}, bf16[1024,1024]{1,0:T(8,128)(2,1)}, u32[]{:S(2)}) copy-start(bf16[1024,1024]{1,0:T(8,128)(2,1)} %constant.38.clone.order_ref) | copy-start | bytes 6291460
  46.5 10.9 %copy-start.2 = (f32[16,2048]{1,0:T(8,128)S(1)}, f32[16,2048]{1,0:T(8,128)}, u32[]{:S(2)}) copy-start(f32[16,2048]{1,0:T(8,128)} %refs_4_.1) | copy-start | bytes 393220

commit v4 on v3

v4 whole, which is shorter than its diff:
```python
import math

import jax
import jax.numpy as jnp
import numpy as np
from jax import lax
from jax.experimental import pallas as pl
from jax.experimental.pallas import tpu as pltpu
from jax.sharding import Mesh
from jax.sharding import PartitionSpec as P

CHAN = 1024
FRAME = 2048
TAPS = 16
INPUTS = 1024
BEAMS = 512
FRAMES = 128

ZH, YX, INP, DEVICES = 4, 16, 4, 256
PLANE = FRAMES // ZH
LATE = 8
HALO = LATE // 2
PART = PLANE // 2
ROWS = INPUTS // INP // YX
OWN = CHAN // DEVICES
PLACES = YX * INP
LANES = 128
ALL = ("zh", "y", "x", "zl", "core")


def dft_tables():
    turn = np.arange(FRAME) * (2.0 * np.pi / FRAME)
    index = np.outer(np.arange(CHAN), np.arange(FRAME // 2)) % FRAME
    table = np.stack([np.cos(turn)[index], -np.sin(turn)[index]], axis=1)
    table = table.reshape(CHAN // 2, 2, 2, FRAME // 2).transpose(1, 0, 2, 3)
    return table.reshape(2, CHAN, FRAME // 2).astype(jnp.bfloat16)


def weighted(frame, taps, newest, delays):
    delays = list(delays)
    total = taps[delays[0]] * frame(newest - delays[0])
    for t in delays[1:]:
        total = total + taps[t] * frame(newest - t)
    return total


def resident(value):
    return pltpu.with_memory_space_constraint(value, pltpu.VMEM)


def transform(sums, tables, result, out_ref, lanes, out_sems, ready):
    steps = out_sems.shape[0]
    block = CHAN // steps
    upper = lax.broadcasted_iota(jnp.int32, (block // 8, 8, ROWS * PART), 1) < 4
    copies = []
    for step in range(steps):
        ready(step)
        cut = slice(step * block, (step + 1) * block)
        even, odd = (
            lax.dot_general(
                tables[k, cut], sums[k], (((1,), (1,)), ((), ())), preferred_element_type=jnp.float32
            ).reshape(block // 8, 8, ROWS * PART)
            * (1.0 / math.sqrt(FRAME))
            for k in range(2)
        )
        one = jnp.where(upper, even, pltpu.roll(odd, 4, 1)).astype(jnp.bfloat16)
        two = jnp.where(upper, pltpu.roll(even, 4, 1), odd).astype(jnp.bfloat16)
        for k in range(block // 8):
            result[step * block // 4 + 2 * k] = one[k]
            result[step * block // 4 + 2 * k + 1] = two[k]
        cut = pl.ds(step * block // 4, block // 4)
        copies.append(pltpu.make_async_copy(result.at[cut], out_ref.at[cut, :, lanes], out_sems.at[step]))
        copies[-1].start()
    for copy in copies:
        copy.wait()


def add_sums(sums, turned, step):
    lanes = pl.ds(pl.multiple_of(step * LANES, LANES), LANES)
    first, second = turned[0], turned[1]
    sums[0, :, lanes] = (first + second).astype(jnp.bfloat16)
    sums[1, :, lanes] = (first - second).astype(jnp.bfloat16)


def loader(ref, base):
    memo = {}

    def load(k):
        if k not in memo:
            memo[k] = ref[k // 2, :, pl.ds(base + (k % 2) * FRAME, LANES)].astype(jnp.float32)
        return memo[k]

    return load


def inner_kernel(keep_ref, own_ref, coeffs_ref, table_ref, out_ref, tables, partial_ref, *scratch):
    sums, turned, result, table_sems, out_sems = scratch
    steps = table_sems.shape[0]
    block = CHAN // steps

    def table_copy(step):
        cut = pl.ds(step * block, block)
        return pltpu.make_async_copy(table_ref.at[:, cut], tables.at[:, cut], table_sems.at[step])

    for step in range(steps):
        table_copy(step).start()

    def tile(step, carry):
        for side in range(2):
            base = pl.multiple_of(step * LANES, LANES) + side * (FRAME // 2)
            own = loader(own_ref, base)
            taps = [coeffs_ref[t : t + 1, pl.ds(base, LANES)] for t in range(TAPS)]
            for j in range(LATE):
                partial_ref[step, side, LATE + j] = weighted(own, taps, LATE + j, range(LATE + j + 1))
            for j in range(PART):
                turned[side, pl.ds(j, ROWS, stride=PART), :] = weighted(own, taps, PART + j, range(TAPS))
            for j in range(LATE):
                part = weighted(own, taps, PLANE + j, range(j + 1, TAPS))
                partial_ref[step, side, j] = part * keep_ref[0]
        add_sums(sums, turned, step)
        return carry

    lax.fori_loop(0, FRAME // 2 // LANES, tile, 0)
    lanes = pl.ds(0, ROWS * PART)
    transform(sums, tables, result, out_ref, lanes, out_sems, lambda step: table_copy(step).wait())


def outer_kernel(prev_ref, next_ref, coeffs_ref, tables, partial_ref, _, out_ref, *scratch):
    sums, turned, result, out_sems = scratch

    def tile(step, carry):
        for side in range(2):
            base = pl.multiple_of(step * LANES, LANES) + side * (FRAME // 2)
            prev, following = loader(prev_ref, base), loader(next_ref, base)
            taps = [coeffs_ref[t : t + 1, pl.ds(base, LANES)] for t in range(TAPS)]
            for j in range(LATE):
                total = partial_ref[step, side, j] + weighted(following, taps, j, range(j + 1))
                turned[side, pl.ds(j, ROWS, stride=PART), :] = total
                total = partial_ref[step, side, LATE + j]
                if LATE + j + 1 < TAPS:
                    total = total + weighted(prev, taps, 2 * LATE + j, range(LATE + j + 1, TAPS))
                turned[side, pl.ds(LATE + j, ROWS, stride=PART), :] = total
        add_sums(sums, turned, step)
        return carry

    lax.fori_loop(0, FRAME // 2 // LANES, tile, 0)
    lanes = pl.ds(ROWS * PART, ROWS * PART)
    transform(sums, tables, result, out_ref, lanes, out_sems, lambda step: None)


SPECTRA = jax.ShapeDtypeStruct((DEVICES, 2 * OWN, ROWS * PLANE), jnp.bfloat16)
STEPS = 4
SPECTRA_SCRATCH = [
    pltpu.VMEM((2, ROWS * PART, FRAME // 2), jnp.bfloat16),
    pltpu.VMEM((2, ROWS * PART, LANES), jnp.float32),
    pltpu.VMEM((DEVICES, 2 * OWN, ROWS * PART), jnp.bfloat16),
]
SEMS = pltpu.SemaphoreType.DMA((STEPS,))


def inner_spectra(keep, own, coeffs, table):
    smem, vmem, hbm = (pl.BlockSpec(memory_space=m) for m in (pltpu.SMEM, pltpu.VMEM, pl.ANY))
    partial = (FRAME // 2 // LANES, 2, PART, ROWS, LANES)
    return pl.pallas_call(
        inner_kernel,
        in_specs=[smem, vmem, vmem, hbm],
        out_specs=[hbm, vmem, vmem],
        out_shape=[SPECTRA, pltpu.VMEM(table.shape, table.dtype), pltpu.VMEM(partial, jnp.float32)],
        scratch_shapes=SPECTRA_SCRATCH + [SEMS, SEMS],
        compiler_params=pltpu.CompilerParams(vmem_limit_bytes=20 << 20),
        cost_estimate=pl.CostEstimate(
            flops=2 * CHAN * FRAME * ROWS * PART, bytes_accessed=7 << 20, transcendentals=0
        ),
    )(keep, own, coeffs, pltpu.with_memory_space_constraint(table, pltpu.HBM))


def outer_spectra(prev, following, coeffs, tables, partial, inner):
    vmem, hbm = (pl.BlockSpec(memory_space=m) for m in (pltpu.VMEM, pl.ANY))
    return pl.pallas_call(
        outer_kernel,
        in_specs=[vmem] * 5 + [hbm],
        out_specs=hbm,
        out_shape=SPECTRA,
        scratch_shapes=SPECTRA_SCRATCH + [SEMS],
        input_output_aliases={5: 0},
        compiler_params=pltpu.CompilerParams(vmem_limit_bytes=16 << 20),
        cost_estimate=pl.CostEstimate(
            flops=2 * CHAN * FRAME * ROWS * PART, bytes_accessed=7 << 20, transcendentals=0
        ),
    )(prev, following, coeffs, resident(tables), resident(partial), inner)


def fit(values):
    nodes = (np.cos(np.pi * (np.arange(64) + 0.5) / 64) + 1.0) / 8.0
    return [float(v) for v in np.polynomial.Polynomial.fit(nodes, values(np.sqrt(nodes)), 6, domain=[0, 0.25], window=[0, 0.25]).coef]


COS = fit(lambda r: np.cos(2 * np.pi * r))
SIN = fit(lambda r: np.sin(2 * np.pi * r) / r)


def cos_sin(turns):
    rest = turns - jnp.round(turns)
    square = rest * rest
    cos, sin = COS[-1], SIN[-1]
    for a, b in zip(COS[-2::-1], SIN[-2::-1]):
        cos = cos * square + a
        sin = sin * square + b
    return cos, sin * rest


def input_order():
    order = np.arange(INPUTS).reshape(INP, YX, ROWS).transpose(2, 1, 0).reshape(-1)
    return (np.arange(INPUTS)[:, None] == order).astype(jnp.bfloat16)


def weights_kernel(first_ref, delays_hbm, order_hbm, out_ref, delays, delays_ref, order_ref, sems):
    copies = [
        pltpu.make_async_copy(delays_hbm, delays_ref, sems.at[0]),
        pltpu.make_async_copy(order_hbm, order_ref, sems.at[1]),
    ]
    for copy in copies:
        copy.start()
    for copy in copies:
        copy.wait()
    block = 128

    def reorder(step, carry):
        at = pl.ds(pl.multiple_of(step * block, block), block)
        rest = delays_ref[at]
        total = jnp.zeros_like(rest)
        for _ in range(3):
            part = rest.astype(jnp.bfloat16)
            rest = rest - part.astype(jnp.float32)
            total = total + jnp.dot(part, order_ref[...], preferred_element_type=jnp.float32)
        delays[at] = total * (1.0 / FRAME)
        return carry

    lax.fori_loop(0, BEAMS // block, reorder, 0)
    block = 16

    def rows(step, carry):
        at = pl.ds(pl.multiple_of(step * block, block), block)
        delay = delays[at]
        step_cos, step_sin = cos_sin(delay)
        cos, sin = cos_sin(delay * first_ref[0])
        for c in range(OWN):
            if c:
                cos, sin = cos * step_cos - sin * step_sin, sin * step_cos + cos * step_sin
            out_ref[c, 0, at] = cos.astype(jnp.bfloat16)
            out_ref[c, 1, at] = (-sin).astype(jnp.bfloat16)
        return carry

    lax.fori_loop(0, BEAMS // block, rows, 0)


def weights(first, delays):
    vmem = pl.BlockSpec(memory_space=pltpu.VMEM)
    return pl.pallas_call(
        weights_kernel,
        in_specs=[pl.BlockSpec(memory_space=m) for m in (pltpu.SMEM, pl.ANY, pl.ANY)],
        out_specs=vmem,
        out_shape=pltpu.VMEM((OWN, 2, BEAMS, INPUTS), jnp.bfloat16),
        scratch_shapes=[
            pltpu.VMEM((BEAMS, INPUTS), jnp.float32),
            pltpu.VMEM((BEAMS, INPUTS), jnp.float32),
            pltpu.VMEM((INPUTS, INPUTS), jnp.bfloat16),
            pltpu.SemaphoreType.DMA((2,)),
        ],
        compiler_params=pltpu.CompilerParams(vmem_limit_bytes=20 << 20),
        cost_estimate=pl.CostEstimate(
            flops=60 * BEAMS * INPUTS, bytes_accessed=12 << 20, transcendentals=0
        ),
    )(
        first,
        pltpu.with_memory_space_constraint(delays, pltpu.HBM),
        pltpu.with_memory_space_constraint(jnp.asarray(input_order()), pltpu.HBM),
    )


def arrange(wide, own, values):
    lane = lax.broadcasted_iota(jnp.int32, (PLACES, LANES), 1)
    group = LANES // PART
    rows = 2 * OWN
    halves = ROWS // group
    for half in range(halves):
        for side in range(2):
            row = 4 * (own % 2) + 2 * (own // 2) + side
            a = [
                wide[half + (1 - inner) * halves, pl.ds(zh * PLACES * rows + row, PLACES, stride=rows), :]
                for zh in range(ZH)
                for inner in range(2)
            ]
            for bit in (4, 2, 1):
                keep = lax.rem(lane, 2 * bit * PART) < bit * PART
                for k in range(group):
                    if not k & bit:
                        x, y = a[k], a[k + bit]
                        a[k] = jnp.where(keep, x, pltpu.roll(y, bit * PART, 1))
                        a[k + bit] = jnp.where(keep, pltpu.roll(x, LANES - bit * PART, 1), y)
            for k in range(group):
                at = (half * group + k) * PLACES
                values[at : at + PLACES, side * LANES : (side + 1) * LANES] = a[k].astype(jnp.bfloat16)


def beams_kernel(spectra_ref, weight, out_ref, wide, values, result, sems):
    for tile in range(ROWS * PLANE // LANES):
        part = spectra_ref[:, :, tile * LANES : (tile + 1) * LANES]
        wide[tile] = part.astype(jnp.float32).reshape(DEVICES * 2 * OWN, LANES)
    lane = lax.broadcasted_iota(jnp.int32, (BEAMS, LANES), 1)
    taken_over = lax.rem(lane, PLANE) < LATE
    copies = []
    for channel in range(OWN):
        arrange(wide, channel, values.at[channel])
        here = values[channel]
        by_re = jnp.dot(weight[channel, 0], here, preferred_element_type=jnp.float32)
        by_im = jnp.dot(weight[channel, 1], here, preferred_element_type=jnp.float32)
        parts = (by_re[:, :LANES] - by_im[:, LANES:], by_re[:, LANES:] + by_im[:, :LANES])
        for side, part in enumerate(parts):
            part = jnp.where(taken_over, pltpu.roll(part, PLANE, 1), part) * (1.0 / math.sqrt(INPUTS))
            result[side, channel] = part.astype(jnp.bfloat16)
        copies.append(pltpu.make_async_copy(result.at[:, channel], out_ref.at[:, channel], sems.at[channel]))
        copies[-1].start()
    for copy in copies:
        copy.wait()


def beams(received, weight):
    vmem = pl.BlockSpec(memory_space=pltpu.VMEM)
    shape = (2, OWN, BEAMS, FRAMES)
    return pl.pallas_call(
        beams_kernel,
        in_specs=[vmem, vmem],
        out_specs=pl.BlockSpec(memory_space=pl.ANY),
        out_shape=jax.ShapeDtypeStruct(shape, jnp.bfloat16),
        scratch_shapes=[
            pltpu.VMEM((ROWS * PLANE // LANES, DEVICES * 2 * OWN, LANES), jnp.float32),
            pltpu.VMEM((OWN, INPUTS, 2 * LANES), jnp.bfloat16),
            pltpu.VMEM(shape, jnp.bfloat16),
            pltpu.SemaphoreType.DMA((OWN,)),
        ],
        compiler_params=pltpu.CompilerParams(vmem_limit_bytes=20 << 20),
        cost_estimate=pl.CostEstimate(
            flops=8 * OWN * BEAMS * INPUTS * FRAMES, bytes_accessed=11 << 20, transcendentals=0
        ),
    )(received, resident(weight))


def body(samples, coeffs, delays):
    first = (lax.axis_index(ALL) * OWN).astype(jnp.float32).reshape(1)
    keep = jnp.where(lax.axis_index("zh") == ZH - 1, 0.0, 1.0).astype(jnp.float32).reshape(1)
    table = jnp.asarray(dft_tables())
    up = [(i, i + 1) for i in range(ZH - 1)]
    down = [(i, (i - 1) % ZH) for i in range(ZH)]

    own = lax.all_to_all(samples.reshape(YX, ROWS, 2 * FRAME), ("y", "x"), 0, 0, tiled=True)
    prev = lax.ppermute(own[YX - HALO :], "zh", up)
    following = lax.ppermute(own[:HALO], "zh", down)
    weight = weights(first, delays)
    inner, tables, partial = inner_spectra(keep, own, coeffs, table)
    prev, weight = lax.optimization_barrier((prev, weight))
    blocks = outer_spectra(prev, following, coeffs, tables, partial, inner)
    received = lax.all_to_all(blocks, ALL, 0, 0, tiled=True)
    return beams(received, weight)


def solution(mesh):
    fine = Mesh(mesh.devices.reshape(4, 4, 4, 2, 2), ALL)
    in_specs = (P(("zl", "core"), ("zh", "y", "x")), P(), P())
    out_specs = P(None, ALL, None, None)
    return jax.shard_map(body, mesh=fine, in_specs=in_specs, out_specs=out_specs, check_vma=False)
```

time: 143 us -> 141 us (0.986)
  local copies, waits for them, and re-layouts: 4.21 us -> 1.04 us
    unnamed x6 -> x2, local copies, waits for them, and re-layouts: 3.18 us -> 0.01 us
  transfers between devices with their start and end apart: 2 -> 2, of which waited for: 1 -> 1; matrix products, arithmetic and copies ran while one was open for 0% -> 0% of each run, Pallas kernels for 11% -> 14%
where the time goes in v4:
time: 141 us; the launch traced here: 140 us
  blocking collectives  97.9 us (69%)
  Pallas kernels  28.3 us (20%)
  starting transfers between devices  7.38 us (5%)
  waiting for transfers between devices  5.7 us (4%)
    all_to_all x1, blocking collectives, body(): received = lax.all_to_all(blocks, ALL, 0, 0, tiled=True)  62.9 us
    all_to_all x1, blocking collectives, body(): lax.all_to_all(samples.reshape(YX, ROWS, 2 * FRAME), ('y', 'x'), 0, 0, ti...  34.9 us
    pallas_call x1, Pallas kernels, weights(): pl.pallas_call(weights_kernel, in_specs=[pl.BlockSpec(memory_space=m) for...  12.6 us
    pallas_call x1, Pallas kernels, inner_spectra(): pl.pallas_call(inner_kernel, in_specs=[smem, vmem, vmem, hbm], out_specs=...  6.75 us
    ppermute x1, waiting for transfers between devices, body(): following = lax.ppermute(own[:HALO], 'zh', down)  5.7 us
    pallas_call x1, Pallas kernels, beams(): pl.pallas_call(beams_kernel, in_specs=[vmem, vmem], out_specs=pl.BlockSpe...  5.67 us
    ppermute x1, starting transfers between devices, body(): prev = lax.ppermute(own[YX - HALO:], 'zh', up)  4.92 us
    pallas_call x1, Pallas kernels, outer_spectra(): pl.pallas_call(outer_kernel, in_specs=[vmem] * 5 + [hbm], out_specs=hbm,...  3.28 us
  transfers between devices with their start and end apart: 2, of which 1 were waited for; matrix products, arithmetic and copies ran while one was open for 0% of the time, Pallas kernels for 14%

profile of v4, /device:TPU:1, one launch (start us, length us, event | category | flops | bytes accessed | tf_op | source)
XLA Modules:
  0.0 140.4 jit_solution(4415061751131120267)
XLA Ops:
  0.0 34.9 %all_to_all.10.own_ref = bf16[16,16,4096]{2,1,0:T(8,128)(2,1)S(1)} all-to-all(bf16[16,16,4096]{2,1,0:T(8,128)(2,1)} %bitcast.3), channel_id=1, replica_groups=mesh['zh'=4,'y'=4,'x'=4,'zl'=2,'core'=2] {'y','x'}, dimensions={0} | all-to-all | bytes 4194304 | tf_op jit(solution)/shard_map/all_to_all | solution.py:356
  34.9 1.0 fusion
  36.0 4.9 %collective-permute-start = (bf16[4,16,4096]{2,1,0:T(8,128)(2,1)}, bf16[4,16,4096]{2,1,0:T(8,128)(2,1)S(1)}, u32[]{:S(2)}, u32[]{:S(2)}) collective-permute-start(bf16[4,16,4096]{2,1,0:T(8,128)(2,1)} %get-tuple-element.16), channel_id=1, source_target_pairs={{0,64},{64,128},{128,192},{1,65},{65,129},{129,193},{2,66},{66,130... | collective-permute-start | bytes 1572872 | tf_op jit(solution)/shard_map/ppermute | solution.py:357
  40.9 2.5 %collective-permute-start.1 = (bf16[4,16,4096]{2,1,0:T(8,128)(2,1)}, bf16[4,16,4096]{2,1,0:T(8,128)(2,1)S(1)}, u32[]{:S(2)}, u32[]{:S(2)}) collective-permute-start(bf16[4,16,4096]{2,1,0:T(8,128)(2,1)} %get-tuple-element.15), channel_id=1, source_target_pairs={{0,192},{64,0},{128,64},{192,128},{1,193},{65,1},{129,65},{193,129... | collective-permute-start | bytes 1572872 | tf_op jit(solution)/shard_map/ppermute | solution.py:358
  43.4 0.0 copy-start
  43.4 12.6 %shard_map.55.weight = bf16[4,2,512,1024]{3,2,1,0:T(8,128)(2,1)S(1)} custom-call(f32[1]{0:T(128)} %bitcast.1.first_ref, f32[512,1024]{1,0:T(8,128)} %delays_hbm.1, bf16[1024,1024]{1,0:T(8,128)(2,1)} %constant.38.clone.order_hbm), custom_call_target="tpu_custom_call" | custom-call | flops 31457280 | bytes 12582912 | tf_op jit(solution)/shard_map/pallas_call | solution.py:259
  56.0 0.0 copy-done
  56.0 6.7 %shard_map.56 = (bf16[256,8,512]{2,1,0:T(8,128)(2,1)S(1)}, bf16[2,1024,1024]{2,1,0:T(8,128)(2,1)S(1)}, f32[8,2,16,16,128]{4,3,2,1,0:T(8,128)S(1)}) custom-call(f32[1]{0:T(128)} %bitcast.2.keep_ref, bf16[16,16,4096]{2,1,0:T(8,128)(2,1)S(1)} %all_to_all.10.own_ref, f32[16,2048]{1,0:T(8,128)S(1)} %copy-done, bf16[2,1024,1024]{2,1,0:T(8,128)(2,1)} %constant.37.clone.table_ref), custom_call_target="tpu_custom_call" | custom-call | flops 1073741824 | bytes 7340032 | tf_op jit(solution)/shard_map/pallas_call | solution.py:164
  62.8 0.0 collective-permute-done.prev_ref
  62.8 5.7 %collective-permute-done.1.next_ref = bf16[4,16,4096]{2,1,0:T(8,128)(2,1)S(1)} collective-permute-done((bf16[4,16,4096]{2,1,0:T(8,128)(2,1)}, bf16[4,16,4096]{2,1,0:T(8,128)(2,1)S(1)}, u32[]{:S(2)}, u32[]{:S(2)}) %collective-permute-start.1) | collective-permute-done | bytes 524320 | tf_op jit(solution)/shard_map/ppermute | solution.py:358
  68.5 3.3 %shard_map.57 = bf16[256,8,512]{2,1,0:T(8,128)(2,1)S(1)} custom-call(bf16[4,16,4096]{2,1,0:T(8,128)(2,1)S(1)} %collective-permute-done.prev_ref, bf16[4,16,4096]{2,1,0:T(8,128)(2,1)S(1)} %collective-permute-done.1.next_ref, f32[16,2048]{1,0:T(8,128)S(1)} %copy-done, ...), custom_call_target="tpu_custom_call", output_to_operand_aliasing={{}: (5, {})} | custom-call | flops 1073741824 | bytes 7340032 | tf_op jit(solution)/shard_map/pallas_call | solution.py:179
  71.8 62.9 %all_to_all.11.spectra_ref = bf16[256,8,512]{2,1,0:T(8,128)(2,1)S(1)} all-to-all(bf16[256,8,512]{2,1,0:T(8,128)(2,1)S(1)} %shard_map.57), channel_id=1, replica_groups=mesh['zh'=4,'y'=4,'x'=4,'zl'=2,'core'=2] {'zh','y','x','zl','core'}, dimensions={0} | all-to-all | bytes 4194304 | tf_op jit(solution)/shard_map/all_to_all | solution.py:363
  134.7 5.7 %shard_map.58 = bf16[2,4,512,128]{3,2,1,0:T(8,128)(2,1)} custom-call(bf16[256,8,512]{2,1,0:T(8,128)(2,1)S(1)} %all_to_all.11.spectra_ref, bf16[4,2,512,1024]{3,2,1,0:T(8,128)(2,1)S(1)} %shard_map.55.weight), custom_call_target="tpu_custom_call" | custom-call | flops 2147483648 | bytes 11534336 | tf_op jit(solution)/shard_map/pallas_call | solution.py:331
Async XLA Ops:
  36.0 26.8 %collective-permute-start = (bf16[4,16,4096]{2,1,0:T(8,128)(2,1)}, bf16[4,16,4096]{2,1,0:T(8,128)(2,1)S(1)}, u32[]{:S(2)}, u32[]{:S(2)}) collective-permute-start(bf16[4,16,4096]{2,1,0:T(8,128)(2,1)} %get-tuple-element.16), channel_id=1, source_target_pairs={{0,64},{64,128},{128,192},{1,65},{65,129},{129,193},{2,66},{66,130... | collective-permute-start | bytes 1572872 | tf_op jit(solution)/shard_map/ppermute | solution.py:357
  40.9 27.6 %collective-permute-start.1 = (bf16[4,16,4096]{2,1,0:T(8,128)(2,1)}, bf16[4,16,4096]{2,1,0:T(8,128)(2,1)S(1)}, u32[]{:S(2)}, u32[]{:S(2)}) collective-permute-start(bf16[4,16,4096]{2,1,0:T(8,128)(2,1)} %get-tuple-element.15), channel_id=1, source_target_pairs={{0,192},{64,0},{128,64},{192,128},{1,193},{65,1},{129,65},{193,129... | collective-permute-start | bytes 1572872 | tf_op jit(solution)/shard_map/ppermute | solution.py:358
  43.4 12.6 %copy-start = (f32[16,2048]{1,0:T(8,128)S(1)}, f32[16,2048]{1,0:T(8,128)}, u32[]{:S(2)}) copy-start(f32[16,2048]{1,0:T(8,128)} %coeffs_ref.3) | copy-start | bytes 393220

commit v5 on v4

--- a/solution.py
+++ b/solution.py
@@ -25,6 +25,7 @@
 OWN = CHAN // DEVICES
 PLACES = YX * INP
 LANES = 128
+GROUP = LANES // PART
 ALL = ("zh", "y", "x", "zl", "core")
 
 
@@ -75,11 +76,14 @@
         copy.wait()
 
 
-def add_sums(sums, turned, step):
+def add_sums(sums, turned, step, shift):
     lanes = pl.ds(pl.multiple_of(step * LANES, LANES), LANES)
-    first, second = turned[0], turned[1]
-    sums[0, :, lanes] = (first + second).astype(jnp.bfloat16)
-    sums[1, :, lanes] = (first - second).astype(jnp.bfloat16)
+    for k in range(ROWS):
+        first, second = (turned[side, k * PART : (k + 1) * PART] for side in range(2))
+        to = k // GROUP * GROUP + lax.rem(k % GROUP + shift, GROUP)
+        to = pl.ds(pl.multiple_of(to * PART, PART), PART)
+        sums[0, to, lanes] = (first + second).astype(jnp.bfloat16)
+        sums[1, to, lanes] = (first - second).astype(jnp.bfloat16)
 
 
 def loader(ref, base):
@@ -93,10 +97,11 @@
     return load
 
 
-def inner_kernel(keep_ref, own_ref, coeffs_ref, table_ref, out_ref, tables, partial_ref, *scratch):
+def inner_kernel(zh_ref, own_ref, coeffs_ref, table_ref, out_ref, tables, partial_ref, *scratch):
     sums, turned, result, table_sems, out_sems = scratch
     steps = table_sems.shape[0]
     block = CHAN // steps
+    keep = jnp.where(zh_ref[0] == ZH - 1, 0.0, 1.0)
 
     def table_copy(step):
         cut = pl.ds(step * block, block)
@@ -116,8 +121,8 @@
                 turned[side, pl.ds(j, ROWS, stride=PART), :] = weighted(own, taps, PART + j, range(TAPS))
             for j in range(LATE):
                 part = weighted(own, taps, PLANE + j, range(j + 1, TAPS))
-                partial_ref[step, side, j] = part * keep_ref[0]
-        add_sums(sums, turned, step)
+                partial_ref[step, side, j] = part * keep
+        add_sums(sums, turned, step, 2 * zh_ref[0] + 1)
         return carry
 
     lax.fori_loop(0, FRAME // 2 // LANES, tile, 0)
@@ -125,7 +130,7 @@
     transform(sums, tables, result, out_ref, lanes, out_sems, lambda step: table_copy(step).wait())
 
 
-def outer_kernel(prev_ref, next_ref, coeffs_ref, tables, partial_ref, _, out_ref, *scratch):
+def outer_kernel(zh_ref, prev_ref, next_ref, coeffs_ref, tables, partial_ref, _, out_ref, *scratch):
     sums, turned, result, out_sems = scratch
 
     def tile(step, carry):
@@ -140,7 +145,7 @@
                 if LATE + j + 1 < TAPS:
                     total = total + weighted(prev, taps, 2 * LATE + j, range(LATE + j + 1, TAPS))
                 turned[side, pl.ds(LATE + j, ROWS, stride=PART), :] = total
-        add_sums(sums, turned, step)
+        add_sums(sums, turned, step, 2 * zh_ref[0])
         return carry
 
     lax.fori_loop(0, FRAME // 2 // LANES, tile, 0)
@@ -158,7 +163,7 @@
 SEMS = pltpu.SemaphoreType.DMA((STEPS,))
 
 
-def inner_spectra(keep, own, coeffs, table):
+def inner_spectra(zh, own, coeffs, table):
     smem, vmem, hbm = (pl.BlockSpec(memory_space=m) for m in (pltpu.SMEM, pltpu.VMEM, pl.ANY))
     partial = (FRAME // 2 // LANES, 2, PART, ROWS, LANES)
     return pl.pallas_call(
@@ -171,23 +176,23 @@
         cost_estimate=pl.CostEstimate(
             flops=2 * CHAN * FRAME * ROWS * PART, bytes_accessed=7 << 20, transcendentals=0
         ),
-    )(keep, own, coeffs, pltpu.with_memory_space_constraint(table, pltpu.HBM))
-
-
-def outer_spectra(prev, following, coeffs, tables, partial, inner):
-    vmem, hbm = (pl.BlockSpec(memory_space=m) for m in (pltpu.VMEM, pl.ANY))
+    )(zh, own, coeffs, pltpu.with_memory_space_constraint(table, pltpu.HBM))
+
+
+def outer_spectra(zh, prev, following, coeffs, tables, partial, inner):
+    smem, vmem, hbm = (pl.BlockSpec(memory_space=m) for m in (pltpu.SMEM, pltpu.VMEM, pl.ANY))
     return pl.pallas_call(
         outer_kernel,
-        in_specs=[vmem] * 5 + [hbm],
+        in_specs=[smem] + [vmem] * 5 + [hbm],
         out_specs=hbm,
         out_shape=SPECTRA,
         scratch_shapes=SPECTRA_SCRATCH + [SEMS],
-        input_output_aliases={5: 0},
+        input_output_aliases={6: 0},
         compiler_params=pltpu.CompilerParams(vmem_limit_bytes=16 << 20),
         cost_estimate=pl.CostEstimate(
             flops=2 * CHAN * FRAME * ROWS * PART, bytes_accessed=7 << 20, transcendentals=0
         ),
-    )(prev, following, coeffs, resident(tables), resident(partial), inner)
+    )(zh, prev, following, coeffs, resident(tables), resident(partial), inner)
 
 
 def fit(values):
@@ -279,28 +284,27 @@
 
 
 def arrange(wide, own, values):
-    lane = lax.broadcasted_iota(jnp.int32, (PLACES, LANES), 1)
-    group = LANES // PART
+    place = lax.broadcasted_iota(jnp.int32, (PLACES, LANES), 1) // PART
     rows = 2 * OWN
-    halves = ROWS // group
+    halves = ROWS // GROUP
     for half in range(halves):
         for side in range(2):
             row = 4 * (own % 2) + 2 * (own // 2) + side
             a = [
-                wide[half + (1 - inner) * halves, pl.ds(zh * PLACES * rows + row, PLACES, stride=rows), :]
+                wide[half + (1 - inner) * halves, pl.ds(zh * PLACES * rows + row, PLACES, stride=rows), :].astype(
+                    jnp.bfloat16
+                )
                 for zh in range(ZH)
                 for inner in range(2)
             ]
-            for bit in (4, 2, 1):
-                keep = lax.rem(lane, 2 * bit * PART) < bit * PART
-                for k in range(group):
-                    if not k & bit:
-                        x, y = a[k], a[k + bit]
-                        a[k] = jnp.where(keep, x, pltpu.roll(y, bit * PART, 1))
-                        a[k + bit] = jnp.where(keep, pltpu.roll(x, LANES - bit * PART, 1), y)
-            for k in range(group):
-                at = (half * group + k) * PLACES
-                values[at : at + PLACES, side * LANES : (side + 1) * LANES] = a[k].astype(jnp.bfloat16)
+            for bit in (1, 2, 4):
+                moved = place & bit != 0
+                a = [jnp.where(moved, a[(k + bit) % GROUP], a[k]) for k in range(GROUP)]
+            for k in range(GROUP):
+                at = (half * GROUP + k) * PLACES
+                value = a[-k % GROUP]
+                value = pltpu.roll(value, LANES - k * PART, 1) if k else value
+                values[at : at + PLACES, side * LANES : (side + 1) * LANES] = value
 
 
 def beams_kernel(spectra_ref, weight, out_ref, wide, values, result, sems):
@@ -348,7 +352,7 @@
 
 def body(samples, coeffs, delays):
     first = (lax.axis_index(ALL) * OWN).astype(jnp.float32).reshape(1)
-    keep = jnp.where(lax.axis_index("zh") == ZH - 1, 0.0, 1.0).astype(jnp.float32).reshape(1)
+    zh = lax.axis_index("zh").astype(jnp.int32).reshape(1)
     table = jnp.asarray(dft_tables())
     up = [(i, i + 1) for i in range(ZH - 1)]
     down = [(i, (i - 1) % ZH) for i in range(ZH)]
@@ -357,9 +361,9 @@
     prev = lax.ppermute(own[YX - HALO :], "zh", up)
     following = lax.ppermute(own[:HALO], "zh", down)
     weight = weights(first, delays)
-    inner, tables, partial = inner_spectra(keep, own, coeffs, table)
+    inner, tables, partial = inner_spectra(zh, own, coeffs, table)
     prev, weight = lax.optimization_barrier((prev, weight))
-    blocks = outer_spectra(prev, following, coeffs, tables, partial, inner)
+    blocks = outer_spectra(zh, prev, following, coeffs, tables, partial, inner)
     received = lax.all_to_all(blocks, ALL, 0, 0, tiled=True)
     return beams(received, weight)
 

time: 141 us -> 139 us (0.986)
  no operation moved by 1% of the time
where the time goes in v5:
time: 139 us
  blocking collectives  97.9 us (70%)
  Pallas kernels  26.9 us (19%)
  starting transfers between devices  7.38 us (5%)
  waiting for transfers between devices  5.73 us (4%)
    all_to_all x1, blocking collectives, body(): received = lax.all_to_all(blocks, ALL, 0, 0, tiled=True)  62.9 us
    all_to_all x1, blocking collectives, body(): lax.all_to_all(samples.reshape(YX, ROWS, 2 * FRAME), ('y', 'x'), 0, 0, ti...  34.9 us
    pallas_call x1, Pallas kernels, weights(): pl.pallas_call(weights_kernel, in_specs=[pl.BlockSpec(memory_space=m) for...  12.6 us
    pallas_call x1, Pallas kernels, inner_spectra(): pl.pallas_call(inner_kernel, in_specs=[smem, vmem, vmem, hbm], out_specs=...  6.72 us
    ppermute x1, waiting for transfers between devices, body(): following = lax.ppermute(own[:HALO], 'zh', down)  5.73 us
    ppermute x1, starting transfers between devices, body(): prev = lax.ppermute(own[YX - HALO:], 'zh', up)  4.92 us
    pallas_call x1, Pallas kernels, beams(): pl.pallas_call(beams_kernel, in_specs=[vmem, vmem], out_specs=pl.BlockSpe...  4.33 us
    pallas_call x1, Pallas kernels, outer_spectra(): pl.pallas_call(outer_kernel, in_specs=[smem] + [vmem] * 5 + [hbm], out_sp...  3.28 us
  transfers between devices with their start and end apart: 2, of which 1 were waited for; matrix products, arithmetic and copies ran while one was open for 0% of the time, Pallas kernels for 14%

profile of v5, /device:TPU:1, one launch (start us, length us, event | category | flops | bytes accessed | tf_op | source)
XLA Modules:
  0.0 139.0 jit_solution(13015690713320765870)
XLA Ops:
  0.0 34.9 %all_to_all.10.own_ref = bf16[16,16,4096]{2,1,0:T(8,128)(2,1)S(1)} all-to-all(bf16[16,16,4096]{2,1,0:T(8,128)(2,1)} %bitcast.3), channel_id=1, replica_groups=mesh['zh'=4,'y'=4,'x'=4,'zl'=2,'core'=2] {'y','x'}, dimensions={0} | all-to-all | bytes 4194304 | tf_op jit(solution)/shard_map/all_to_all | solution.py:360
  34.9 1.0 fusion
  36.0 4.9 %collective-permute-start = (bf16[4,16,4096]{2,1,0:T(8,128)(2,1)}, bf16[4,16,4096]{2,1,0:T(8,128)(2,1)S(1)}, u32[]{:S(2)}, u32[]{:S(2)}) collective-permute-start(bf16[4,16,4096]{2,1,0:T(8,128)(2,1)} %get-tuple-element.16), channel_id=1, source_target_pairs={{0,64},{64,128},{128,192},{1,65},{65,129},{129,193},{2,66},{66,130... | collective-permute-start | bytes 1572872 | tf_op jit(solution)/shard_map/ppermute | solution.py:361
  40.9 2.5 %collective-permute-start.1 = (bf16[4,16,4096]{2,1,0:T(8,128)(2,1)}, bf16[4,16,4096]{2,1,0:T(8,128)(2,1)S(1)}, u32[]{:S(2)}, u32[]{:S(2)}) collective-permute-start(bf16[4,16,4096]{2,1,0:T(8,128)(2,1)} %get-tuple-element.15), channel_id=1, source_target_pairs={{0,192},{64,0},{128,64},{192,128},{1,193},{65,1},{129,65},{193,129... | collective-permute-start | bytes 1572872 | tf_op jit(solution)/shard_map/ppermute | solution.py:362
  43.4 0.0 copy-start
  43.4 12.6 %shard_map.55.weight = bf16[4,2,512,1024]{3,2,1,0:T(8,128)(2,1)S(1)} custom-call(f32[1]{0:T(128)} %bitcast.2.first_ref, f32[512,1024]{1,0:T(8,128)} %delays_hbm.1, bf16[1024,1024]{1,0:T(8,128)(2,1)} %constant.32.clone.order_hbm), custom_call_target="tpu_custom_call" | custom-call | flops 31457280 | bytes 12582912 | tf_op jit(solution)/shard_map/pallas_call | solution.py:264
  56.0 0.0 copy-done
  56.0 6.7 %shard_map.56 = (bf16[256,8,512]{2,1,0:T(8,128)(2,1)S(1)}, bf16[2,1024,1024]{2,1,0:T(8,128)(2,1)S(1)}, f32[8,2,16,16,128]{4,3,2,1,0:T(8,128)S(1)}) custom-call(s32[1]{0:T(128)} %bitcast.zh_ref, bf16[16,16,4096]{2,1,0:T(8,128)(2,1)S(1)} %all_to_all.10.own_ref, f32[16,2048]{1,0:T(8,128)S(1)} %copy-done, bf16[2,1024,1024]{2,1,0:T(8,128)(2,1)} %constant.31.clone.table_ref), custom_call_target="tpu_custom_call" | custom-call | flops 1073741824 | bytes 7340032 | tf_op jit(solution)/shard_map/pallas_call | solution.py:169
  62.7 0.0 collective-permute-done.prev_ref
  62.7 5.7 %collective-permute-done.1.next_ref = bf16[4,16,4096]{2,1,0:T(8,128)(2,1)S(1)} collective-permute-done((bf16[4,16,4096]{2,1,0:T(8,128)(2,1)}, bf16[4,16,4096]{2,1,0:T(8,128)(2,1)S(1)}, u32[]{:S(2)}, u32[]{:S(2)}) %collective-permute-start.1) | collective-permute-done | bytes 524320 | tf_op jit(solution)/shard_map/ppermute | solution.py:362
  68.5 3.3 %shard_map.57 = bf16[256,8,512]{2,1,0:T(8,128)(2,1)S(1)} custom-call(s32[1]{0:T(128)} %bitcast.zh_ref, bf16[4,16,4096]{2,1,0:T(8,128)(2,1)S(1)} %collective-permute-done.prev_ref, bf16[4,16,4096]{2,1,0:T(8,128)(2,1)S(1)} %collective-permute-done.1.next_ref, f32[16,2048]{1,0:T(8,128)S(1)} %copy-done, ...), custom_call_target="tpu_custom_call", output_to_operand_aliasing={{}: (6, {})} | custom-call | flops 1073741824 | bytes 7340032 | tf_op jit(solution)/shard_map/pallas_call | solution.py:184
  71.8 62.9 %all_to_all.11.spectra_ref = bf16[256,8,512]{2,1,0:T(8,128)(2,1)S(1)} all-to-all(bf16[256,8,512]{2,1,0:T(8,128)(2,1)S(1)} %shard_map.57), channel_id=1, replica_groups=mesh['zh'=4,'y'=4,'x'=4,'zl'=2,'core'=2] {'zh','y','x','zl','core'}, dimensions={0} | all-to-all | bytes 4194304 | tf_op jit(solution)/shard_map/all_to_all | solution.py:367
  134.7 4.3 %shard_map.58 = bf16[2,4,512,128]{3,2,1,0:T(8,128)(2,1)} custom-call(bf16[256,8,512]{2,1,0:T(8,128)(2,1)S(1)} %all_to_all.11.spectra_ref, bf16[4,2,512,1024]{3,2,1,0:T(8,128)(2,1)S(1)} %shard_map.55.weight), custom_call_target="tpu_custom_call" | custom-call | flops 2147483648 | bytes 11534336 | tf_op jit(solution)/shard_map/pallas_call | solution.py:335
Async XLA Ops:
  36.0 26.7 %collective-permute-start = (bf16[4,16,4096]{2,1,0:T(8,128)(2,1)}, bf16[4,16,4096]{2,1,0:T(8,128)(2,1)S(1)}, u32[]{:S(2)}, u32[]{:S(2)}) collective-permute-start(bf16[4,16,4096]{2,1,0:T(8,128)(2,1)} %get-tuple-element.16), channel_id=1, source_target_pairs={{0,64},{64,128},{128,192},{1,65},{65,129},{129,193},{2,66},{66,130... | collective-permute-start | bytes 1572872 | tf_op jit(solution)/shard_map/ppermute | solution.py:361
  40.9 27.6 %collective-permute-start.1 = (bf16[4,16,4096]{2,1,0:T(8,128)(2,1)}, bf16[4,16,4096]{2,1,0:T(8,128)(2,1)S(1)}, u32[]{:S(2)}, u32[]{:S(2)}) collective-permute-start(bf16[4,16,4096]{2,1,0:T(8,128)(2,1)} %get-tuple-element.15), channel_id=1, source_target_pairs={{0,192},{64,0},{128,64},{192,128},{1,193},{65,1},{129,65},{193,129... | collective-permute-start | bytes 1572872 | tf_op jit(solution)/shard_map/ppermute | solution.py:362
  43.4 12.6 %copy-start = (f32[16,2048]{1,0:T(8,128)S(1)}, f32[16,2048]{1,0:T(8,128)}, u32[]{:S(2)}) copy-start(f32[16,2048]{1,0:T(8,128)} %coeffs_ref.3) | copy-start | bytes 393220

commit v6 on v5

--- a/solution.py
+++ b/solution.py
@@ -27,13 +27,14 @@
 LANES = 128
 GROUP = LANES // PART
 ALL = ("zh", "y", "x", "zl", "core")
+OWNERS = ("zh", "zl", "core", "y", "x")
 
 
 def dft_tables():
     turn = np.arange(FRAME) * (2.0 * np.pi / FRAME)
     index = np.outer(np.arange(CHAN), np.arange(FRAME // 2)) % FRAME
     table = np.stack([np.cos(turn)[index], -np.sin(turn)[index]], axis=1)
-    table = table.reshape(CHAN // 2, 2, 2, FRAME // 2).transpose(1, 0, 2, 3)
+    table = table.reshape(ZH, YX, INP, OWN // 2, 2, 2, FRAME // 2).transpose(4, 0, 2, 1, 3, 5, 6)
     return table.reshape(2, CHAN, FRAME // 2).astype(jnp.bfloat16)
 
 
@@ -97,6 +98,17 @@
     return load
 
 
+def frame_loader(ref, base):
+    memo = {}
+
+    def load(k):
+        if k not in memo:
+            memo[k] = ref[k, :, pl.ds(base, LANES)].astype(jnp.float32)
+        return memo[k]
+
+    return load
+
+
 def inner_kernel(zh_ref, own_ref, coeffs_ref, table_ref, out_ref, tables, partial_ref, *scratch):
     sums, turned, result, table_sems, out_sems = scratch
     steps = table_sems.shape[0]
@@ -130,20 +142,20 @@
     transform(sums, tables, result, out_ref, lanes, out_sems, lambda step: table_copy(step).wait())
 
 
-def outer_kernel(zh_ref, prev_ref, next_ref, coeffs_ref, tables, partial_ref, _, out_ref, *scratch):
+def outer_kernel(zh_ref, next_ref, prev_ref, coeffs_ref, tables, partial_ref, _, out_ref, *scratch):
     sums, turned, result, out_sems = scratch
 
     def tile(step, carry):
         for side in range(2):
             base = pl.multiple_of(step * LANES, LANES) + side * (FRAME // 2)
-            prev, following = loader(prev_ref, base), loader(next_ref, base)
+            prev, following = frame_loader(prev_ref, base), loader(next_ref, base)
             taps = [coeffs_ref[t : t + 1, pl.ds(base, LANES)] for t in range(TAPS)]
             for j in range(LATE):
                 total = partial_ref[step, side, j] + weighted(following, taps, j, range(j + 1))
                 turned[side, pl.ds(j, ROWS, stride=PART), :] = total
                 total = partial_ref[step, side, LATE + j]
                 if LATE + j + 1 < TAPS:
-                    total = total + weighted(prev, taps, 2 * LATE + j, range(LATE + j + 1, TAPS))
+                    total = total + weighted(prev, taps, 2 * LATE - 1 + j, range(LATE + j + 1, TAPS))
                 turned[side, pl.ds(LATE + j, ROWS, stride=PART), :] = total
         add_sums(sums, turned, step, 2 * zh_ref[0])
         return carry
@@ -192,12 +204,12 @@
         cost_estimate=pl.CostEstimate(
             flops=2 * CHAN * FRAME * ROWS * PART, bytes_accessed=7 << 20, transcendentals=0
         ),
-    )(zh, prev, following, coeffs, resident(tables), resident(partial), inner)
+    )(zh, following, prev, coeffs, resident(tables), resident(partial), inner)
 
 
 def fit(values):
     nodes = (np.cos(np.pi * (np.arange(64) + 0.5) / 64) + 1.0) / 8.0
-    return [float(v) for v in np.polynomial.Polynomial.fit(nodes, values(np.sqrt(nodes)), 6, domain=[0, 0.25], window=[0, 0.25]).coef]
+    return [float(v) for v in np.polynomial.Polynomial.fit(nodes, values(np.sqrt(nodes)), 5, domain=[0, 0.25], window=[0, 0.25]).coef]
 
 
 COS = fit(lambda r: np.cos(2 * np.pi * r))
@@ -215,8 +227,8 @@
 
 
 def input_order():
-    order = np.arange(INPUTS).reshape(INP, YX, ROWS).transpose(2, 1, 0).reshape(-1)
-    return (np.arange(INPUTS)[:, None] == order).astype(jnp.bfloat16)
+    order = np.arange(YX * ROWS).reshape(YX, ROWS).transpose(1, 0).reshape(-1)
+    return (np.arange(YX * ROWS)[:, None] == order).astype(jnp.bfloat16)
 
 
 def weights_kernel(first_ref, delays_hbm, order_hbm, out_ref, delays, delays_ref, order_ref, sems):
@@ -229,16 +241,19 @@
     for copy in copies:
         copy.wait()
     block = 128
+    size = YX * ROWS
 
     def reorder(step, carry):
         at = pl.ds(pl.multiple_of(step * block, block), block)
-        rest = delays_ref[at]
-        total = jnp.zeros_like(rest)
-        for _ in range(3):
-            part = rest.astype(jnp.bfloat16)
-            rest = rest - part.astype(jnp.float32)
-            total = total + jnp.dot(part, order_ref[...], preferred_element_type=jnp.float32)
-        delays[at] = total * (1.0 / FRAME)
+        for group in range(INP):
+            cut = slice(group * size, (group + 1) * size)
+            rest = delays_ref[at, cut]
+            total = jnp.zeros_like(rest)
+            for _ in range(3):
+                part = rest.astype(jnp.bfloat16)
+                rest = rest - part.astype(jnp.float32)
+                total = total + jnp.dot(part, order_ref[...], preferred_element_type=jnp.float32)
+            delays[at, cut] = total * (1.0 / FRAME)
         return carry
 
     lax.fori_loop(0, BEAMS // block, reorder, 0)
@@ -269,7 +284,7 @@
         scratch_shapes=[
             pltpu.VMEM((BEAMS, INPUTS), jnp.float32),
             pltpu.VMEM((BEAMS, INPUTS), jnp.float32),
-            pltpu.VMEM((INPUTS, INPUTS), jnp.bfloat16),
+            pltpu.VMEM((YX * ROWS, YX * ROWS), jnp.bfloat16),
             pltpu.SemaphoreType.DMA((2,)),
         ],
         compiler_params=pltpu.CompilerParams(vmem_limit_bytes=20 << 20),
@@ -301,10 +316,12 @@
                 moved = place & bit != 0
                 a = [jnp.where(moved, a[(k + bit) % GROUP], a[k]) for k in range(GROUP)]
             for k in range(GROUP):
-                at = (half * GROUP + k) * PLACES
                 value = a[-k % GROUP]
                 value = pltpu.roll(value, LANES - k * PART, 1) if k else value
-                values[at : at + PLACES, side * LANES : (side + 1) * LANES] = value
+                for group in range(INP):
+                    at = (group * ROWS + half * GROUP + k) * YX
+                    cut = slice(side * LANES, (side + 1) * LANES)
+                    values[at : at + YX, cut] = value[group * YX : (group + 1) * YX]
 
 
 def beams_kernel(spectra_ref, weight, out_ref, wide, values, result, sems):
@@ -358,13 +375,15 @@
     down = [(i, (i - 1) % ZH) for i in range(ZH)]
 
     own = lax.all_to_all(samples.reshape(YX, ROWS, 2 * FRAME), ("y", "x"), 0, 0, tiled=True)
-    prev = lax.ppermute(own[YX - HALO :], "zh", up)
     following = lax.ppermute(own[:HALO], "zh", down)
+    last = own[YX - HALO :].reshape(HALO, ROWS, 2, FRAME)
+    last = jnp.concatenate([last[:1, :, 1], last[1:].transpose(0, 2, 1, 3).reshape(LATE - 2, ROWS, FRAME)])
+    prev = lax.ppermute(last, "zh", up)
     weight = weights(first, delays)
     inner, tables, partial = inner_spectra(zh, own, coeffs, table)
-    prev, weight = lax.optimization_barrier((prev, weight))
+    following, weight = lax.optimization_barrier((following, weight))
     blocks = outer_spectra(zh, prev, following, coeffs, tables, partial, inner)
-    received = lax.all_to_all(blocks, ALL, 0, 0, tiled=True)
+    received = lax.all_to_all(blocks, OWNERS, 0, 0, tiled=True)
     return beams(received, weight)
 
 

time: 139 us -> 134 us (0.964)
  Pallas kernels: 26.9 us -> 23.3 us
  waiting for transfers between devices: 5.73 us -> 2.43 us
    ppermute x1, starting transfers between devices: 2.46 us -> 6.1 us  [body(): following = lax.ppermute(own[:HALO], 'zh', down)]
    ppermute x1, starting transfers between devices: 4.92 us -> 1.32 us  [body(): prev = lax.ppermute(last, 'zh', up)]
    pallas_call x1, Pallas kernels: 12.6 us -> 9.06 us  [weights(): pl.pallas_call(weights_kernel, in_specs=[pl.BlockSpec(memory_space=m) for...]
    ppermute x1, waiting for transfers between devices: 5.73 us -> 2.43 us  [body(): following = lax.ppermute(own[:HALO], 'zh', down)]
  transfers between devices with their start and end apart: 2 -> 2, of which waited for: 1 -> 1; matrix products, arithmetic and copies ran while one was open for 0% -> 0% of each run, Pallas kernels for 14% -> 12%
where the time goes in v6:
time: 134 us
  blocking collectives  99 us (74%)
  Pallas kernels  23.3 us (17%)
  starting transfers between devices  7.42 us (6%)
  waiting for transfers between devices  2.43 us (2%)
  local copies, waits for them, and re-layouts  1.48 us (1%)
    all_to_all x1, blocking collectives, body(): received = lax.all_to_all(blocks, OWNERS, 0, 0, tiled=True)  64.1 us
    all_to_all x1, blocking collectives, body(): lax.all_to_all(samples.reshape(YX, ROWS, 2 * FRAME), ('y', 'x'), 0, 0, ti...  34.9 us
    pallas_call x1, Pallas kernels, weights(): pl.pallas_call(weights_kernel, in_specs=[pl.BlockSpec(memory_space=m) for...  9.06 us
    pallas_call x1, Pallas kernels, inner_spectra(): pl.pallas_call(inner_kernel, in_specs=[smem, vmem, vmem, hbm], out_specs=...  6.72 us
    ppermute x1, starting transfers between devices, body(): following = lax.ppermute(own[:HALO], 'zh', down)  6.1 us
    pallas_call x1, Pallas kernels, beams(): pl.pallas_call(beams_kernel, in_specs=[vmem, vmem], out_specs=pl.BlockSpe...  4.22 us
    pallas_call x1, Pallas kernels, outer_spectra(): pl.pallas_call(outer_kernel, in_specs=[smem] + [vmem] * 5 + [hbm], out_sp...  3.26 us
  transfers between devices with their start and end apart: 2, of which 1 were waited for; matrix products, arithmetic and copies ran while one was open for 0% of the time, Pallas kernels for 12%

profile of v6, /device:TPU:1, one launch (start us, length us, event | category | flops | bytes accessed | tf_op | source)
XLA Modules:
  0.0 133.8 jit_solution(11053753501269000376)
XLA Ops:
  0.0 34.9 %all_to_all.10.own_ref = bf16[16,16,4096]{2,1,0:T(8,128)(2,1)S(1)} all-to-all(bf16[16,16,4096]{2,1,0:T(8,128)(2,1)} %bitcast.7), channel_id=1, replica_groups=mesh['zh'=4,'y'=4,'x'=4,'zl'=2,'core'=2] {'y','x'}, dimensions={0} | all-to-all | bytes 4194304 | tf_op jit(solution)/shard_map/all_to_all | solution.py:377
  34.9 0.9 fusion
  35.8 0.4 reshape.19
  36.2 0.1 slice.27
  36.4 6.1 %collective-permute-start = (bf16[4,16,4096]{2,1,0:T(8,128)(2,1)}, bf16[4,16,4096]{2,1,0:T(8,128)(2,1)S(1)}, u32[]{:S(2)}, u32[]{:S(2)}) collective-permute-start(bf16[4,16,4096]{2,1,0:T(8,128)(2,1)} %get-tuple-element.16), channel_id=1, source_target_pairs={{0,192},{64,0},{128,64},{192,128},{1,193},{65,1},{129,65},{193,129... | collective-permute-start | bytes 1572872 | tf_op jit(solution)/shard_map/ppermute | solution.py:378
  42.6 1.3 collective-permute-start.1
  44.0 0.0 copy-start
  44.0 9.1 %shard_map.55.weight = bf16[4,2,512,1024]{3,2,1,0:T(8,128)(2,1)S(1)} custom-call(f32[1]{0:T(128)} %bitcast.2.first_ref, f32[512,1024]{1,0:T(8,128)} %delays_hbm.1, bf16[256,256]{1,0:T(8,128)(2,1)} %constant.32.clone.order_hbm), custom_call_target="tpu_custom_call" | custom-call | flops 31457280 | bytes 12582912 | tf_op jit(solution)/shard_map/pallas_call | solution.py:279
  53.0 0.0 copy-done
  53.1 6.7 %shard_map.56 = (bf16[256,8,512]{2,1,0:T(8,128)(2,1)S(1)}, bf16[2,1024,1024]{2,1,0:T(8,128)(2,1)S(1)}, f32[8,2,16,16,128]{4,3,2,1,0:T(8,128)S(1)}) custom-call(s32[1]{0:T(128)} %bitcast.zh_ref, bf16[16,16,4096]{2,1,0:T(8,128)(2,1)S(1)} %all_to_all.10.own_ref, f32[16,2048]{1,0:T(8,128)S(1)} %copy-done, bf16[2,1024,1024]{2,1,0:T(8,128)(2,1)} %constant.31.clone.table_ref), custom_call_target="tpu_custom_call" | custom-call | flops 1073741824 | bytes 7340032 | tf_op jit(solution)/shard_map/pallas_call | solution.py:181
  59.8 2.4 %collective-permute-done.next_ref = bf16[4,16,4096]{2,1,0:T(8,128)(2,1)S(1)} collective-permute-done((bf16[4,16,4096]{2,1,0:T(8,128)(2,1)}, bf16[4,16,4096]{2,1,0:T(8,128)(2,1)S(1)}, u32[]{:S(2)}, u32[]{:S(2)}) %collective-permute-start) | collective-permute-done | bytes 524320 | tf_op jit(solution)/shard_map/ppermute | solution.py:378
  62.2 0.0 collective-permute-done.1.prev_ref
  62.2 3.3 %shard_map.57 = bf16[256,8,512]{2,1,0:T(8,128)(2,1)S(1)} custom-call(s32[1]{0:T(128)} %bitcast.zh_ref, bf16[4,16,4096]{2,1,0:T(8,128)(2,1)S(1)} %collective-permute-done.next_ref, bf16[7,16,2048]{2,1,0:T(8,128)(2,1)S(1)} %collective-permute-done.1.prev_ref, f32[16,2048]{1,0:T(8,128)S(1)} %copy-done, ...), custom_call_target="tpu_custom_call", output_to_operand_aliasing={{}: (6, {})} | custom-call | flops 1073741824 | bytes 7340032 | tf_op jit(solution)/shard_map/pallas_call | solution.py:196
  65.5 64.1 %all_to_all.11.spectra_ref = bf16[256,8,512]{2,1,0:T(8,128)(2,1)S(1)} all-to-all(bf16[256,8,512]{2,1,0:T(8,128)(2,1)S(1)} %shard_map.57), channel_id=1, replica_groups=mesh['zh'=4,'y'=4,'x'=4,'zl'=2,'core'=2] {'zh','zl','core','y','x'}, dimensions={0} | all-to-all | bytes 4194304 | tf_op jit(solution)/shard_map/all_to_all | solution.py:386
  129.5 4.2 %shard_map.58 = bf16[2,4,512,128]{3,2,1,0:T(8,128)(2,1)} custom-call(bf16[256,8,512]{2,1,0:T(8,128)(2,1)S(1)} %all_to_all.11.spectra_ref, bf16[4,2,512,1024]{3,2,1,0:T(8,128)(2,1)S(1)} %shard_map.55.weight), custom_call_target="tpu_custom_call" | custom-call | flops 2147483648 | bytes 11534336 | tf_op jit(solution)/shard_map/pallas_call | solution.py:352
  (4 shorter events, 0.1 us)
Async XLA Ops:
  36.4 25.8 %collective-permute-start = (bf16[4,16,4096]{2,1,0:T(8,128)(2,1)}, bf16[4,16,4096]{2,1,0:T(8,128)(2,1)S(1)}, u32[]{:S(2)}, u32[]{:S(2)}) collective-permute-start(bf16[4,16,4096]{2,1,0:T(8,128)(2,1)} %get-tuple-element.16), channel_id=1, source_target_pairs={{0,192},{64,0},{128,64},{192,128},{1,193},{65,1},{129,65},{193,129... | collective-permute-start | bytes 1572872 | tf_op jit(solution)/shard_map/ppermute | solution.py:378
  42.6 19.6 %collective-permute-start.1 = (bf16[7,16,2048]{2,1,0:T(8,128)(2,1)S(1)}, bf16[7,16,2048]{2,1,0:T(8,128)(2,1)S(1)}, u32[]{:S(2)}, u32[]{:S(2)}) collective-permute-start(bf16[7,16,2048]{2,1,0:T(8,128)(2,1)S(1)} %pad_maximum_fusion), channel_id=1, source_target_pairs={{0,64},{64,128},{128,192},{1,65},{65,129},{129,193},{2,66},{66,130... | collective-permute-start | bytes 1376264 | tf_op jit(solution)/shard_map/ppermute | solution.py:381
  44.0 9.1 %copy-start = (f32[16,2048]{1,0:T(8,128)S(1)}, f32[16,2048]{1,0:T(8,128)}, u32[]{:S(2)}) copy-start(f32[16,2048]{1,0:T(8,128)} %coeffs_ref.3) | copy-start | bytes 393220

commit v7 on v6

--- a/solution.py
+++ b/solution.py
@@ -26,6 +26,7 @@
 PLACES = YX * INP
 LANES = 128
 GROUP = LANES // PART
+PITCH = PART + 8
 ALL = ("zh", "y", "x", "zl", "core")
 OWNERS = ("zh", "zl", "core", "y", "x")
 
@@ -80,7 +81,7 @@
 def add_sums(sums, turned, step, shift):
     lanes = pl.ds(pl.multiple_of(step * LANES, LANES), LANES)
     for k in range(ROWS):
-        first, second = (turned[side, k * PART : (k + 1) * PART] for side in range(2))
+        first, second = (turned[side, k * PITCH : k * PITCH + PART] for side in range(2))
         to = k // GROUP * GROUP + lax.rem(k % GROUP + shift, GROUP)
         to = pl.ds(pl.multiple_of(to * PART, PART), PART)
         sums[0, to, lanes] = (first + second).astype(jnp.bfloat16)
@@ -130,7 +131,7 @@
             for j in range(LATE):
                 partial_ref[step, side, LATE + j] = weighted(own, taps, LATE + j, range(LATE + j + 1))
             for j in range(PART):
-                turned[side, pl.ds(j, ROWS, stride=PART), :] = weighted(own, taps, PART + j, range(TAPS))
+                turned[side, pl.ds(j, ROWS, stride=PITCH), :] = weighted(own, taps, PART + j, range(TAPS))
             for j in range(LATE):
                 part = weighted(own, taps, PLANE + j, range(j + 1, TAPS))
                 partial_ref[step, side, j] = part * keep
@@ -152,11 +153,11 @@
             taps = [coeffs_ref[t : t + 1, pl.ds(base, LANES)] for t in range(TAPS)]
             for j in range(LATE):
                 total = partial_ref[step, side, j] + weighted(following, taps, j, range(j + 1))
-                turned[side, pl.ds(j, ROWS, stride=PART), :] = total
+                turned[side, pl.ds(j, ROWS, stride=PITCH), :] = total
                 total = partial_ref[step, side, LATE + j]
                 if LATE + j + 1 < TAPS:
                     total = total + weighted(prev, taps, 2 * LATE - 1 + j, range(LATE + j + 1, TAPS))
-                turned[side, pl.ds(LATE + j, ROWS, stride=PART), :] = total
+                turned[side, pl.ds(LATE + j, ROWS, stride=PITCH), :] = total
         add_sums(sums, turned, step, 2 * zh_ref[0])
         return carry
 
@@ -169,7 +170,7 @@
 STEPS = 4
 SPECTRA_SCRATCH = [
     pltpu.VMEM((2, ROWS * PART, FRAME // 2), jnp.bfloat16),
-    pltpu.VMEM((2, ROWS * PART, LANES), jnp.float32),
+    pltpu.VMEM((2, (ROWS + 1) * PITCH, LANES), jnp.float32),
     pltpu.VMEM((DEVICES, 2 * OWN, ROWS * PART), jnp.bfloat16),
 ]
 SEMS = pltpu.SemaphoreType.DMA((STEPS,))
@@ -327,7 +328,7 @@
 def beams_kernel(spectra_ref, weight, out_ref, wide, values, result, sems):
     for tile in range(ROWS * PLANE // LANES):
         part = spectra_ref[:, :, tile * LANES : (tile + 1) * LANES]
-        wide[tile] = part.astype(jnp.float32).reshape(DEVICES * 2 * OWN, LANES)
+        wide[tile, : DEVICES * 2 * OWN] = part.astype(jnp.float32).reshape(DEVICES * 2 * OWN, LANES)
     lane = lax.broadcasted_iota(jnp.int32, (BEAMS, LANES), 1)
     taken_over = lax.rem(lane, PLANE) < LATE
     copies = []
@@ -355,7 +356,7 @@
         out_specs=pl.BlockSpec(memory_space=pl.ANY),
         out_shape=jax.ShapeDtypeStruct(shape, jnp.bfloat16),
         scratch_shapes=[
-            pltpu.VMEM((ROWS * PLANE // LANES, DEVICES * 2 * OWN, LANES), jnp.float32),
+            pltpu.VMEM((ROWS * PLANE // LANES, (DEVICES + 1) * 2 * OWN, LANES), jnp.float32),
             pltpu.VMEM((OWN, INPUTS, 2 * LANES), jnp.bfloat16),
             pltpu.VMEM(shape, jnp.bfloat16),
             pltpu.SemaphoreType.DMA((OWN,)),

time: 134 us -> 134 us (level)
  no operation moved by 1% of the time
where the time goes in v7:
time: 134 us
  blocking collectives  99 us (74%)
  Pallas kernels  22.9 us (17%)
  starting transfers between devices  7.42 us (6%)
  waiting for transfers between devices  2.61 us (2%)
  local copies, waits for them, and re-layouts  1.48 us (1%)
    all_to_all x1, blocking collectives, body(): received = lax.all_to_all(blocks, OWNERS, 0, 0, tiled=True)  64.1 us
    all_to_all x1, blocking collectives, body(): lax.all_to_all(samples.reshape(YX, ROWS, 2 * FRAME), ('y', 'x'), 0, 0, ti...  34.9 us
    pallas_call x1, Pallas kernels, weights(): pl.pallas_call(weights_kernel, in_specs=[pl.BlockSpec(memory_space=m) for...  9.06 us
    pallas_call x1, Pallas kernels, inner_spectra(): pl.pallas_call(inner_kernel, in_specs=[smem, vmem, vmem, hbm], out_specs=...  6.54 us
    ppermute x1, starting transfers between devices, body(): following = lax.ppermute(own[:HALO], 'zh', down)  6.1 us
    pallas_call x1, Pallas kernels, beams(): pl.pallas_call(beams_kernel, in_specs=[vmem, vmem], out_specs=pl.BlockSpe...  4.22 us
    pallas_call x1, Pallas kernels, outer_spectra(): pl.pallas_call(outer_kernel, in_specs=[smem] + [vmem] * 5 + [hbm], out_sp...  3.12 us
  transfers between devices with their start and end apart: 2, of which 1 were waited for; matrix products, arithmetic and copies ran while one was open for 0% of the time, Pallas kernels for 12%

profile of v7, /device:TPU:1, one launch (start us, length us, event | category | flops | bytes accessed | tf_op | source)
XLA Modules:
  0.0 133.6 jit_solution(5163958415395730700)
XLA Ops:
  0.0 34.9 %all_to_all.10.own_ref = bf16[16,16,4096]{2,1,0:T(8,128)(2,1)S(1)} all-to-all(bf16[16,16,4096]{2,1,0:T(8,128)(2,1)} %bitcast.7), channel_id=1, replica_groups=mesh['zh'=4,'y'=4,'x'=4,'zl'=2,'core'=2] {'y','x'}, dimensions={0} | all-to-all | bytes 4194304 | tf_op jit(solution)/shard_map/all_to_all | solution.py:378
  34.9 0.9 fusion
  35.8 0.4 reshape.19
  36.2 0.1 slice.27
  36.4 6.1 %collective-permute-start = (bf16[4,16,4096]{2,1,0:T(8,128)(2,1)}, bf16[4,16,4096]{2,1,0:T(8,128)(2,1)S(1)}, u32[]{:S(2)}, u32[]{:S(2)}) collective-permute-start(bf16[4,16,4096]{2,1,0:T(8,128)(2,1)} %get-tuple-element.16), channel_id=1, source_target_pairs={{0,192},{64,0},{128,64},{192,128},{1,193},{65,1},{129,65},{193,129... | collective-permute-start | bytes 1572872 | tf_op jit(solution)/shard_map/ppermute | solution.py:379
  42.6 1.3 collective-permute-start.1
  44.0 0.0 copy-start
  44.0 9.1 %shard_map.55.weight = bf16[4,2,512,1024]{3,2,1,0:T(8,128)(2,1)S(1)} custom-call(f32[1]{0:T(128)} %bitcast.2.first_ref, f32[512,1024]{1,0:T(8,128)} %delays_hbm.1, bf16[256,256]{1,0:T(8,128)(2,1)} %constant.32.clone.order_hbm), custom_call_target="tpu_custom_call" | custom-call | flops 31457280 | bytes 12582912 | tf_op jit(solution)/shard_map/pallas_call | solution.py:280
  53.0 0.0 copy-done
  53.1 6.5 %shard_map.56 = (bf16[256,8,512]{2,1,0:T(8,128)(2,1)S(1)}, bf16[2,1024,1024]{2,1,0:T(8,128)(2,1)S(1)}, f32[8,2,16,16,128]{4,3,2,1,0:T(8,128)S(1)}) custom-call(s32[1]{0:T(128)} %bitcast.zh_ref, bf16[16,16,4096]{2,1,0:T(8,128)(2,1)S(1)} %all_to_all.10.own_ref, f32[16,2048]{1,0:T(8,128)S(1)} %copy-done, bf16[2,1024,1024]{2,1,0:T(8,128)(2,1)} %constant.31.clone.table_ref), custom_call_target="tpu_custom_call" | custom-call | flops 1073741824 | bytes 7340032 | tf_op jit(solution)/shard_map/pallas_call | solution.py:182
  59.6 2.6 %collective-permute-done.next_ref = bf16[4,16,4096]{2,1,0:T(8,128)(2,1)S(1)} collective-permute-done((bf16[4,16,4096]{2,1,0:T(8,128)(2,1)}, bf16[4,16,4096]{2,1,0:T(8,128)(2,1)S(1)}, u32[]{:S(2)}, u32[]{:S(2)}) %collective-permute-start) | collective-permute-done | bytes 524320 | tf_op jit(solution)/shard_map/ppermute | solution.py:379
  62.2 0.0 collective-permute-done.1.prev_ref
  62.2 3.1 %shard_map.57 = bf16[256,8,512]{2,1,0:T(8,128)(2,1)S(1)} custom-call(s32[1]{0:T(128)} %bitcast.zh_ref, bf16[4,16,4096]{2,1,0:T(8,128)(2,1)S(1)} %collective-permute-done.next_ref, bf16[7,16,2048]{2,1,0:T(8,128)(2,1)S(1)} %collective-permute-done.1.prev_ref, f32[16,2048]{1,0:T(8,128)S(1)} %copy-done, ...), custom_call_target="tpu_custom_call", output_to_operand_aliasing={{}: (6, {})} | custom-call | flops 1073741824 | bytes 7340032 | tf_op jit(solution)/shard_map/pallas_call | solution.py:197
  65.3 64.1 %all_to_all.11.spectra_ref = bf16[256,8,512]{2,1,0:T(8,128)(2,1)S(1)} all-to-all(bf16[256,8,512]{2,1,0:T(8,128)(2,1)S(1)} %shard_map.57), channel_id=1, replica_groups=mesh['zh'=4,'y'=4,'x'=4,'zl'=2,'core'=2] {'zh','zl','core','y','x'}, dimensions={0} | all-to-all | bytes 4194304 | tf_op jit(solution)/shard_map/all_to_all | solution.py:387
  129.4 4.2 %shard_map.58 = bf16[2,4,512,128]{3,2,1,0:T(8,128)(2,1)} custom-call(bf16[256,8,512]{2,1,0:T(8,128)(2,1)S(1)} %all_to_all.11.spectra_ref, bf16[4,2,512,1024]{3,2,1,0:T(8,128)(2,1)S(1)} %shard_map.55.weight), custom_call_target="tpu_custom_call" | custom-call | flops 2147483648 | bytes 11534336 | tf_op jit(solution)/shard_map/pallas_call | solution.py:353
  (4 shorter events, 0.1 us)
Async XLA Ops:
  36.4 25.8 %collective-permute-start = (bf16[4,16,4096]{2,1,0:T(8,128)(2,1)}, bf16[4,16,4096]{2,1,0:T(8,128)(2,1)S(1)}, u32[]{:S(2)}, u32[]{:S(2)}) collective-permute-start(bf16[4,16,4096]{2,1,0:T(8,128)(2,1)} %get-tuple-element.16), channel_id=1, source_target_pairs={{0,192},{64,0},{128,64},{192,128},{1,193},{65,1},{129,65},{193,129... | collective-permute-start | bytes 1572872 | tf_op jit(solution)/shard_map/ppermute | solution.py:379
  42.6 19.6 %collective-permute-start.1 = (bf16[7,16,2048]{2,1,0:T(8,128)(2,1)S(1)}, bf16[7,16,2048]{2,1,0:T(8,128)(2,1)S(1)}, u32[]{:S(2)}, u32[]{:S(2)}) collective-permute-start(bf16[7,16,2048]{2,1,0:T(8,128)(2,1)S(1)} %pad_maximum_fusion), channel_id=1, source_target_pairs={{0,64},{64,128},{128,192},{1,65},{65,129},{129,193},{2,66},{66,130... | collective-permute-start | bytes 1376264 | tf_op jit(solution)/shard_map/ppermute | solution.py:382
  44.0 9.1 %copy-start = (f32[16,2048]{1,0:T(8,128)S(1)}, f32[16,2048]{1,0:T(8,128)}, u32[]{:S(2)}) copy-start(f32[16,2048]{1,0:T(8,128)} %coeffs_ref.3) | copy-start | bytes 393220

commit v8 on v7

--- a/solution.py
+++ b/solution.py
@@ -166,6 +166,26 @@
     transform(sums, tables, result, out_ref, lanes, out_sems, lambda step: None)
 
 
+def ends_kernel(own_ref, first_ref, last_ref):
+    first_ref[...] = own_ref[:HALO]
+    for k in range(TAPS - 1 - LATE):
+        f = PLANE - (TAPS - 1 - LATE) + k
+        last_ref[k] = own_ref[f // 2, :, f % 2 * FRAME : (f % 2 + 1) * FRAME]
+
+
+def ends(own):
+    vmem = pl.BlockSpec(memory_space=pltpu.VMEM)
+    shapes = (HALO, ROWS, 2 * FRAME), (TAPS - 1 - LATE, ROWS, FRAME)
+    return pl.pallas_call(
+        ends_kernel,
+        in_specs=[vmem],
+        out_specs=[vmem, vmem],
+        out_shape=[jax.ShapeDtypeStruct(shape, own.dtype) for shape in shapes],
+        compiler_params=pltpu.CompilerParams(vmem_limit_bytes=8 << 20),
+        cost_estimate=pl.CostEstimate(flops=0, bytes_accessed=2 << 20, transcendentals=0),
+    )(own)
+
+
 SPECTRA = jax.ShapeDtypeStruct((DEVICES, 2 * OWN, ROWS * PLANE), jnp.bfloat16)
 STEPS = 4
 SPECTRA_SCRATCH = [
@@ -376,10 +396,9 @@
     down = [(i, (i - 1) % ZH) for i in range(ZH)]
 
     own = lax.all_to_all(samples.reshape(YX, ROWS, 2 * FRAME), ("y", "x"), 0, 0, tiled=True)
-    following = lax.ppermute(own[:HALO], "zh", down)
-    last = own[YX - HALO :].reshape(HALO, ROWS, 2, FRAME)
-    last = jnp.concatenate([last[:1, :, 1], last[1:].transpose(0, 2, 1, 3).reshape(LATE - 2, ROWS, FRAME)])
-    prev = lax.ppermute(last, "zh", up)
+    down_frames, up_frames = ends(own)
+    following = lax.ppermute(down_frames, "zh", down)
+    prev = lax.ppermute(up_frames, "zh", up)
     weight = weights(first, delays)
     inner, tables, partial = inner_spectra(zh, own, coeffs, table)
     following, weight = lax.optimization_barrier((following, weight))

time: 134 us -> 133 us (level)
  local copies, waits for them, and re-layouts: 1.48 us -> 0.01 us
where the time goes in v8:
time: 133 us
  blocking collectives  99 us (74%)
  Pallas kernels  23.8 us (18%)
  starting transfers between devices  7.33 us (6%)
  waiting for transfers between devices  2.73 us (2%)
    all_to_all x1, blocking collectives, body(): received = lax.all_to_all(blocks, OWNERS, 0, 0, tiled=True)  64.1 us
    all_to_all x1, blocking collectives, body(): lax.all_to_all(samples.reshape(YX, ROWS, 2 * FRAME), ('y', 'x'), 0, 0, ti...  34.9 us
    pallas_call x1, Pallas kernels, weights(): pl.pallas_call(weights_kernel, in_specs=[pl.BlockSpec(memory_space=m) for...  9.06 us
    pallas_call x1, Pallas kernels, inner_spectra(): pl.pallas_call(inner_kernel, in_specs=[smem, vmem, vmem, hbm], out_specs=...  6.53 us
    ppermute x1, starting transfers between devices, body(): following = lax.ppermute(down_frames, 'zh', down)  6.02 us
    pallas_call x1, Pallas kernels, beams(): pl.pallas_call(beams_kernel, in_specs=[vmem, vmem], out_specs=pl.BlockSpe...  4.22 us
    pallas_call x1, Pallas kernels, outer_spectra(): pl.pallas_call(outer_kernel, in_specs=[smem] + [vmem] * 5 + [hbm], out_sp...  3.12 us
    ppermute x1, waiting for transfers between devices, body(): following = lax.ppermute(down_frames, 'zh', down)  2.73 us
  transfers between devices with their start and end apart: 2, of which 1 were waited for; matrix products, arithmetic and copies ran while one was open for 0% of the time, Pallas kernels for 12%

profile of v8, /device:TPU:1, one launch (start us, length us, event | category | flops | bytes accessed | tf_op | source)
XLA Modules:
  0.0 132.9 jit_solution(17189371952721422682)
XLA Ops:
  0.0 34.9 %all_to_all.10.own_ref = bf16[16,16,4096]{2,1,0:T(8,128)(2,1)S(1)} all-to-all(bf16[16,16,4096]{2,1,0:T(8,128)(2,1)} %bitcast.3), channel_id=1, replica_groups=mesh['zh'=4,'y'=4,'x'=4,'zl'=2,'core'=2] {'y','x'}, dimensions={0} | all-to-all | bytes 4194304 | tf_op jit(solution)/shard_map/all_to_all | solution.py:398
  34.9 0.9 shard_map.55
  35.8 6.0 %collective-permute-start = (bf16[4,16,4096]{2,1,0:T(8,128)(2,1)}, bf16[4,16,4096]{2,1,0:T(8,128)(2,1)S(1)}, u32[]{:S(2)}, u32[]{:S(2)}) collective-permute-start(bf16[4,16,4096]{2,1,0:T(8,128)(2,1)} %get-tuple-element.12), channel_id=1, source_target_pairs={{0,192},{64,0},{128,64},{192,128},{1,193},{65,1},{129,65},{193,129... | collective-permute-start | bytes 1572872 | tf_op jit(solution)/shard_map/ppermute | solution.py:400
  41.8 1.3 collective-permute-start.1
  43.2 0.0 copy-start
  43.2 9.1 %shard_map.56.weight = bf16[4,2,512,1024]{3,2,1,0:T(8,128)(2,1)S(1)} custom-call(f32[1]{0:T(128)} %bitcast.2.first_ref, f32[512,1024]{1,0:T(8,128)} %delays_hbm.1, bf16[256,256]{1,0:T(8,128)(2,1)} %constant.32.clone.order_hbm), custom_call_target="tpu_custom_call" | custom-call | flops 31457280 | bytes 12582912 | tf_op jit(solution)/shard_map/pallas_call | solution.py:300
  52.2 0.0 copy-done
  52.2 6.5 %shard_map.57 = (bf16[256,8,512]{2,1,0:T(8,128)(2,1)S(1)}, bf16[2,1024,1024]{2,1,0:T(8,128)(2,1)S(1)}, f32[8,2,16,16,128]{4,3,2,1,0:T(8,128)S(1)}) custom-call(s32[1]{0:T(128)} %bitcast.zh_ref, bf16[16,16,4096]{2,1,0:T(8,128)(2,1)S(1)} %all_to_all.10.own_ref, f32[16,2048]{1,0:T(8,128)S(1)} %copy-done, bf16[2,1024,1024]{2,1,0:T(8,128)(2,1)} %constant.31.clone.table_ref), custom_call_target="tpu_custom_call" | custom-call | flops 1073741824 | bytes 7340032 | tf_op jit(solution)/shard_map/pallas_call | solution.py:202
  58.8 2.7 %collective-permute-done.next_ref = bf16[4,16,4096]{2,1,0:T(8,128)(2,1)S(1)} collective-permute-done((bf16[4,16,4096]{2,1,0:T(8,128)(2,1)}, bf16[4,16,4096]{2,1,0:T(8,128)(2,1)S(1)}, u32[]{:S(2)}, u32[]{:S(2)}) %collective-permute-start) | collective-permute-done | bytes 524320 | tf_op jit(solution)/shard_map/ppermute | solution.py:400
  61.5 0.0 collective-permute-done.1.prev_ref
  61.5 3.1 %shard_map.58 = bf16[256,8,512]{2,1,0:T(8,128)(2,1)S(1)} custom-call(s32[1]{0:T(128)} %bitcast.zh_ref, bf16[4,16,4096]{2,1,0:T(8,128)(2,1)S(1)} %collective-permute-done.next_ref, bf16[7,16,2048]{2,1,0:T(8,128)(2,1)S(1)} %collective-permute-done.1.prev_ref, f32[16,2048]{1,0:T(8,128)S(1)} %copy-done, ...), custom_call_target="tpu_custom_call", output_to_operand_aliasing={{}: (6, {})} | custom-call | flops 1073741824 | bytes 7340032 | tf_op jit(solution)/shard_map/pallas_call | solution.py:217
  64.6 64.1 %all_to_all.11.spectra_ref = bf16[256,8,512]{2,1,0:T(8,128)(2,1)S(1)} all-to-all(bf16[256,8,512]{2,1,0:T(8,128)(2,1)S(1)} %shard_map.58), channel_id=1, replica_groups=mesh['zh'=4,'y'=4,'x'=4,'zl'=2,'core'=2] {'zh','zl','core','y','x'}, dimensions={0} | all-to-all | bytes 4194304 | tf_op jit(solution)/shard_map/all_to_all | solution.py:406
  128.7 4.2 %shard_map.59 = bf16[2,4,512,128]{3,2,1,0:T(8,128)(2,1)} custom-call(bf16[256,8,512]{2,1,0:T(8,128)(2,1)S(1)} %all_to_all.11.spectra_ref, bf16[4,2,512,1024]{3,2,1,0:T(8,128)(2,1)S(1)} %shard_map.56.weight), custom_call_target="tpu_custom_call" | custom-call | flops 2147483648 | bytes 11534336 | tf_op jit(solution)/shard_map/pallas_call | solution.py:373
Async XLA Ops:
  35.8 25.7 %collective-permute-start = (bf16[4,16,4096]{2,1,0:T(8,128)(2,1)}, bf16[4,16,4096]{2,1,0:T(8,128)(2,1)S(1)}, u32[]{:S(2)}, u32[]{:S(2)}) collective-permute-start(bf16[4,16,4096]{2,1,0:T(8,128)(2,1)} %get-tuple-element.12), channel_id=1, source_target_pairs={{0,192},{64,0},{128,64},{192,128},{1,193},{65,1},{129,65},{193,129... | collective-permute-start | bytes 1572872 | tf_op jit(solution)/shard_map/ppermute | solution.py:400
  41.8 19.7 %collective-permute-start.1 = (bf16[7,16,2048]{2,1,0:T(8,128)(2,1)S(1)}, bf16[7,16,2048]{2,1,0:T(8,128)(2,1)S(1)}, u32[]{:S(2)}, u32[]{:S(2)}) collective-permute-start(bf16[7,16,2048]{2,1,0:T(8,128)(2,1)S(1)} %get-tuple-element.14), channel_id=1, source_target_pairs={{0,64},{64,128},{128,192},{1,65},{65,129},{129,193},{2,66},{66,130... | collective-permute-start | bytes 1376264 | tf_op jit(solution)/shard_map/ppermute | solution.py:401
  43.2 9.1 %copy-start = (f32[16,2048]{1,0:T(8,128)S(1)}, f32[16,2048]{1,0:T(8,128)}, u32[]{:S(2)}) copy-start(f32[16,2048]{1,0:T(8,128)} %coeffs_ref.3) | copy-start | bytes 393220

commit v9 on v8

--- a/solution.py
+++ b/solution.py
@@ -187,7 +187,7 @@
 
 
 SPECTRA = jax.ShapeDtypeStruct((DEVICES, 2 * OWN, ROWS * PLANE), jnp.bfloat16)
-STEPS = 4
+STEPS = 2
 SPECTRA_SCRATCH = [
     pltpu.VMEM((2, ROWS * PART, FRAME // 2), jnp.bfloat16),
     pltpu.VMEM((2, (ROWS + 1) * PITCH, LANES), jnp.float32),

time: 133 us -> 133 us (level)
  transfers between devices with their start and end apart: 2 -> 2, of which waited for: 1 -> 1; matrix products, arithmetic and copies ran while one was open for 0% -> 0% of each run, Pallas kernels for 12% -> 11%
where the time goes in v9:
time: 133 us; the launch traced here: 132 us
  blocking collectives  99 us (74%)
  Pallas kernels  22.9 us (17%)
  starting transfers between devices  7.33 us (6%)
  waiting for transfers between devices  3.18 us (2%)
    all_to_all x1, blocking collectives, body(): received = lax.all_to_all(blocks, OWNERS, 0, 0, tiled=True)  64.1 us
    all_to_all x1, blocking collectives, body(): lax.all_to_all(samples.reshape(YX, ROWS, 2 * FRAME), ('y', 'x'), 0, 0, ti...  34.9 us
    pallas_call x1, Pallas kernels, weights(): pl.pallas_call(weights_kernel, in_specs=[pl.BlockSpec(memory_space=m) for...  9.06 us
    pallas_call x1, Pallas kernels, inner_spectra(): pl.pallas_call(inner_kernel, in_specs=[smem, vmem, vmem, hbm], out_specs=...  6.09 us
    ppermute x1, starting transfers between devices, body(): following = lax.ppermute(down_frames, 'zh', down)  6.02 us
    pallas_call x1, Pallas kernels, beams(): pl.pallas_call(beams_kernel, in_specs=[vmem, vmem], out_specs=pl.BlockSpe...  4.22 us
    ppermute x1, waiting for transfers between devices, body(): following = lax.ppermute(down_frames, 'zh', down)  3.17 us
    pallas_call x1, Pallas kernels, outer_spectra(): pl.pallas_call(outer_kernel, in_specs=[smem] + [vmem] * 5 + [hbm], out_sp...  2.68 us
  transfers between devices with their start and end apart: 2, of which 1 were waited for; matrix products, arithmetic and copies ran while one was open for 0% of the time, Pallas kernels for 11%

profile of v9, /device:TPU:1, one launch (start us, length us, event | category | flops | bytes accessed | tf_op | source)
XLA Modules:
  0.0 132.5 jit_solution(13346320270551694660)
XLA Ops:
  0.0 34.9 %all_to_all.10.own_ref = bf16[16,16,4096]{2,1,0:T(8,128)(2,1)S(1)} all-to-all(bf16[16,16,4096]{2,1,0:T(8,128)(2,1)} %bitcast.3), channel_id=1, replica_groups=mesh['zh'=4,'y'=4,'x'=4,'zl'=2,'core'=2] {'y','x'}, dimensions={0} | all-to-all | bytes 4194304 | tf_op jit(solution)/shard_map/all_to_all | solution.py:398
  34.9 0.9 shard_map.55
  35.8 6.0 %collective-permute-start = (bf16[4,16,4096]{2,1,0:T(8,128)(2,1)}, bf16[4,16,4096]{2,1,0:T(8,128)(2,1)S(1)}, u32[]{:S(2)}, u32[]{:S(2)}) collective-permute-start(bf16[4,16,4096]{2,1,0:T(8,128)(2,1)} %get-tuple-element.12), channel_id=1, source_target_pairs={{0,192},{64,0},{128,64},{192,128},{1,193},{65,1},{129,65},{193,129... | collective-permute-start | bytes 1572872 | tf_op jit(solution)/shard_map/ppermute | solution.py:400
  41.8 1.3 collective-permute-start.1
  43.2 0.0 copy-start
  43.2 9.1 %shard_map.56.weight = bf16[4,2,512,1024]{3,2,1,0:T(8,128)(2,1)S(1)} custom-call(f32[1]{0:T(128)} %bitcast.2.first_ref, f32[512,1024]{1,0:T(8,128)} %delays_hbm.1, bf16[256,256]{1,0:T(8,128)(2,1)} %constant.32.clone.order_hbm), custom_call_target="tpu_custom_call" | custom-call | flops 31457280 | bytes 12582912 | tf_op jit(solution)/shard_map/pallas_call | solution.py:300
  52.2 0.0 copy-done
  52.2 6.1 %shard_map.57 = (bf16[256,8,512]{2,1,0:T(8,128)(2,1)S(1)}, bf16[2,1024,1024]{2,1,0:T(8,128)(2,1)S(1)}, f32[8,2,16,16,128]{4,3,2,1,0:T(8,128)S(1)}) custom-call(s32[1]{0:T(128)} %bitcast.zh_ref, bf16[16,16,4096]{2,1,0:T(8,128)(2,1)S(1)} %all_to_all.10.own_ref, f32[16,2048]{1,0:T(8,128)S(1)} %copy-done, bf16[2,1024,1024]{2,1,0:T(8,128)(2,1)} %constant.31.clone.table_ref), custom_call_target="tpu_custom_call" | custom-call | flops 1073741824 | bytes 7340032 | tf_op jit(solution)/shard_map/pallas_call | solution.py:202
  58.3 3.2 %collective-permute-done.next_ref = bf16[4,16,4096]{2,1,0:T(8,128)(2,1)S(1)} collective-permute-done((bf16[4,16,4096]{2,1,0:T(8,128)(2,1)}, bf16[4,16,4096]{2,1,0:T(8,128)(2,1)S(1)}, u32[]{:S(2)}, u32[]{:S(2)}) %collective-permute-start) | collective-permute-done | bytes 524320 | tf_op jit(solution)/shard_map/ppermute | solution.py:400
  61.5 0.0 collective-permute-done.1.prev_ref
  61.5 2.7 %shard_map.58 = bf16[256,8,512]{2,1,0:T(8,128)(2,1)S(1)} custom-call(s32[1]{0:T(128)} %bitcast.zh_ref, bf16[4,16,4096]{2,1,0:T(8,128)(2,1)S(1)} %collective-permute-done.next_ref, bf16[7,16,2048]{2,1,0:T(8,128)(2,1)S(1)} %collective-permute-done.1.prev_ref, f32[16,2048]{1,0:T(8,128)S(1)} %copy-done, ...), custom_call_target="tpu_custom_call", output_to_operand_aliasing={{}: (6, {})} | custom-call | flops 1073741824 | bytes 7340032 | tf_op jit(solution)/shard_map/pallas_call | solution.py:217
  64.2 64.1 %all_to_all.11.spectra_ref = bf16[256,8,512]{2,1,0:T(8,128)(2,1)S(1)} all-to-all(bf16[256,8,512]{2,1,0:T(8,128)(2,1)S(1)} %shard_map.58), channel_id=1, replica_groups=mesh['zh'=4,'y'=4,'x'=4,'zl'=2,'core'=2] {'zh','zl','core','y','x'}, dimensions={0} | all-to-all | bytes 4194304 | tf_op jit(solution)/shard_map/all_to_all | solution.py:406
  128.3 4.2 %shard_map.59 = bf16[2,4,512,128]{3,2,1,0:T(8,128)(2,1)} custom-call(bf16[256,8,512]{2,1,0:T(8,128)(2,1)S(1)} %all_to_all.11.spectra_ref, bf16[4,2,512,1024]{3,2,1,0:T(8,128)(2,1)S(1)} %shard_map.56.weight), custom_call_target="tpu_custom_call" | custom-call | flops 2147483648 | bytes 11534336 | tf_op jit(solution)/shard_map/pallas_call | solution.py:373
Async XLA Ops:
  35.8 25.7 %collective-permute-start = (bf16[4,16,4096]{2,1,0:T(8,128)(2,1)}, bf16[4,16,4096]{2,1,0:T(8,128)(2,1)S(1)}, u32[]{:S(2)}, u32[]{:S(2)}) collective-permute-start(bf16[4,16,4096]{2,1,0:T(8,128)(2,1)} %get-tuple-element.12), channel_id=1, source_target_pairs={{0,192},{64,0},{128,64},{192,128},{1,193},{65,1},{129,65},{193,129... | collective-permute-start | bytes 1572872 | tf_op jit(solution)/shard_map/ppermute | solution.py:400
  41.8 19.7 %collective-permute-start.1 = (bf16[7,16,2048]{2,1,0:T(8,128)(2,1)S(1)}, bf16[7,16,2048]{2,1,0:T(8,128)(2,1)S(1)}, u32[]{:S(2)}, u32[]{:S(2)}) collective-permute-start(bf16[7,16,2048]{2,1,0:T(8,128)(2,1)S(1)} %get-tuple-element.14), channel_id=1, source_target_pairs={{0,64},{64,128},{128,192},{1,65},{65,129},{129,193},{2,66},{66,130... | collective-permute-start | bytes 1376264 | tf_op jit(solution)/shard_map/ppermute | solution.py:401
  43.2 9.1 %copy-start = (f32[16,2048]{1,0:T(8,128)S(1)}, f32[16,2048]{1,0:T(8,128)}, u32[]{:S(2)}) copy-start(f32[16,2048]{1,0:T(8,128)} %coeffs_ref.3) | copy-start | bytes 393220

commit v10 on v9

--- a/solution.py
+++ b/solution.py
@@ -161,7 +161,7 @@
         add_sums(sums, turned, step, 2 * zh_ref[0])
         return carry
 
-    lax.fori_loop(0, FRAME // 2 // LANES, tile, 0)
+    lax.fori_loop(0, FRAME // 2 // LANES, tile, 0, unroll=2)
     lanes = pl.ds(ROWS * PART, ROWS * PART)
     transform(sums, tables, result, out_ref, lanes, out_sems, lambda step: None)
 

time: 133 us -> 133 us (level)
  no operation moved by 1% of the time
where the time goes in v10:
time: 133 us; the launch traced here: 132 us
  blocking collectives  99 us (74%)
  Pallas kernels  22.9 us (17%)
  starting transfers between devices  7.33 us (6%)
  waiting for transfers between devices  3.18 us (2%)
    all_to_all x1, blocking collectives, body(): received = lax.all_to_all(blocks, OWNERS, 0, 0, tiled=True)  64.1 us
    all_to_all x1, blocking collectives, body(): lax.all_to_all(samples.reshape(YX, ROWS, 2 * FRAME), ('y', 'x'), 0, 0, ti...  34.9 us
    pallas_call x1, Pallas kernels, weights(): pl.pallas_call(weights_kernel, in_specs=[pl.BlockSpec(memory_space=m) for...  9.06 us
    pallas_call x1, Pallas kernels, inner_spectra(): pl.pallas_call(inner_kernel, in_specs=[smem, vmem, vmem, hbm], out_specs=...  6.09 us
    ppermute x1, starting transfers between devices, body(): following = lax.ppermute(down_frames, 'zh', down)  6.02 us
    pallas_call x1, Pallas kernels, beams(): pl.pallas_call(beams_kernel, in_specs=[vmem, vmem], out_specs=pl.BlockSpe...  4.22 us
    ppermute x1, waiting for transfers between devices, body(): following = lax.ppermute(down_frames, 'zh', down)  3.17 us
  transfers between devices with their start and end apart: 2, of which 1 were waited for; matrix products, arithmetic and copies ran while one was open for 0% of the time, Pallas kernels for 11%

profile of v10, /device:TPU:1, one launch (start us, length us, event | category | flops | bytes accessed | tf_op | source)
XLA Modules:
  0.0 132.5 jit_solution(18273936369231675207)
XLA Ops:
  0.0 34.9 %all_to_all.10.own_ref = bf16[16,16,4096]{2,1,0:T(8,128)(2,1)S(1)} all-to-all(bf16[16,16,4096]{2,1,0:T(8,128)(2,1)} %bitcast.3), channel_id=1, replica_groups=mesh['zh'=4,'y'=4,'x'=4,'zl'=2,'core'=2] {'y','x'}, dimensions={0} | all-to-all | bytes 4194304 | tf_op jit(solution)/shard_map/all_to_all | solution.py:398
  34.9 0.9 shard_map.55
  35.8 6.0 %collective-permute-start = (bf16[4,16,4096]{2,1,0:T(8,128)(2,1)}, bf16[4,16,4096]{2,1,0:T(8,128)(2,1)S(1)}, u32[]{:S(2)}, u32[]{:S(2)}) collective-permute-start(bf16[4,16,4096]{2,1,0:T(8,128)(2,1)} %get-tuple-element.12), channel_id=1, source_target_pairs={{0,192},{64,0},{128,64},{192,128},{1,193},{65,1},{129,65},{193,129... | collective-permute-start | bytes 1572872 | tf_op jit(solution)/shard_map/ppermute | solution.py:400
  41.8 1.3 collective-permute-start.1
  43.2 0.0 copy-start
  43.2 9.1 %shard_map.56.weight = bf16[4,2,512,1024]{3,2,1,0:T(8,128)(2,1)S(1)} custom-call(f32[1]{0:T(128)} %bitcast.2.first_ref, f32[512,1024]{1,0:T(8,128)} %delays_hbm.1, bf16[256,256]{1,0:T(8,128)(2,1)} %constant.32.clone.order_hbm), custom_call_target="tpu_custom_call" | custom-call | flops 31457280 | bytes 12582912 | tf_op jit(solution)/shard_map/pallas_call | solution.py:300
  52.2 0.0 copy-done
  52.2 6.1 %shard_map.57 = (bf16[256,8,512]{2,1,0:T(8,128)(2,1)S(1)}, bf16[2,1024,1024]{2,1,0:T(8,128)(2,1)S(1)}, f32[8,2,16,16,128]{4,3,2,1,0:T(8,128)S(1)}) custom-call(s32[1]{0:T(128)} %bitcast.zh_ref, bf16[16,16,4096]{2,1,0:T(8,128)(2,1)S(1)} %all_to_all.10.own_ref, f32[16,2048]{1,0:T(8,128)S(1)} %copy-done, bf16[2,1024,1024]{2,1,0:T(8,128)(2,1)} %constant.31.clone.table_ref), custom_call_target="tpu_custom_call" | custom-call | flops 1073741824 | bytes 7340032 | tf_op jit(solution)/shard_map/pallas_call | solution.py:202
  58.3 3.2 %collective-permute-done.next_ref = bf16[4,16,4096]{2,1,0:T(8,128)(2,1)S(1)} collective-permute-done((bf16[4,16,4096]{2,1,0:T(8,128)(2,1)}, bf16[4,16,4096]{2,1,0:T(8,128)(2,1)S(1)}, u32[]{:S(2)}, u32[]{:S(2)}) %collective-permute-start) | collective-permute-done | bytes 524320 | tf_op jit(solution)/shard_map/ppermute | solution.py:400
  61.5 0.0 collective-permute-done.1.prev_ref
  61.5 2.7 %shard_map.58 = bf16[256,8,512]{2,1,0:T(8,128)(2,1)S(1)} custom-call(s32[1]{0:T(128)} %bitcast.zh_ref, bf16[4,16,4096]{2,1,0:T(8,128)(2,1)S(1)} %collective-permute-done.next_ref, bf16[7,16,2048]{2,1,0:T(8,128)(2,1)S(1)} %collective-permute-done.1.prev_ref, f32[16,2048]{1,0:T(8,128)S(1)} %copy-done, ...), custom_call_target="tpu_custom_call", output_to_operand_aliasing={{}: (6, {})} | custom-call | flops 1073741824 | bytes 7340032 | tf_op jit(solution)/shard_map/pallas_call | solution.py:217
  64.2 64.1 %all_to_all.11.spectra_ref = bf16[256,8,512]{2,1,0:T(8,128)(2,1)S(1)} all-to-all(bf16[256,8,512]{2,1,0:T(8,128)(2,1)S(1)} %shard_map.58), channel_id=1, replica_groups=mesh['zh'=4,'y'=4,'x'=4,'zl'=2,'core'=2] {'zh','zl','core','y','x'}, dimensions={0} | all-to-all | bytes 4194304 | tf_op jit(solution)/shard_map/all_to_all | solution.py:406
  128.3 4.2 %shard_map.59 = bf16[2,4,512,128]{3,2,1,0:T(8,128)(2,1)} custom-call(bf16[256,8,512]{2,1,0:T(8,128)(2,1)S(1)} %all_to_all.11.spectra_ref, bf16[4,2,512,1024]{3,2,1,0:T(8,128)(2,1)S(1)} %shard_map.56.weight), custom_call_target="tpu_custom_call" | custom-call | flops 2147483648 | bytes 11534336 | tf_op jit(solution)/shard_map/pallas_call | solution.py:373
Async XLA Ops:
  35.8 25.7 %collective-permute-start = (bf16[4,16,4096]{2,1,0:T(8,128)(2,1)}, bf16[4,16,4096]{2,1,0:T(8,128)(2,1)S(1)}, u32[]{:S(2)}, u32[]{:S(2)}) collective-permute-start(bf16[4,16,4096]{2,1,0:T(8,128)(2,1)} %get-tuple-element.12), channel_id=1, source_target_pairs={{0,192},{64,0},{128,64},{192,128},{1,193},{65,1},{129,65},{193,129... | collective-permute-start | bytes 1572872 | tf_op jit(solution)/shard_map/ppermute | solution.py:400
  41.8 19.7 %collective-permute-start.1 = (bf16[7,16,2048]{2,1,0:T(8,128)(2,1)S(1)}, bf16[7,16,2048]{2,1,0:T(8,128)(2,1)S(1)}, u32[]{:S(2)}, u32[]{:S(2)}) collective-permute-start(bf16[7,16,2048]{2,1,0:T(8,128)(2,1)S(1)} %get-tuple-element.14), channel_id=1, source_target_pairs={{0,64},{64,128},{128,192},{1,65},{65,129},{129,193},{2,66},{66,130... | collective-permute-start | bytes 1376264 | tf_op jit(solution)/shard_map/ppermute | solution.py:401
  43.2 9.1 %copy-start = (f32[16,2048]{1,0:T(8,128)S(1)}, f32[16,2048]{1,0:T(8,128)}, u32[]{:S(2)}) copy-start(f32[16,2048]{1,0:T(8,128)} %coeffs_ref.3) | copy-start | bytes 393220
